TPU v7x, 32 devices: a whole 2x2x4 slice. The times are simulated.
32 devices in a mesh: groups: 2 (over y), tr: 8 (over z, x), tc: 2 (over core).
Axes of the slice: x: 2, y: 2, z: 4, core: 2. Of those that a mesh axis runs over, the one named last changes fastest.
Arguments:
- shift_plane: float32 [2, 8192, 4096], P(None, ('groups', 'tr'), 'tc'), parts along dimension 1, may hold values from -0.2 to 0.2
- height: float32 [8192, 4096], P(('groups', 'tr'), 'tc'), parts along dimension 0, may hold values from -4 to 4
- dipole: float32 [8192, 4096], P(('groups', 'tr'), 'tc'), parts along dimension 0, may hold values from -6 to 6
Outputs:
- velocity_update: float32 [3, 8192, 4096], P(None, ('groups', 'tr'), 'tc'), parts along dimension 1
- dipole_update: float32 [8192, 4096], P(('groups', 'tr'), 'tc'), parts along dimension 0
There are 2 independent parts, one for each index of `groups`. A program takes and returns all parts, laid end to end along the dimension named above; each array names one. Nothing has to cross between parts.
All inputs are finite; a program needn't handle non-finite values.
Results may differ from a plain program's by a relative error of at most 0.00009.
Values sent between devices are 32-bit elements; how exact they have to be, the bound alone decides.
No kernel may reach another device: no remote copies, remote signals or barrier semaphores. Data moves between devices by JAX's collectives and lax.ppermute only.
A program may use at most 256 MiB of HBM per device.

v0:
```python
import math

import jax
import jax.numpy as jnp
from jax import lax
from jax.sharding import PartitionSpec as P

largest_wavenumber = lax.Precision.HIGHEST


def padded_2(x, sides, width):
    for axis, dim in sides:
        devices, length = (lax.axis_size(axis), x.shape[dim])
        up = [(i, (i + 1) % devices) for i in range(devices)]
        down = [(j, i) for i, j in up]
        last = lax.slice_in_dim(x, length - width, length, axis=dim)
        initial = lax.slice_in_dim(x, 0, width, axis=dim)
        before = lax.ppermute(last, axis, up)
        after = lax.ppermute(initial, axis, down)
        x = jnp.concatenate([before, x, after], axis=dim)
    return x


def rows_first(field):
    return (
        field[..., :-4, :]
        - 8.0 * field[..., 1:-3, :]
        + 8.0 * field[..., 3:-1, :]
        - field[..., 4:, :]
    ) / 12.0


def cols_first(field):
    return (
        field[..., :-4] - 8.0 * field[..., 1:-3] + 8.0 * field[..., 3:-1] - field[..., 4:]
    ) / 12.0


def rows_second(field):
    return (
        -field[..., :-4, :]
        + 16.0 * field[..., 1:-3, :]
        - 30.0 * field[..., 2:-2, :]
        + 16.0 * field[..., 3:-1, :]
        - field[..., 4:, :]
    ) / 12.0


def second_column_split(field):
    return (
        -field[..., :-4]
        + 16.0 * field[..., 1:-3]
        - 30.0 * field[..., 2:-2]
        + 16.0 * field[..., 3:-1]
        - field[..., 4:]
    ) / 12.0


def surface(grad_a, grad_b, curve_aa, curve_bb, curve_ab):
    tan_a = (1.0 + grad_a[0], grad_a[1], grad_a[2])
    tan_b = (grad_b[0], 1.0 + grad_b[1], grad_b[2])
    normal = (
        tan_a[1] * tan_b[2] - tan_a[2] * tan_b[1],
        tan_a[2] * tan_b[0] - tan_a[0] * tan_b[2],
        tan_a[0] * tan_b[1] - tan_a[1] * tan_b[0],
    )
    area_stretch_factor = jnp.sqrt(
        normal[0] * normal[0] + normal[1] * normal[1] + normal[2] * normal[2]
    )
    unit = (
        normal[0] / area_stretch_factor,
        normal[1] / area_stretch_factor,
        normal[2] / area_stretch_factor,
    )
    first_edge_term = tan_a[0] * tan_a[0] + tan_a[1] * tan_a[1] + tan_a[2] * tan_a[2]
    first_f = tan_a[0] * tan_b[0] + tan_a[1] * tan_b[1] + tan_a[2] * tan_b[2]
    first_g = tan_b[0] * tan_b[0] + tan_b[1] * tan_b[1] + tan_b[2] * tan_b[2]
    second_l = curve_aa[0] * unit[0] + curve_aa[1] * unit[1] + curve_aa[2] * unit[2]
    second_m = curve_ab[0] * unit[0] + curve_ab[1] * unit[1] + curve_ab[2] * unit[2]
    second_n = curve_bb[0] * unit[0] + curve_bb[1] * unit[1] + curve_bb[2] * unit[2]
    curvature = (first_edge_term * second_n - 2.0 * first_f * second_m + first_g * second_l) / (
        2.0 * area_stretch_factor * area_stretch_factor
    )
    omega = (grad_a[3] / area_stretch_factor, grad_b[3] / area_stretch_factor)
    return (unit, curvature, omega)


def factors(length):
    inner = min(length, 256)
    return (length // inner, inner)


def angles(count_one, count_two, modulus):
    sample_lattice = (
        jnp.arange(count_one, dtype=jnp.int32)[:, None]
        * jnp.arange(count_two, dtype=jnp.int32)[None, :]
        % modulus
    )
    theta = sample_lattice.astype(jnp.float32) * (2.0 * math.pi / modulus)
    return (jnp.cos(theta), jnp.sin(theta))


def rotation(cos_table, sin_table, sense):
    top = jnp.stack([cos_table, sense * sin_table])
    low = jnp.stack([-sense * sin_table, cos_table])
    return jnp.stack([top, low])


def twisted(sheet_portion, cos_table, sin_table, sense):
    twist_re = sheet_portion[0] * cos_table + sense * sheet_portion[1] * sin_table
    twist_im = sheet_portion[1] * cos_table - sense * sheet_portion[0] * sin_table
    return jnp.stack([twist_re, twist_im])


def forward(values, length, kept, real_input):
    outer, inner = factors(length)
    cos_outer, sin_outer = angles(outer, outer, outer)
    if real_input:
        leading = values.shape[:-1]
        sample_lattice = values.reshape(leading + (outer, inner))
        lookup_array = jnp.stack([cos_outer, -sin_outer])
        sheet_portion = jnp.einsum(
            "...lm,zln->z...nm", sample_lattice, lookup_array, precision=largest_wavenumber
        )
    else:
        leading = values.shape[1:-1]
        sample_lattice = values.reshape((2,) + leading + (outer, inner))
        sheet_portion = jnp.einsum(
            "s...ab,tsac->t...cb",
            sample_lattice,
            rotation(cos_outer, sin_outer, 1.0),
            precision=largest_wavenumber,
        )
    cos_twist, sin_twist = angles(outer, inner, length)
    sheet_portion = twisted(sheet_portion, cos_twist, sin_twist, 1.0)
    cos_inner, sin_inner = angles(inner, kept, inner)
    result = jnp.einsum(
        "s...cb,tsbd->t...cd",
        sheet_portion,
        rotation(cos_inner, sin_inner, 1.0),
        precision=largest_wavenumber,
    )
    return result.reshape((2,) + leading + (outer * kept,))


def inverse(values, length, kept, want_imag):
    outer, inner = factors(length)
    leading = values.shape[1:-1]
    sample_lattice = values.reshape((2,) + leading + (outer, kept))
    cos_inner, sin_inner = angles(kept, inner, inner)
    sheet_portion = jnp.einsum(
        "s...cd,tsdb->t...cb",
        sample_lattice,
        rotation(cos_inner, sin_inner, -1.0),
        precision=largest_wavenumber,
    )
    cos_twist, sin_twist = angles(outer, inner, length)
    sheet_portion = twisted(sheet_portion, cos_twist, sin_twist, -1.0)
    cos_outer, sin_outer = angles(outer, outer, outer)
    if want_imag:
        result = jnp.einsum(
            "s...cb,tsca->t...ab",
            sheet_portion,
            rotation(cos_outer, sin_outer, -1.0),
            precision=largest_wavenumber,
        )
        return result.reshape((2,) + leading + (length,)) / length
    lookup_array = jnp.stack([cos_outer, -sin_outer])
    result = jnp.einsum(
        "s...cb,sca->...ab", sheet_portion, lookup_array, precision=largest_wavenumber
    )
    return result.reshape(leading + (length,)) / length


def wavenumbers(length, kept, positions):
    outer, inner = factors(length)
    number = positions // kept + outer * (positions % kept)
    signed = jnp.where(number >= length // 2, number - length, number)
    return (signed.astype(jnp.float32) / length, number == length // 2)


def local(shift_plane, height, dipole):
    fields = jnp.concatenate([shift_plane, height[None], dipole[None]], 0)
    padded = padded_2(fields, (("tr", 1), ("tc", 2)), 2)
    grad_a = rows_first(padded)[..., 2:-2]
    grad_b = cols_first(padded)[..., 2:-2, :]
    curve_aa = rows_second(padded[:3])[..., 2:-2]
    curve_bb = second_column_split(padded[:3])[..., 2:-2, :]
    curve_ab = rows_first(cols_first(padded[:3]))
    unit, curvature, omega = surface(grad_a, grad_b, curve_aa, curve_bb, curve_ab)
    vorticity = jnp.stack([omega[0], omega[1]])
    sheet_rows = lax.all_to_all(vorticity, "tc", split_axis=1, concat_axis=2, tiled=True)
    col_count = sheet_rows.shape[-1]
    row_count = height.shape[0] * lax.axis_size("tr")
    col_outer, col_inner = factors(col_count)
    row_outer, row_inner = factors(row_count)
    kept = col_inner // 2
    row_spec = forward(sheet_rows, col_count, kept, True)
    stacked = row_spec.reshape((4,) + row_spec.shape[2:])
    columns = lax.all_to_all(stacked, ("tr", "tc"), split_axis=2, concat_axis=1, tiled=True)
    columns = jnp.swapaxes(columns, 1, 2)
    local_width = columns.shape[1]
    full = forward(columns.reshape((2, 2) + columns.shape[1:]), row_count, row_inner, False)
    complete_real_part = full[0]
    full_im = full[1]
    place = lax.axis_index(("tr", "tc")) * local_width + jnp.arange(local_width, dtype=jnp.int32)
    freq_two, nyquist_two = wavenumbers(col_count, kept, place)
    freq_one, nyquist_one = wavenumbers(
        row_count, row_inner, jnp.arange(row_count, dtype=jnp.int32)
    )
    freq_one = freq_one[None, :]
    freq_two = freq_two[:, None]
    radius = jnp.sqrt(freq_one * freq_one + freq_two * freq_two)
    live = (
        jnp.logical_not(nyquist_one[None, :])
        & jnp.logical_not(nyquist_two[:, None])
        & (radius > 0.0)
    )
    factor = jnp.where(live, 0.5 / jnp.where(live, radius, 1.0), 0.0)
    summed_re = factor * (freq_one * complete_real_part[0] + freq_two * complete_real_part[1])
    summed_im = factor * (freq_one * full_im[0] + freq_two * full_im[1])
    speed_parts = inverse(jnp.stack([summed_im, -summed_re]), row_count, row_inner, True)
    partial_value = jnp.swapaxes(speed_parts, 1, 2)
    back_rows = lax.all_to_all(partial_value, ("tr", "tc"), split_axis=1, concat_axis=2, tiled=True)
    weights = (
        jnp.full((col_outer, kept), 2.0, jnp.float32).at[0, 0].set(1.0).reshape(col_outer * kept)
    )
    speed_rows = inverse(back_rows * weights, col_count, kept, False)
    speed = lax.all_to_all(speed_rows, "tc", split_axis=1, concat_axis=0, tiled=True)
    velocity_update = jnp.stack([speed * unit[0], speed * unit[1], speed * unit[2]])
    dipole_update = -2.0 * 0.5 * 0.5 * height + 0.3 * curvature + 0.5 * speed * speed
    return (velocity_update, dipole_update)


def solution(mesh):
    in_specs = (
        P(None, ("groups", "tr"), "tc"),
        P(("groups", "tr"), "tc"),
        P(("groups", "tr"), "tc"),
    )
    out_specs = (P(None, ("groups", "tr"), "tc"), P(("groups", "tr"), "tc"))
    return jax.shard_map(local, mesh=mesh, in_specs=in_specs, out_specs=out_specs, check_vma=False)
```

profile of v0, /device:TPU:21, one launch (start us, length us, event | category | flops | bytes accessed | tf_op | source)
XLA Modules:
  0.0 736.5 jit_solution(17802370308646644525)
XLA Ops:
  5.6 1.7 collective-permute-done
  7.4 8.5 %pad_maximum_fusion.1 = f32[4,516,2048]{2,1,0:T(8,128)S(1)} fusion(f32[4,2,2048]{2,1,0:T(2,128)S(1)} %copy.106, f32[1,512,2048]{2,1,0:T(8,128)S(1)} %bitcast.310, f32[1,512,2048]{2,1,0:T(8,128)S(1)} %bitcast.306, f32[2,512,2048]{2,1,0:T(8,128)S(1)} %bitcast.303, f32[4,2,2048]{2,1,0:T(2,128)S(1)} %copy.105), kind=kLoop, calls=%fused_computation.14 | loop fusion | flops 16908288 | bytes 33816576 | tf_op jit(solution)/shard_map/concatenate | solution.py:20
  15.9 5.8 copy-done
  22.9 2.1 collective-permute-start.2
  27.0 22.0 %concatenate.26 = f32[4,516,2052]{2,1,0:T(8,128)} concatenate(f32[4,516,2]{2,1,0:T(8,128)S(1)} %copy.109, f32[4,516,2048]{2,1,0:T(8,128)} %copy-done, f32[4,516,2]{2,1,0:T(8,128)S(1)} %copy.110), dimensions={2} | concatenate | bytes 33882624 | tf_op jit(solution)/shard_map/concatenate | solution.py:20
  49.0 31.9 %maximum_maximum_fusion = (f32[4,516,2050]{2,1,0:T(8,128)}, f32[4,516,2050]{2,1,0:T(8,128)}) fusion(f32[4,2,2048]{2,1,0:T(2,128)S(1)} %copy.106, f32[1,512,2048]{2,1,0:T(8,128)} %bitcast.309, f32[1,512,2048]{2,1,0:T(8,128)} %bitcast.305, f32[2,512,2048]{2,1,0:T(8,128)} %param.5, f32[4,2,2048]{2,1,0:T(2,128)S(1)} %copy.105, f32[4,516,2]{2,1,0:T(8,128)S(1)} %copy.109, ...), kind=kLoop, calls=%fused_computation | loop fusion | flops 42312000 | bytes 50790912 | tf_op jit(solution)/shard_map/concatenate | solution.py:20
  80.9 31.6 %fusion = f32[4,512,2052]{2,1,0:T(8,128)} fusion(f32[4,516,2052]{2,1,0:T(8,128)} %concatenate.26), kind=kLoop, calls=%fused_computation.3 | loop fusion | flops 25214976 | bytes 84049920 | tf_op jit(solution)/shard_map/div | solution.py:25
  112.6 34.9 %fusion.3 = f32[4,516,2048]{2,1,0:T(8,128)} fusion(f32[4,516,2050]{2,1,0:T(8,128)} %get-tuple-element.26, f32[4,516,2050]{2,1,0:T(8,128)} %get-tuple-element.25), kind=kLoop, calls=%fused_computation.9 | loop fusion | flops 25362432 | bytes 84541440 | tf_op jit(solution)/shard_map/div | solution.py:34
  147.5 18.2 %slice_multiply_fusion.11 = (f32[1,512,2048]{2,1,0:T(8,128)}, f32[1,512,2048]{2,1,0:T(8,128)S(1)}, f32[1,512,2048]{2,1,0:T(8,128)}, f32[1,512,2048]{2,1,0:T(8,128)}, f32[1,512,2048]{2,1,0:T(8,128)}) fusion(f32[4,512,2052]{2,1,0:T(8,128)} %fusion, f32[4,516,2048]{2,1,0:T(8,128)} %fusion.3), kind=kLoop, calls=%fused_computation.92 | loop fusion | flops 17825792 | bytes 50331648 | tf_op jit(solution)/shard_map/div | solution.py:84
  165.7 4.7 slice_multiply_fusion.10
  171.8 7.3 copy.113
  179.1 10.7 %all_to_all.64 = f32[2,512,2048]{2,0,1:T(2,128)S(1)} all-to-all(f32[2,512,2048]{2,0,1:T(2,128)S(1)} %copy.113), channel_id=1, replica_groups=mesh['groups'=2,'tr'=8,'tc'=2] {'tc'}, dimensions={1} | all-to-all | bytes 16777216 | tf_op jit(solution)/shard_map/all_to_all | solution.py:192
  189.7 9.7 %copy.170 = f32[2,2,256,2048]{3,1,2,0:T(2,128)} copy(f32[2,2,256,2048]{3,0,2,1:T(2,128)S(1)} %bitcast.312) | data formatting | bytes 16777216 | tf_op jit(solution)/shard_map/all_to_all | solution.py:192
  199.5 11.5 %reshape.791 = f32[2,256,16,256,1]{3,2,1,0,4:T(8,128)} reshape(f32[2,256,2,2048]{3,2,1,0:T(2,128)} %bitcast.313) | data formatting | bytes 16777216 | tf_op jit(solution)/shard_map/reshape | solution.py:120
  211.0 16.0 %convolution_bitcast_fusion = f32[2,2,256,16,256]{4,3,2,1,0:T(8,128)S(1)} fusion(f32[2,256,16,256,1]{3,2,1,0,4:T(8,128)} %reshape.791, f32[1,16,16]{1,2,0:T(8,128)S(1)} %get-tuple-element.58, f32[1,16,16]{1,2,0:T(8,128)S(1)} %get-tuple-element.59), kind=kOutput, calls=%fused_computation.53 | convolution fusion | flops 805306880 | bytes 25167872 | tf_op jit(solution)/shard_map/...lm,zln->z...nm/dot_general | solution.py:122
  227.0 7.1 multiply_add_fusion
  234.1 6.9 pad_maximum_fusion.2
  241.0 23.2 %fusion.6 = f32[2,128,2,256,16,1]{3,1,5,4,2,0:T(8,128)} fusion(f32[2,2,256,16,256]{4,3,2,1,0:T(8,128)S(1)} %pad_maximum_fusion.2, f32[1,2,256,128]{2,3,1,0:T(8,128)S(1)} %copy-done.12, f32[1,2,256,128]{2,3,1,0:T(8,128)S(1)} %copy-done.11), kind=kOutput, calls=%fused_computation.16 | convolution fusion | flops 12885032960 | bytes 25690112 | tf_op jit(solution)/shard_map/s...cb,tsbd->t...cd/dot_general | solution.py:137
  264.2 11.8 %copy.116 = f32[4,256,2048]{1,0,2:T(4,128)} copy(f32[4,256,2048]{1,2,0:T(8,128)} %bitcast.307) | data formatting | bytes 16777216 | tf_op jit(solution)/shard_map/reshape;reshape | solution.py:199
  276.0 10.2 %all-to-all-start.1 = ((f32[4,256,2048]{1,0,2:T(4,128)}), f32[4,256,2048]{1,0,2:T(4,128)}, u32[]{:S(2)}, u32[]{:S(2)}) async-start(f32[4,256,2048]{1,0,2:T(4,128)} %copy.116), calls=%async_computation.1 | async-start | bytes 16777216 | tf_op jit(solution)/shard_map/all_to_all | solution.py:200
  288.7 179.2 %all-to-all-done.1 = f32[4,256,2048]{1,0,2:T(4,128)} async-done(((f32[4,256,2048]{1,0,2:T(4,128)}), f32[4,256,2048]{1,0,2:T(4,128)}, u32[]{:S(2)}, u32[]{:S(2)}) %all-to-all-start.1) | async-done | bytes 8388640 | tf_op jit(solution)/shard_map/all_to_all | solution.py:200
  467.9 5.0 copy.117
  472.9 12.8 %fusion.69 = f32[2,2,128,16,256]{4,3,2,1,0:T(8,128)S(1)} fusion(f32[2,2,128,16,256]{4,2,3,1,0:T(8,128)S(1)} %bitcast.311, f32[1,2,16,16]{2,3,1,0:T(8,128)S(1)} %get-tuple-element.53, f32[1,2,16,16]{2,3,1,0:T(8,128)S(1)} %get-tuple-element.56), kind=kOutput, calls=%fused_computation.127 | convolution fusion | flops 805307392 | bytes 16781312 | tf_op jit(solution)/shard_map/s...ab,tsac->t...cb/dot_general | solution.py:128
  485.8 1.8 multiply_add_fusion.2
  488.5 18.4 %fusion.66 = f32[2,2,128,16,256]{2,4,3,1,0:T(8,128)S(1)} fusion(f32[2,2,128,16,256]{4,3,2,1,0:T(8,128)S(1)} %pad_maximum_fusion.5, f32[1,2,256,256]{2,3,1,0:T(8,128)S(1)} %get-tuple-element.43, f32[1,2,256,256]{2,3,1,0:T(8,128)S(1)} %get-tuple-element.46), kind=kOutput, calls=%fused_computation.126 | convolution fusion | flops 12885164032 | bytes 17825792 | tf_op jit(solution)/shard_map/s...cb,tsbd->t...cd/dot_general | solution.py:137
  506.9 2.9 fusion.82
  509.9 7.2 fusion.74
  517.0 1.4 multiply_add_fusion.3
  518.4 2.3 pad_maximum_fusion.7
  520.7 5.4 copy.122
  526.2 7.9 %fusion.59 = f32[2,128,16,256]{3,2,1,0:T(8,128)} fusion(f32[2,128,16,256]{3,2,0,1:T(8,128)} %copy.122, f32[1,2,16,16]{2,3,1,0:T(8,128)S(1)} %get-tuple-element.57, f32[1,2,16,16]{2,3,1,0:T(8,128)S(1)} %get-tuple-element.52), kind=kOutput, calls=%fused_computation.112 | convolution fusion | flops 403702784 | bytes 8392704 | tf_op jit(solution)/shard_map/s...cb,tsca->t...ab/dot_general | solution.py:161
  534.0 5.2 copy.146
  539.3 5.5 all-to-all-start.2
  545.8 34.2 %fusion.16 = (f32[3,516,2048]{2,1,0:T(8,128)}, f32[3,516,2048]{2,1,0:T(8,128)}) fusion(f32[4,516,2048]{2,1,0:T(8,128)} %copy-done, f32[4,516,2050]{2,1,0:T(8,128)} %get-tuple-element.26, f32[4,516,2050]{2,1,0:T(8,128)} %get-tuple-element.25), kind=kLoop, calls=%fused_computation.32 | loop fusion | flops 47554560 | bytes 88768512 | tf_op jit(solution)/shard_map/div | solution.py:50
  580.0 27.0 %fusion.17 = f32[3,512,2048]{2,1,0:T(8,128)} fusion(f32[3,516,2048]{2,1,0:T(8,128)} %get-tuple-element.22), kind=kLoop, calls=%fused_computation.35 | loop fusion | flops 18874368 | bytes 62914560 | tf_op jit(solution)/shard_map/div | solution.py:25
  607.0 28.6 %fusion.9 = f32[3,512,2052]{2,1,0:T(8,128)} fusion(f32[4,516,2052]{2,1,0:T(8,128)} %concatenate.26), kind=kLoop, calls=%fused_computation.20 | loop fusion | flops 28366848 | bytes 75644928 | tf_op jit(solution)/shard_map/div | solution.py:40
  636.8 2.5 copy.124
  639.3 6.8 fusion.63
  646.1 1.4 multiply_add_fusion.1
  647.6 4.0 pad_maximum_fusion.6
  651.5 10.3 %copy.126 = f32[2,256,16,256]{3,2,0,1:T(8,128)} copy(f32[2,256,16,256]{1,3,2,0:T(8,128)} %pad_maximum_fusion.6) | data formatting | bytes 16777216 | tf_op jit(solution)/shard_map/stack | solution.py:112
  661.9 7.7 %fusion.56 = f32[256,16,256]{2,1,0:T(8,128)} fusion(f32[2,256,16,256]{3,2,0,1:T(8,128)} %copy.126, f32[1,16,16]{1,2,0:T(8,128)S(1)} %get-tuple-element.58, f32[1,16,16]{1,2,0:T(8,128)S(1)} %copy-done.14), kind=kOutput, calls=%fused_computation.108 | convolution fusion | flops 403702272 | bytes 12584960 | tf_op jit(solution)/shard_map/s...cb,sca->...ab/dot_general | solution.py:169
  669.6 6.1 div.165
  675.7 4.8 copy.127
  680.5 8.0 %all_to_all.65 = f32[256,2,2048]{2,0,1:T(8,128)S(1)} all-to-all(f32[256,2,2048]{2,0,1:T(8,128)S(1)} %copy.127), channel_id=1, replica_groups=mesh['groups'=2,'tr'=8,'tc'=2] {'tc'}, dimensions={1} | all-to-all | bytes 8388608 | tf_op jit(solution)/shard_map/all_to_all | solution.py:229
  688.5 5.9 bitcast_multiply_fusion.5
  694.4 11.8 %pad_maximum_fusion.3 = f32[3,512,2048]{2,1,0:T(8,128)} fusion(f32[1,512,2048]{2,1,0:T(8,128)} %get-tuple-element.39, f32[1,512,2048]{2,1,0:T(8,128)} %get-tuple-element.38, f32[1,512,2048]{2,1,0:T(8,128)} %get-tuple-element.37), kind=kLoop, calls=%fused_computation.40 | loop fusion | flops 6291456 | bytes 25165824 | tf_op jit(solution)/shard_map/stack | solution.py:230
  706.1 29.8 %fusion.29 = f32[512,2048]{1,0:T(8,128)} fusion(f32[3,512,2052]{2,1,0:T(8,128)} %fusion.9, f32[3,512,2048]{2,1,0:T(8,128)} %fusion.17, f32[3,516,2048]{2,1,0:T(8,128)} %get-tuple-element.21, f32[256,2,2048]{2,0,1:T(8,128)} %copy-done.9, f32[1,512,2048]{2,1,0:T(8,128)} %get-tuple-element.20, f32[1,512,2048]{2,1,0:T(8,128)} %get-tuple-element.19, ...), kind=kLoop, calls=%fused_computation.59 | loop fusion | flops 57671680 | bytes 88080384 | tf_op jit(solution)/shard_map/add | solution.py:231
  (73 shorter events, 15.1 us)
Async XLA Ops:
  0.6 6.7 slice-start
  0.6 6.7 slice-start.1
  0.7 6.7 copy-start.1
  0.7 6.7 copy-start.5
  2.0 3.5 collective-permute-start.1
  3.2 4.1 collective-permute-start
  15.9 5.8 copy-start
  22.9 3.7 collective-permute-start.2
  25.0 1.2 collective-permute-start.3
  25.1 185.9 %copy-start.13 = (f32[1,16,16]{1,2,0:T(8,128)}, f32[1,16,16]{1,2,0:T(8,128)S(1)}, u32[]{:S(2)}) copy-start(f32[1,16,16]{1,2,0:T(8,128)S(1)} %get-tuple-element.59) | copy-start | bytes 3076
  165.7 4.7 copy-start.3
  165.7 5.0 copy-start.10
  234.1 6.9 copy-start.11
  234.1 6.9 copy-start.12
  276.0 191.9 %all-to-all-start.1 = ((f32[4,256,2048]{1,0,2:T(4,128)}), f32[4,256,2048]{1,0,2:T(4,128)}, u32[]{:S(2)}, u32[]{:S(2)}) async-start(f32[4,256,2048]{1,0,2:T(4,128)} %copy.116), calls=%async_computation.1 | async-start | bytes 16777216 | tf_op jit(solution)/shard_map/all_to_all | solution.py:200
  539.3 97.5 %all-to-all-start.2 = ((f32[2,4096,128]{2,0,1:T(2,128)}), f32[2,4096,128]{2,0,1:T(2,128)}, u32[]{:S(2)}, u32[]{:S(2)}) async-start(f32[2,4096,128]{2,0,1:T(2,128)} %bitcast.314), calls=%async_computation.2 | async-start | bytes 8388608 | tf_op jit(solution)/shard_map/all_to_all | solution.py:224
  635.6 3.7 copy-start.15
  651.5 10.3 %copy-start.14 = (f32[1,16,16]{1,2,0:T(8,128)S(1)}, f32[1,16,16]{1,2,0:T(8,128)}, u32[]{:S(2)}) copy-start(f32[1,16,16]{1,2,0:T(8,128)} %copy-done.13) | copy-start | bytes 3076
  675.7 12.8 %copy-start.7 = (f32[1,512,2048]{2,1,0:T(8,128)S(1)}, f32[1,512,2048]{2,1,0:T(8,128)}, u32[]{:S(2)}) copy-start(f32[1,512,2048]{2,1,0:T(8,128)} %get-tuple-element.19) | copy-start | bytes 12582916
  675.7 12.8 %copy-start.8 = (f32[1,512,2048]{2,1,0:T(8,128)S(1)}, f32[1,512,2048]{2,1,0:T(8,128)}, u32[]{:S(2)}) copy-start(f32[1,512,2048]{2,1,0:T(8,128)} %get-tuple-element.20) | copy-start | bytes 12582916
  680.5 8.0 %copy-start.4 = (f32[1,512,2048]{2,1,0:T(8,128)S(1)}, f32[1,512,2048]{2,1,0:T(8,128)}, u32[]{:S(2)}) copy-start(f32[1,512,2048]{2,1,0:T(8,128)} %copy-done.3) | copy-start | bytes 12582916
  680.5 8.0 %copy-start.6 = (f32[1,512,2048]{2,1,0:T(8,128)S(1)}, f32[1,512,2048]{2,1,0:T(8,128)}, u32[]{:S(2)}) copy-start(f32[1,512,2048]{2,1,0:T(8,128)} %get-tuple-element.18) | copy-start | bytes 12582916
  688.5 5.9 copy-start.9
  694.4 11.8 %copy-start.2 = (f32[512,2048]{1,0:T(8,128)S(1)}, f32[512,2048]{1,0:T(8,128)}, u32[]{:S(2)}) copy-start(f32[512,2048]{1,0:T(8,128)} %param.6) | copy-start | bytes 12582916
where the time goes:
time: 746 us; the launch traced here: 736 us
  other arithmetic  304 us (41%)
  waiting for transfers between devices  183 us (25%)
  local copies, waits for them, and re-layouts  110 us (15%)
  matrix products  100 us (13%)
  starting transfers between devices  19.5 us (3%)
  blocking collectives  18.7 us (3%)
    all_to_all x1, waiting for transfers between devices, local(): lax.all_to_all(stacked, ('tr', 'tc'), split_axis=2, concat_axis=1, tiled=...  179 us
    div x2, other arithmetic, rows_first(): (field[..., :-4, :] - 8.0 * field[..., 1:-3, :] + 8.0 * field[..., 3:-1,...  58.6 us
    dot_general x2, matrix products, forward(): jnp.einsum('s...cb,tsbd->t...cd', sheet_portion, rotation(cos_inner, sin_...  41.6 us
    concatenate x2, other arithmetic, padded_2(): x = jnp.concatenate([before, x, after], axis=dim)  40.4 us
    div x1, other arithmetic, cols_first(): (field[..., :-4] - 8.0 * field[..., 1:-3] + 8.0 * field[..., 3:-1] - fiel...  34.9 us
    div x1, other arithmetic, second_column_split(): (-field[..., :-4] + 16.0 * field[..., 1:-3] - 30.0 * field[..., 2:-2] + 1...  34.2 us
    add x1, other arithmetic, local(): -2.0 * 0.5 * 0.5 * height + 0.3 * curvature + 0.5 * speed * speed  29.8 us
    div x1, other arithmetic, rows_second(): (-field[..., :-4, :] + 16.0 * field[..., 1:-3, :] - 30.0 * field[..., 2:-...  28.6 us
  transfers between devices with their start and end apart: 6, of which 4 were waited for; matrix products, arithmetic and copies ran while one was open for 13% of the time, Pallas kernels for 0%

commit v1 on v0

v1 whole, which is shorter than its diff:
```python
import functools

import jax
import jax.numpy as jnp
import numpy as np
from jax import lax
from jax.experimental import pallas as pl
from jax.experimental.pallas import tpu as pltpu
from jax.sharding import PartitionSpec as P

LANE = 128
SUB = 8
F32 = jnp.float32
BF16 = jnp.bfloat16
VMEM_LIMIT = 60 * 1024 * 1024


def times_unit(value, turn, count):
    re, im = value
    turn %= count
    if turn == 0:
        return value
    if 4 * turn == count:
        return (-im, re)
    if 2 * turn == count:
        return (-re, -im)
    if 4 * turn == 3 * count:
        return (im, -re)
    c = float(np.cos(2 * np.pi * turn / count))
    s = float(np.sin(2 * np.pi * turn / count))
    if 8 * turn % count == 0:
        h = abs(c)
        if c * s > 0:
            out = (h * (re - im), h * (re + im))
        else:
            out = (h * (re + im), h * (im - re))
        if c < 0:
            out = (-out[0], -out[1])
        return out
    return (c * re - s * im, c * im + s * re)


def add(p, q):
    return (p[0] + q[0], p[1] + q[1])


def sub(p, q):
    return (p[0] - q[0], p[1] - q[1])


def fft_list(vals, sign):
    n = len(vals)
    if n == 1:
        return vals
    if n == 2:
        return [add(vals[0], vals[1]), sub(vals[0], vals[1])]
    quarter = n // 4
    parts = [fft_list(vals[j::4], sign) for j in range(4)]
    out = [None] * n
    for k in range(quarter):
        t = [times_unit(parts[j][k], sign * j * k, n) for j in range(4)]
        a, b = add(t[0], t[2]), sub(t[0], t[2])
        c, d = add(t[1], t[3]), sub(t[1], t[3])
        d = (-d[1], d[0]) if sign > 0 else (d[1], -d[0])
        out[k] = add(a, c)
        out[k + quarter] = add(b, d)
        out[k + 2 * quarter] = sub(a, c)
        out[k + 3 * quarter] = sub(b, d)
    return out


def rfft_list(vals):
    n = len(vals)
    if n == 2:
        return [(vals[0] + vals[1], None), (vals[0] - vals[1], None)]
    even, odd = rfft_list(vals[0::2]), rfft_list(vals[1::2])
    out = [None] * (n // 2 + 1)
    out[0] = (even[0][0] + odd[0][0], None)
    out[n // 2] = (even[0][0] - odd[0][0], None)
    for k in range(1, n // 4):
        t = times_unit(odd[k], -k, n)
        out[k] = add(even[k], t)
        low = sub(even[k], t)
        out[n // 2 - k] = (low[0], -low[1])
    out[n // 4] = (even[n // 4][0], -odd[n // 4][0])
    return out


def irfft_list(spec):
    n = 2 * (len(spec) - 1)
    if n == 2:
        return [spec[0][0] + spec[1][0], spec[0][0] - spec[1][0]]
    q = n // 4
    even, odd = [None] * (q + 1), [None] * (q + 1)
    even[0] = (spec[0][0] + spec[n // 2][0], None)
    odd[0] = (spec[0][0] - spec[n // 2][0], None)
    for k in range(1, q):
        other = (spec[n // 2 - k][0], -spec[n // 2 - k][1])
        even[k] = add(spec[k], other)
        odd[k] = times_unit(sub(spec[k], other), k, n)
    even[q] = (2.0 * spec[q][0], None)
    odd[q] = (-2.0 * spec[q][1], None)
    out = [None] * n
    out[0::2] = irfft_list(even)
    out[1::2] = irfft_list(odd)
    return out


def hi_lo(table):
    hi = table.astype(np.float32).astype(jnp.bfloat16)
    lo = (table - hi.astype(np.float64)).astype(np.float32).astype(jnp.bfloat16)
    return hi, lo


def row_numbers(length):
    outer = length // LANE
    blocks, half = outer // 2, LANE // 2
    number = np.arange(blocks)[:, None] + outer * np.arange(LANE)[None, :]
    number[0, :half] = outer * np.arange(half)
    number[0, half:] = blocks + outer * np.arange(half)
    return number


def row_tables(length):
    outer = length // LANE
    blocks, half = outer // 2, LANE // 2
    number = row_numbers(length)
    place = np.arange(LANE)
    ahead = np.zeros((blocks, 2 * LANE, 2 * LANE))
    back = np.zeros((blocks, 2 * LANE, 2 * LANE))
    for k in range(blocks):
        theta = 2 * np.pi * ((number[k][:, None] * place[None, :]) % length) / length
        c, s = np.cos(theta), np.sin(theta)
        if k:
            ahead[k] = np.block([[c, s], [-s, c]])
            back[k] = np.block([[c.T, -s.T], [s.T, c.T]])
        else:
            zero = np.zeros((half, LANE))
            ahead[0] = np.block(
                [[c[:half], zero], [zero, c[half:]], [-s[:half], zero], [zero, -s[half:]]]
            )
            weight = np.full((half, 1), 2.0)
            weight[0] = 1.0
            back[0] = np.block(
                [
                    [(weight * c[:half]).T, zero.T, -(weight * s[:half]).T, zero.T],
                    [zero.T, 2 * c[half:].T, zero.T, -2 * s[half:].T],
                ]
            )
    def packed(t):
        hi, lo = hi_lo(t)
        return np.concatenate([hi, lo, hi], axis=-1)

    return packed(ahead), packed(back)


def col_tables(length, scale):
    outer = length // LANE
    place = np.arange(LANE)
    theta = 2 * np.pi * ((place[:, None] * place[None, :]) % LANE) / LANE
    c, s = np.cos(theta), np.sin(theta)
    ahead = np.block([[c, -s], [s, c]])
    turned = np.block([[s, -c], [c, s]])
    back = turned * scale
    def packed(t):
        hi, lo = hi_lo(t)
        return np.concatenate([hi, lo, hi], axis=0)

    first = np.arange(outer)[:, None]
    angle = 2 * np.pi * ((first * place[None, :]) % length) / length
    twist = np.stack([np.cos(angle), np.sin(angle)]).astype(np.float32)
    twist = np.ascontiguousarray(np.broadcast_to(twist[:, :, None, :], (2, outer, SUB, LANE)))
    number = first + outer * place[None, :]
    signed = np.where(number >= length // 2, number - length, number)
    freq = (signed / length).astype(np.float32)
    live = np.where(number == length // 2, 0.0, 0.5).astype(np.float32)
    freq = np.stack([freq, live])[:, :, None, :]
    freq = np.ascontiguousarray(np.broadcast_to(freq, (2, outer, SUB, LANE)))
    return packed(ahead), packed(back), twist, freq


def split(x):
    hi = x.astype(BF16)
    return hi, (x - hi.astype(F32)).astype(BF16)


def params(**more):
    return pltpu.CompilerParams(vmem_limit_bytes=VMEM_LIMIT, **more)


def whole(array):
    zeros = (0,) * array.ndim
    return pl.BlockSpec(array.shape, lambda *_: zeros, pipeline_mode=pl.Buffered(1))


def row_kernel(x_ref, w_ref, o_ref, s_ref):
    sides, _, rows, width = x_ref.shape
    per = width // LANE
    outer = sides * per
    blocks = outer // 2

    for field in range(2):

        def short(g, _, field=field):
            at = pl.ds(pl.multiple_of(g * SUB, SUB), SUB)
            vals = [
                x_ref[a // per, field, at, (a % per) * LANE : (a % per + 1) * LANE]
                for a in range(outer)
            ]
            spec = rfft_list(vals)
            to = pl.ds(pl.multiple_of(field * rows + g * SUB, SUB), SUB)
            s_ref[0, to, :LANE] = spec[0][0]
            s_ref[0, to, LANE:] = spec[blocks][0]
            for k in range(1, blocks):
                s_ref[k, to, :LANE] = spec[k][0]
                s_ref[k, to, LANE:] = spec[k][1]
            return 0

        lax.fori_loop(0, rows // SUB, short, 0)

    def long(k, _):
        hi, lo = split(s_ref[k])
        y = lax.dot_general(
            w_ref[k],
            jnp.concatenate([hi, hi, lo], axis=1),
            (((1,), (1,)), ((), ())),
            preferred_element_type=F32,
        )
        for field in range(2):
            for part in range(2):
                o_ref[k, 2 * field + part] = y[
                    part * LANE : (part + 1) * LANE, field * rows : (field + 1) * rows
                ]
        return 0

    lax.fori_loop(0, blocks, long, 0, unroll=2)


def row_forward(x, table):
    sides, _, rows, width = x.shape
    blocks = sides * width // LANE // 2
    step = LANE if rows % LANE == 0 else rows
    return pl.pallas_call(
        row_kernel,
        grid=(rows // step,),
        in_specs=[
            pl.BlockSpec((sides, 2, step, width), lambda i: (0, 0, i, 0)),
            whole(table),
        ],
        out_specs=pl.BlockSpec((blocks, 4, LANE, step), lambda i: (0, 0, 0, i)),
        out_shape=jax.ShapeDtypeStruct((blocks, 4, LANE, rows), F32),
        scratch_shapes=[pltpu.VMEM((blocks, 2 * step, 2 * LANE), F32)],
        compiler_params=params(),
        name="row_forward",
    )(x, table)


def col_kernel(x_ref, f2_ref, wf_ref, wb_ref, tw_ref, f1_ref, o_ref, a_ref, z_ref, *, chunk):
    sources, _, _, count, length = x_ref.shape
    per = length // LANE
    outer = tw_ref.shape[1]

    for field in range(2):

        def short(g, _, field=field):
            at = pl.ds(pl.multiple_of(g * SUB, SUB), SUB)

            def part(a, which):
                lanes = slice((a % per) * LANE, (a % per + 1) * LANE)
                return x_ref[a // per, 0, 2 * field + which, at, lanes]

            spec = fft_list([(part(a, 0), part(a, 1)) for a in range(outer)], -1)
            for k in range(outer):
                re, im = spec[k]
                if k:
                    c, s = tw_ref[0, k], tw_ref[1, k]
                    re, im = (re * c + im * s, im * c - re * s)
                a_ref[field, k, at, :LANE] = re
                a_ref[field, k, at, LANE:] = im
            return 0

        lax.fori_loop(0, count // SUB, short, 0)

    f2 = f2_ref[0]
    f2_square = jnp.maximum(f2 * f2, 1e-30)

    def long(j, _):
        at = pl.ds(j * chunk, chunk)

        def product(x, w_ref):
            hi, lo = split(x.reshape(chunk * count, 2 * LANE))
            return jnp.dot(
                jnp.concatenate([hi, hi, lo], axis=1), w_ref[...], preferred_element_type=F32
            ).reshape(chunk, count, 2 * LANE)

        y0 = product(a_ref[0, at], wf_ref)
        y1 = product(a_ref[1, at], wf_ref)
        f1 = f1_ref[0, at][:, :1]
        factor = f1_ref[1, at][:, :1] * lax.rsqrt(f1 * f1 + f2_square[None])
        m0, m1 = factor * f1, factor * f2[None]
        m0 = jnp.concatenate([m0, m0], axis=-1)
        m1 = jnp.concatenate([m1, m1], axis=-1)
        z_ref[at] = product(m0 * y0 + m1 * y1, wb_ref)
        return 0

    lax.fori_loop(0, outer // chunk, long, 0)

    def last(g, _):
        at = pl.ds(pl.multiple_of(g * SUB, SUB), SUB)
        vals = []
        for k in range(outer):
            re, im = z_ref[k, at, :LANE], z_ref[k, at, LANE:]
            if k:
                c, s = tw_ref[0, k], tw_ref[1, k]
                re, im = (re * c - im * s, im * c + re * s)
            vals.append((re, im))
        res = fft_list(vals, 1)
        for a in range(outer):
            lanes = slice((a % per) * LANE, (a % per + 1) * LANE)
            o_ref[a // per, 0, 0, at, lanes] = res[a][0]
            o_ref[a // per, 0, 1, at, lanes] = res[a][1]
        return 0

    lax.fori_loop(0, count // SUB, last, 0)


def col_stage(x, f2, tables):
    sources, u, _, n, rows = x.shape
    outer = sources * rows // LANE
    step = n
    while step > 32 and step % 2 == 0:
        step //= 2
    chunk = max(1, min(outer, 256 // step))
    return pl.pallas_call(
        functools.partial(col_kernel, chunk=chunk),
        grid=(u, n // step),
        in_specs=[
            pl.BlockSpec((sources, 1, 4, step, rows), lambda i, j: (0, i, 0, j, 0)),
            pl.BlockSpec((1, step, LANE), lambda i, j: (i, j, 0)),
        ]
        + [whole(t) for t in tables],
        out_specs=pl.BlockSpec((sources, 1, 2, step, rows), lambda i, j: (0, i, 0, j, 0)),
        out_shape=jax.ShapeDtypeStruct((sources, u, 2, n, rows), F32),
        scratch_shapes=[
            pltpu.VMEM((2, outer, step, 2 * LANE), F32),
            pltpu.VMEM((outer, step, 2 * LANE), F32),
        ],
        compiler_params=params(),
        name="col_stage",
    )(x, f2, *tables)


def back_kernel(x_ref, w_ref, o_ref, z_ref, t_ref):
    blocks, _, _, rows = x_ref.shape
    sides, _, width = o_ref.shape
    outer = 2 * blocks
    per = width // LANE

    def long(k, _):
        hi, lo = split(x_ref[k].reshape(2 * LANE, rows))
        z_ref[k] = jnp.dot(
            w_ref[k], jnp.concatenate([hi, hi, lo], axis=0), preferred_element_type=F32
        )
        return 0

    lax.fori_loop(0, blocks, long, 0, unroll=2)

    def short(g, _):
        at = pl.ds(pl.multiple_of(g * SUB, SUB), SUB)
        low = pl.ds(pl.multiple_of(LANE + g * SUB, SUB), SUB)
        spec = [(z_ref[0, at], None)]
        spec += [(z_ref[k, at], z_ref[k, low]) for k in range(1, blocks)]
        spec += [(z_ref[0, low], None)]
        res = irfft_list(spec)
        for a in range(outer):
            t_ref[a, at] = res[a]
        return 0

    lax.fori_loop(0, LANE // SUB, short, 0)

    for a in range(outer):
        lanes = slice((a % per) * LANE, (a % per + 1) * LANE)
        o_ref[a // per, :, lanes] = t_ref[a].T


def row_back(x, table, sides):
    blocks, _, _, rows = x.shape
    width = 2 * blocks * LANE // sides
    step = LANE if rows % LANE == 0 else rows
    return pl.pallas_call(
        back_kernel,
        grid=(rows // step,),
        in_specs=[
            pl.BlockSpec((blocks, 2, LANE, step), lambda i: (0, 0, 0, i)),
            whole(table),
        ],
        out_specs=pl.BlockSpec((sides, step, width), lambda i: (0, i, 0)),
        out_shape=jax.ShapeDtypeStruct((sides, rows, width), F32),
        scratch_shapes=[
            pltpu.VMEM((blocks, 2 * LANE, step), F32),
            pltpu.VMEM((2 * blocks, LANE, step), F32),
        ],
        compiler_params=params(),
        name="row_back",
    )(x, table)


def diff_one(m2, m1, p1, p2):
    return (p1 - m1) * (2.0 / 3.0) - (p2 - m2) * (1.0 / 12.0)


def diff_two(m2, m1, zero, p1, p2):
    return (p1 + m1) * (4.0 / 3.0) - (p2 + m2) * (1.0 / 12.0) - 2.5 * zero


def normal_of(ga, gb):
    a = (1.0 + ga[0], ga[1], ga[2])
    b = (gb[0], 1.0 + gb[1], gb[2])
    normal = (
        a[1] * b[2] - a[2] * b[1],
        a[2] * b[0] - a[0] * b[2],
        a[0] * b[1] - a[1] * b[0],
    )
    return a, b, normal


def dot3(p, q):
    return p[0] * q[0] + p[1] * q[1] + p[2] * q[2]


def fill(ext_ref, index, refs, field, edge):
    block, prev, after = refs
    rows, width = block.shape[-2:]
    top_ref, low_ref, left_ref, right_ref = edge
    i, n = pl.program_id(0), pl.num_programs(0)
    mid = slice(LANE, LANE + width)
    ext_ref[index, SUB : SUB + rows, mid] = block[field]
    ext_ref[index, :SUB, mid] = jnp.where(i == 0, top_ref[index], prev[field])
    ext_ref[index, SUB + rows :, mid] = jnp.where(i == n - 1, low_ref[index], after[field])
    lines = left_ref.shape[1]
    if lines == rows:
        ext_ref[index, SUB : SUB + rows, :LANE] = left_ref[index]
        ext_ref[index, SUB : SUB + rows, LANE + width :] = right_ref[index]
    else:
        at = pl.ds(pl.multiple_of(i * rows, SUB), rows + 2 * SUB)
        ext_ref[index, :, :LANE] = left_ref[index, at]
        ext_ref[index, :, LANE + width :] = right_ref[index, at]


def shifted(x, by, width):
    total = x.shape[-1]
    return pltpu.roll(x, (-by) % total, x.ndim - 1)[..., LANE : LANE + width]


def tiles(rows, width, body):
    wide = 2 * LANE if width % (2 * LANE) == 0 else LANE
    across = width // wide

    def step(t, _):
        r = pl.multiple_of((t // across) * SUB, SUB)
        c = pl.multiple_of((t % across) * wide, LANE)
        body(r, c, wide)
        return 0

    lax.fori_loop(0, rows // SUB * across, step, 0)


def around(ext_ref, index, r, c, wide):
    return ext_ref[index, pl.ds(r, 3 * SUB), pl.ds(c, wide + 2 * LANE)]


def vorticity_kernel(*refs):
    planes, heights, dipoles, edge = refs[0:3], refs[3:6], refs[6:9], refs[9:13]
    o_ref, ext_ref = refs[13], refs[14]
    rows, width = o_ref.shape[-2:]
    for index, (source, field) in enumerate(
        [(planes, 0), (planes, 1), (heights, 0), (dipoles, 0)]
    ):
        fill(ext_ref, index, source, field, edge)

    def body(r, c, wide):
        ga, gb = [], []
        for index in range(4):
            x = around(ext_ref, index, r, c, wide)
            tall = x[:, LANE : LANE + wide]
            ga.append(diff_one(*[tall[SUB + s : 2 * SUB + s] for s in (-2, -1, 1, 2)]))
            flat = x[SUB : 2 * SUB]
            gb.append(diff_one(*[shifted(flat, s, wide) for s in (-2, -1, 1, 2)]))
        _, _, normal = normal_of(ga, gb)
        inverse = lax.rsqrt(dot3(normal, normal))
        o_ref[0, 0, pl.ds(r, SUB), pl.ds(c, wide)] = ga[3] * inverse
        o_ref[0, 1, pl.ds(r, SUB), pl.ds(c, wide)] = gb[3] * inverse

    tiles(rows, width, body)


def geometry_kernel(*refs):
    planes, heights, edge = refs[0:3], refs[3:6], refs[6:10]
    unit_ref, base_ref, ext_ref = refs[10:13]
    rows, width = base_ref.shape[-2:]
    for index, (source, field) in enumerate([(planes, 0), (planes, 1), (heights, 0)]):
        fill(ext_ref, index, source, field, edge)

    def body(r, c, wide):
        ga, gb, caa, cbb, cab = [], [], [], [], []
        for index in range(3):
            x = around(ext_ref, index, r, c, wide)
            moved = [shifted(x, s, wide) for s in (-2, -1, 1, 2)]
            across = diff_one(*moved)
            tall = x[:, LANE : LANE + wide]
            rowed = [tall[SUB + s : 2 * SUB + s] for s in (-2, -1, 0, 1, 2)]
            ga.append(diff_one(rowed[0], rowed[1], rowed[3], rowed[4]))
            caa.append(diff_two(*rowed))
            gb.append(across[SUB : 2 * SUB])
            m = [v[SUB : 2 * SUB] for v in moved]
            cbb.append(diff_two(m[0], m[1], rowed[2], m[2], m[3]))
            cab.append(diff_one(*[across[SUB + s : 2 * SUB + s] for s in (-2, -1, 1, 2)]))
            if index == 2:
                height = rowed[2]
        a, b, normal = normal_of(ga, gb)
        inverse = lax.rsqrt(dot3(normal, normal))
        top = (
            dot3(a, a) * dot3(cbb, normal)
            - 2.0 * dot3(a, b) * dot3(cab, normal)
            + dot3(b, b) * dot3(caa, normal)
        )
        curvature = 0.5 * top * (inverse * inverse * inverse)
        at = (pl.ds(r, SUB), pl.ds(c, wide))
        for axis in range(3):
            unit_ref[(axis,) + at] = normal[axis] * inverse
        base_ref[at] = 0.3 * curvature - 0.5 * height

    tiles(rows, width, body)


def row_step(rows):
    step = 64
    while rows % step:
        step //= 2
    return step


def block_specs(count, step, rows, width):
    per, total = step // SUB, rows // SUB
    return [
        pl.BlockSpec((count, step, width), lambda i: (0, i, 0)),
        pl.BlockSpec((count, SUB, width), lambda i: (0, jnp.maximum(i * per - 1, 0), 0)),
        pl.BlockSpec((count, SUB, width), lambda i: (0, jnp.minimum((i + 1) * per, total - 1), 0)),
    ]


def vorticity_stage(planes, height, dipole, edge, sides):
    _, rows, width = planes.shape
    part = rows // sides
    step = row_step(part)
    rim = lambda: pl.BlockSpec((4, step, LANE), lambda i: (0, i, 0))
    return pl.pallas_call(
        vorticity_kernel,
        grid=(rows // step,),
        in_specs=block_specs(2, step, rows, width)
        + block_specs(1, step, rows, width) * 2
        + [whole(edge[0]), whole(edge[1]), rim(), rim()],
        out_specs=pl.BlockSpec(
            (1, 2, step, width), lambda i: (i // (part // step), 0, i % (part // step), 0)
        ),
        out_shape=jax.ShapeDtypeStruct((sides, 2, part, width), F32),
        scratch_shapes=[pltpu.VMEM((4, step + 2 * SUB, width + 2 * LANE), F32)],
        compiler_params=params(),
        name="vorticity_stage",
    )(*[planes] * 3, *[height[None]] * 3, *[dipole[None]] * 3, *edge)


def geometry_stage(planes, height, edge):
    _, rows, width = planes.shape
    step = row_step(rows)
    return pl.pallas_call(
        geometry_kernel,
        grid=(rows // step,),
        in_specs=block_specs(2, step, rows, width)
        + block_specs(1, step, rows, width)
        + [whole(e) for e in edge],
        out_specs=[
            pl.BlockSpec((3, step, width), lambda i: (0, i, 0)),
            pl.BlockSpec((step, width), lambda i: (i, 0)),
        ],
        out_shape=[
            jax.ShapeDtypeStruct((3, rows, width), F32),
            jax.ShapeDtypeStruct((rows, width), F32),
        ],
        scratch_shapes=[pltpu.VMEM((3, step + 2 * SUB, width + 2 * LANE), F32)],
        compiler_params=params(),
        cost_estimate=pl.CostEstimate(
            flops=200 * rows * width, bytes_accessed=7 * 4 * rows * width, transcendentals=rows * width
        ),
        name="geometry_stage",
    )(*[planes] * 3, *[height[None]] * 3, *edge)


def final_kernel(speed_ref, unit_ref, base_ref, velocity_ref, update_ref):
    speed = speed_ref[...]
    for axis in range(3):
        velocity_ref[axis] = speed * unit_ref[axis]
    update_ref[...] = base_ref[...] + 0.5 * speed * speed


def final_stage(speed, unit, base):
    rows, width = base.shape
    step = row_step(rows)
    three = lambda: pl.BlockSpec((3, step, width), lambda i: (0, i, 0))
    one = lambda: pl.BlockSpec((step, width), lambda i: (i, 0))
    return pl.pallas_call(
        final_kernel,
        grid=(rows // step,),
        in_specs=[one(), three(), one()],
        out_specs=[three(), one()],
        out_shape=[
            jax.ShapeDtypeStruct((3, rows, width), F32),
            jax.ShapeDtypeStruct((rows, width), F32),
        ],
        compiler_params=params(),
        name="final_stage",
    )(speed, unit, base)


def both_ways(last, initial, axis):
    devices = lax.axis_size(axis)
    up = [(i, (i + 1) % devices) for i in range(devices)]
    down = [(j, i) for i, j in up]
    return lax.ppermute(last, axis, up), lax.ppermute(initial, axis, down)


def local(shift_plane, height, dipole):
    _, rows, width = shift_plane.shape
    tr, tc = lax.axis_size("tr"), lax.axis_size("tc")
    devices = tr * tc
    row_count, col_count = rows * tr, width * tc
    part = rows // tc

    def cut(a, b, dim):
        pieces = [shift_plane, height[None], dipole[None]]
        return jnp.concatenate([lax.slice_in_dim(p, a, b, axis=dim) for p in pieces], 0)

    left, right = both_ways(cut(width - LANE, width, 2), cut(0, LANE, 2), "tc")
    top, low = both_ways(cut(rows - SUB, rows, 1), cut(0, SUB, 1), "tr")
    vorticity = vorticity_stage(
        shift_plane, height, dipole, (top, low, left, right), tc
    )
    sheet = lax.all_to_all(vorticity, "tc", split_axis=0, concat_axis=0, tiled=True)
    row_table, back_table = row_tables(col_count)
    spec = row_forward(sheet, row_table)
    blocks = spec.shape[0]
    n = blocks * LANE // devices
    u = max(1, n // LANE)
    n = n // u
    pieces = LANE // n
    spec = spec.reshape(blocks, 4, pieces, n, part)
    spec = jnp.swapaxes(spec, 1, 2).reshape(devices, u, 4, n, part)
    columns = lax.all_to_all(spec, ("tr", "tc"), split_axis=0, concat_axis=0, tiled=True)

    ends = jnp.stack([top[:3], low[:3]])
    left_ends, right_ends = both_ways(ends[..., width - LANE :], ends[..., :LANE], "tc")
    edge = (
        top[:3],
        low[:3],
        jnp.concatenate([left_ends[0], left[:3], left_ends[1]], 1),
        jnp.concatenate([right_ends[0], right[:3], right_ends[1]], 1),
    )
    unit, base = geometry_stage(shift_plane, height, edge)

    direct = part % LANE == 0
    if not direct:
        columns = columns.transpose(1, 2, 3, 0, 4).reshape(1, u, 4, n, row_count)
    number = row_numbers(col_count).reshape(-1)
    signed = np.where(number >= col_count // 2, number - col_count, number)
    freq = (signed / col_count).astype(np.float32)
    freq = np.ascontiguousarray(np.broadcast_to(freq[:, None], (freq.size, LANE)))
    place = lax.axis_index(("tr", "tc")) * (u * n)
    mine = lax.dynamic_slice_in_dim(jnp.asarray(freq), place, u * n, 0).reshape(u, n, LANE)
    tables = col_tables(row_count, 1.0 / (row_count * col_count))
    partial = col_stage(columns, mine, tables)
    if not direct:
        partial = partial.reshape(u, 2, n, devices, part).transpose(3, 0, 1, 2, 4)
    back = lax.all_to_all(partial, ("tr", "tc"), split_axis=0, concat_axis=0, tiled=True)
    back = back.reshape(blocks, pieces, 2, n, part)
    back = jnp.swapaxes(back, 1, 2).reshape(blocks, 2, LANE, part)
    speed_rows = row_back(back, back_table, tc)
    speed = lax.all_to_all(speed_rows, "tc", split_axis=0, concat_axis=0, tiled=True)
    velocity_update, dipole_update = final_stage(speed.reshape(rows, width), unit, base)
    return (velocity_update, dipole_update)


def solution(mesh):
    in_specs = (
        P(None, ("groups", "tr"), "tc"),
        P(("groups", "tr"), "tc"),
        P(("groups", "tr"), "tc"),
    )
    out_specs = (P(None, ("groups", "tr"), "tc"), P(("groups", "tr"), "tc"))
    return jax.shard_map(local, mesh=mesh, in_specs=in_specs, out_specs=out_specs, check_vma=False)
```

time: 746 us -> 501 us (0.67)
  other arithmetic: 304 us -> 2.08 us
  Pallas kernels: 0 us -> 247 us
  local copies, waits for them, and re-layouts: 110 us -> 9.5 us
  matrix products: 100 us -> 0 us
  blocking collectives: 18.7 us -> 30.3 us
  waiting for transfers between devices: 183 us -> 194 us
    pallas_call x0 -> x6, Pallas kernels: none -> 247 us  [the longest x1 112 us: geometry_stage(): pl.pallas_call(geometry_kernel, grid=(rows // step,), in_specs=block_spec...]
    div x9 -> x0, other arithmetic: 179 us -> none  [the longest x2 58.6 us: rows_first(): (field[..., :-4, :] - 8.0 * field[..., 1:-3, :] + 8.0 * field[..., 3:-1,...]
    dot_general x8 -> x0, matrix products: 100 us -> none  [the longest x2 41.6 us: forward(): jnp.einsum('s...cb,tsbd->t...cd', sheet_portion, rotation(cos_inner, sin_...]
    add x5 -> x0, other arithmetic: 41.5 us -> none  [the longest x1 29.8 us: local(): -2.0 * 0.5 * 0.5 * height + 0.3 * curvature + 0.5 * speed * speed]
    concatenate x2 -> x6, other arithmetic: 40.4 us -> 2.07 us  [the longest x1 0.96 us: local(): jnp.concatenate([right_ends[0], right[:3], right_ends[1]], 1)]
    another operation x4 -> x2, local copies, waits for them, and re-layouts: 34.9 us -> 1.41 us  [local(): ends = jnp.stack([top[:3], low[:3]])]
    another operation x10 -> x1, other arithmetic: 28 us -> 0.01 us  [local(): ends = jnp.stack([top[:3], low[:3]])]
    concatenate x1 -> x0, local copies, waits for them, and re-layouts: 22 us -> none  [padded_2(): x = jnp.concatenate([before, x, after], axis=dim)]
  transfers between devices with their start and end apart: 6 -> 8, of which waited for: 4 -> 5; matrix products, arithmetic and copies ran while one was open for 13% -> 1% of each run, Pallas kernels for 0% -> 22%
where the time goes in v1:
time: 501 us; the launch traced here: 498 us
  Pallas kernels  247 us (49%)
  waiting for transfers between devices  194 us (39%)
  blocking collectives  30.3 us (6%)
  starting transfers between devices  14.5 us (3%)
  local copies, waits for them, and re-layouts  9.5 us (2%)
    all_to_all x1, waiting for transfers between devices, local(): lax.all_to_all(spec, ('tr', 'tc'), split_axis=0, concat_axis=0, tiled=True)  181 us
    pallas_call x1, Pallas kernels, geometry_stage(): pl.pallas_call(geometry_kernel, grid=(rows // step,), in_specs=block_spec...  112 us
    pallas_call x1, Pallas kernels, vorticity_stage(): pl.pallas_call(vorticity_kernel, grid=(rows // step,), in_specs=block_spe...  72.4 us
    pallas_call x1, Pallas kernels, col_stage(): pl.pallas_call(functools.partial(col_kernel, chunk=chunk), grid=(u, n //...  20 us
    all_to_all x1, blocking collectives, local(): lax.all_to_all(vorticity, 'tc', split_axis=0, concat_axis=0, tiled=True)  18.6 us
    pallas_call x1, Pallas kernels, row_forward(): pl.pallas_call(row_kernel, grid=(rows // step,), in_specs=[pl.BlockSpec((...  15.2 us
    pallas_call x1, Pallas kernels, final_stage(): pl.pallas_call(final_kernel, grid=(rows // step,), in_specs=[one(), three...  14.6 us
    pallas_call x1, Pallas kernels, row_back(): pl.pallas_call(back_kernel, grid=(rows // step,), in_specs=[pl.BlockSpec(...  13.4 us
  transfers between devices with their start and end apart: 8, of which 5 were waited for; matrix products, arithmetic and copies ran while one was open for 1% of the time, Pallas kernels for 22%

profile of v1, /device:TPU:21, one launch (start us, length us, event | category | flops | bytes accessed | tf_op | source)
XLA Modules:
  0.0 498.5 jit_solution(9677581636662105785)
XLA Ops:
  0.6 1.3 fusion
  1.9 1.3 fusion.2
  3.2 0.1 pad_maximum_fusion
  3.3 0.7 collective-permute-start.2
  4.0 0.1 pad_maximum_fusion.1
  4.1 0.1 collective-permute-start.3
  4.2 1.0 fusion.4
  5.1 1.0 fusion.1
  6.1 1.3 collective-permute-start
  7.4 1.2 collective-permute-start.1
  8.6 9.6 %collective-permute-done.refs_9_ = f32[4,8,2048]{2,1,0:T(8,128)S(1)} collective-permute-done((f32[4,8,2048]{2,1,0:T(8,128)S(1)}, f32[4,8,2048]{2,1,0:T(8,128)S(1)}, u32[]{:S(2)}, u32[]{:S(2)}) %collective-permute-start) | collective-permute-done | bytes 262176 | tf_op jit(solution)/shard_map/ppermute | solution.py:629
  18.2 0.0 copy-start.2
  18.2 2.7 collective-permute-done.1.refs_10_
  20.9 0.0 copy-start.4
  20.9 0.0 collective-permute-done.2.refs_11_
  20.9 0.0 copy-start
  20.9 0.0 collective-permute-done.3.refs_12_
  20.9 0.0 copy-done.2
  21.0 0.7 copy-done.4
  21.6 0.4 copy-done
  22.1 1.0 copy-done.1
  23.1 72.4 %vorticity_stage.1 = f32[2,2,256,2048]{3,2,1,0:T(8,128)} custom-call(f32[2,512,2048]{2,1,0:T(8,128)} %refs_2_.3, f32[2,512,2048]{2,1,0:T(8,128)} %refs_2_.3, f32[2,512,2048]{2,1,0:T(8,128)} %refs_2_.3, f32[1,512,2048]{2,1,0:T(8,128)} %bitcast.21, f32[1,512,2048]{2,1,0:T(8,128)} %bitcast.22, f32[1,512,2048]{2,1,0:T(8,128)} %bitcast.23, ...), custom_call_target="tpu_custom_call" | custom-call | tf_op jit(solution)/shard_map/vorticity_stage/pallas_call | solution.py:557
  95.5 18.6 %all_to_all.20.x_ref = f32[2,2,256,2048]{3,2,1,0:T(8,128)} all-to-all(f32[2,2,256,2048]{3,2,1,0:T(8,128)} %vorticity_stage.1), channel_id=1, replica_groups=mesh['groups'=2,'tr'=8,'tc'=2] {'tc'}, dimensions={0} | all-to-all | bytes 16777216 | tf_op jit(solution)/shard_map/all_to_all | solution.py:648
  114.1 15.2 %row_forward.1 = f32[16,4,128,256]{3,2,1,0:T(8,128)} custom-call(f32[2,2,256,2048]{3,2,1,0:T(8,128)} %all_to_all.20.x_ref, bf16[16,256,768]{2,1,0:T(8,128)(2,1)} %constant.30.clone.w_ref), custom_call_target="tpu_custom_call" | custom-call | tf_op jit(solution)/shard_map/row_forward/pallas_call | solution.py:243
  129.2 5.4 %all-to-all-start.1 = ((f32[16,1,4,128,256]{4,3,2,1,0:T(8,128)}), f32[16,1,4,128,256]{4,3,2,1,0:T(8,128)}, u32[]{:S(2)}, u32[]{:S(2)}) async-start(f32[16,1,4,128,256]{4,3,2,1,0:T(8,128)} %bitcast.32), calls=%async_computation.1 | async-start | bytes 16777216 | tf_op jit(solution)/shard_map/all_to_all | solution.py:658
  134.6 1.5 dynamic-slice_bitcast_fusion.f2_ref
  136.1 180.6 %all-to-all-done.1.x_ref = f32[16,1,4,128,256]{4,3,2,1,0:T(8,128)} async-done(((f32[16,1,4,128,256]{4,3,2,1,0:T(8,128)}), f32[16,1,4,128,256]{4,3,2,1,0:T(8,128)}, u32[]{:S(2)}, u32[]{:S(2)}) %all-to-all-start.1) | async-done | bytes 8388640 | tf_op jit(solution)/shard_map/all_to_all | solution.py:658
  316.7 20.0 %col_stage.1 = f32[16,1,2,128,256]{4,3,2,1,0:T(8,128)} custom-call(f32[16,1,4,128,256]{4,3,2,1,0:T(8,128)} %all-to-all-done.1.x_ref, f32[1,128,128]{2,1,0:T(8,128)} %dynamic-slice_bitcast_fusion.f2_ref, bf16[768,256]{1,0:T(8,128)(2,1)} %constant.32.clone.wf_ref, bf16[768,256]{1,0:T(8,128)(2,1)} %constant.33.clone.wb_ref, ...), custom_call_target="tpu_custom_call" | custom-call | tf_op jit(solution)/shard_map/col_stage/pallas_call | solution.py:334
  336.7 5.3 %all-to-all-start.2 = ((f32[16,1,2,128,256]{4,3,2,1,0:T(8,128)}), f32[16,1,2,128,256]{4,3,2,1,0:T(8,128)}, u32[]{:S(2)}, u32[]{:S(2)}) async-start(f32[16,1,2,128,256]{4,3,2,1,0:T(8,128)} %col_stage.1), calls=%async_computation.2 | async-start | bytes 8388608 | tf_op jit(solution)/shard_map/all_to_all | solution.py:683
  342.1 0.0 copy-done.5
  342.1 0.0 slice-start
  342.1 0.0 slice-start.1
  342.1 0.7 slice_bitcast_fusion.4
  342.8 0.0 copy-done.3
  342.8 0.7 slice_bitcast_fusion.5
  343.5 0.4 collective-permute-start.5
  343.9 0.1 collective-permute-start.4
  344.0 0.7 collective-permute-done.5
  344.7 0.3 collective-permute-done.4
  345.1 0.0 slice-done
  345.1 0.9 pad_maximum_fusion.2.refs_8_
  346.0 0.0 slice-done.1
  346.0 1.0 pad_maximum_fusion.3.refs_9_
  347.0 111.8 %geometry_stage.1 = (f32[3,512,2048]{2,1,0:T(8,128)}, f32[512,2048]{1,0:T(8,128)}) custom-call(f32[2,512,2048]{2,1,0:T(8,128)} %refs_2_.3, f32[2,512,2048]{2,1,0:T(8,128)} %refs_2_.3, f32[2,512,2048]{2,1,0:T(8,128)} %refs_2_.3, f32[1,512,2048]{2,1,0:T(8,128)} %bitcast.24, f32[1,512,2048]{2,1,0:T(8,128)} %bitcast.25, f32[1,512,2048]{2,1,0:T(8,128)} %bitcast.26, ...), custom_call_target="tpu_custom_call" | custom-call | flops 209715200 | bytes 29360128 | tf_op jit(solution)/shard_map/geometry_stage/pallas_call | solution.py:576
  458.8 0.0 all-to-all-done.2
  458.8 13.4 %row_back.1 = f32[2,256,2048]{2,1,0:T(8,128)} custom-call(f32[16,2,128,256]{3,2,1,0:T(8,128)} %bitcast.4.x_ref, bf16[16,256,768]{2,1,0:T(8,128)(2,1)} %constant.36.clone.w_ref), custom_call_target="tpu_custom_call" | custom-call | tf_op jit(solution)/shard_map/row_back/pallas_call | solution.py:390
  472.2 11.7 %all_to_all.21 = f32[2,256,2048]{2,1,0:T(8,128)} all-to-all(f32[2,256,2048]{2,1,0:T(8,128)} %row_back.1), channel_id=1, replica_groups=mesh['groups'=2,'tr'=8,'tc'=2] {'tc'}, dimensions={0} | all-to-all | bytes 8388608 | tf_op jit(solution)/shard_map/all_to_all | solution.py:687
  483.9 14.6 %final_stage.1 = (f32[3,512,2048]{2,1,0:T(8,128)}, f32[512,2048]{1,0:T(8,128)}) custom-call(f32[512,2048]{1,0:T(8,128)} %bitcast.33, f32[3,512,2048]{2,1,0:T(8,128)} %get-tuple-element.4.unit_ref, f32[512,2048]{1,0:T(8,128)} %get-tuple-element.5.base_ref), custom_call_target="tpu_custom_call" | custom-call | tf_op jit(solution)/shard_map/final_stage/pallas_call | solution.py:611
  (8 shorter events, 0.1 us)
Async XLA Ops:
  3.3 17.7 %collective-permute-start.2 = (f32[4,512,128]{2,1,0:T(8,128)S(1)}, f32[4,512,128]{2,1,0:T(8,128)S(1)}, u32[]{:S(2)}, u32[]{:S(2)}) collective-permute-start(f32[4,512,128]{2,1,0:T(8,128)S(1)} %pad_maximum_fusion), channel_id=1, source_target_pairs={{0,1},{1,0},{2,3},{3,2},{4,5},{5,4},{6,7},{7,6},{8,9},{9,8},{10,11... | collective-permute-start | bytes 3145736 | tf_op jit(solution)/shard_map/ppermute | solution.py:629
  4.1 16.9 %collective-permute-start.3 = (f32[4,512,128]{2,1,0:T(8,128)S(1)}, f32[4,512,128]{2,1,0:T(8,128)S(1)}, u32[]{:S(2)}, u32[]{:S(2)}) collective-permute-start(f32[4,512,128]{2,1,0:T(8,128)S(1)} %pad_maximum_fusion.1), channel_id=1, source_target_pairs={{1,0},{0,1},{3,2},{2,3},{5,4},{4,5},{7,6},{6,7},{9,8},{8,9},{11,10... | collective-permute-start | bytes 3145736 | tf_op jit(solution)/shard_map/ppermute | solution.py:629
  6.1 12.1 %collective-permute-start = (f32[4,8,2048]{2,1,0:T(8,128)S(1)}, f32[4,8,2048]{2,1,0:T(8,128)S(1)}, u32[]{:S(2)}, u32[]{:S(2)}) collective-permute-start(f32[4,8,2048]{2,1,0:T(8,128)S(1)} %pad_maximum_fusion.4), channel_id=1, source_target_pairs={{0,2},{2,4},{4,6},{6,8},{8,10},{10,12},{12,14},{14,0},{1,3},{3,5},... | collective-permute-start | bytes 786440 | tf_op jit(solution)/shard_map/ppermute | solution.py:629
  7.4 13.5 %collective-permute-start.1 = (f32[4,8,2048]{2,1,0:T(8,128)S(1)}, f32[4,8,2048]{2,1,0:T(8,128)S(1)}, u32[]{:S(2)}, u32[]{:S(2)}) collective-permute-start(f32[4,8,2048]{2,1,0:T(8,128)S(1)} %pad_maximum_fusion.5), channel_id=1, source_target_pairs={{2,0},{4,2},{6,4},{8,6},{10,8},{12,10},{14,12},{0,14},{3,1},{5,3},... | collective-permute-start | bytes 786440 | tf_op jit(solution)/shard_map/ppermute | solution.py:629
  18.2 2.7 copy-start.2
  20.9 0.7 copy-start.4
  20.9 1.1 copy-start
  22.1 1.0 copy-start.1
  129.2 187.5 %all-to-all-start.1 = ((f32[16,1,4,128,256]{4,3,2,1,0:T(8,128)}), f32[16,1,4,128,256]{4,3,2,1,0:T(8,128)}, u32[]{:S(2)}, u32[]{:S(2)}) async-start(f32[16,1,4,128,256]{4,3,2,1,0:T(8,128)} %bitcast.32), calls=%async_computation.1 | async-start | bytes 16777216 | tf_op jit(solution)/shard_map/all_to_all | solution.py:658
  336.7 5.3 %copy-start.5 = (f32[4,8,2048]{2,1,0:T(8,128)S(1)}, f32[4,8,2048]{2,1,0:T(8,128)}, u32[]{:S(2)}) copy-start(f32[4,8,2048]{2,1,0:T(8,128)} %copy-done.4) | copy-start | bytes 786436
  336.7 6.1 %copy-start.3 = (f32[4,8,2048]{2,1,0:T(8,128)S(1)}, f32[4,8,2048]{2,1,0:T(8,128)}, u32[]{:S(2)}) copy-start(f32[4,8,2048]{2,1,0:T(8,128)} %copy-done.2) | copy-start | bytes 786436
  336.7 122.1 %all-to-all-start.2 = ((f32[16,1,2,128,256]{4,3,2,1,0:T(8,128)}), f32[16,1,2,128,256]{4,3,2,1,0:T(8,128)}, u32[]{:S(2)}, u32[]{:S(2)}) async-start(f32[16,1,2,128,256]{4,3,2,1,0:T(8,128)} %col_stage.1), calls=%async_computation.2 | async-start | bytes 8388608 | tf_op jit(solution)/shard_map/all_to_all | solution.py:683
  342.1 3.0 slice-start
  342.1 3.9 slice-start.1
  343.5 1.2 collective-permute-start.5
  343.9 1.2 collective-permute-start.4

commit v2 on v1

--- a/solution.py
+++ b/solution.py
@@ -10,6 +10,8 @@
 
 LANE = 128
 SUB = 8
+MANY = 4
+RIM = 2
 F32 = jnp.float32
 BF16 = jnp.bfloat16
 VMEM_LIMIT = 60 * 1024 * 1024
@@ -148,8 +150,7 @@
                 ]
             )
     def packed(t):
-        hi, lo = hi_lo(t)
-        return np.concatenate([hi, lo, hi], axis=-1)
+        return np.concatenate(hi_lo(t), axis=1)
 
     return packed(ahead), packed(back)
 
@@ -193,20 +194,28 @@
     return pl.BlockSpec(array.shape, lambda *_: zeros, pipeline_mode=pl.Buffered(1))
 
 
-def row_kernel(x_ref, w_ref, o_ref, s_ref):
-    sides, _, rows, width = x_ref.shape
-    per = width // LANE
-    outer = sides * per
+def row_kernel(me_ref, *refs):
+    x_refs, (w_ref, o_ref, s_ref) = refs[:-3], refs[-3:]
+    sides = len(x_refs)
+    for me in range(sides):
+
+        @pl.when(me_ref[0] == me)
+        def _(me=me):
+            row_short([x_refs[(me - side) % sides] for side in range(sides)], s_ref)
+
+    row_long(w_ref, o_ref, s_ref, x_refs[0].shape[2])
+
+
+def row_short(x_refs, s_ref):
+    _, per, rows, _ = x_refs[0].shape
+    outer = len(x_refs) * per
     blocks = outer // 2
 
     for field in range(2):
 
         def short(g, _, field=field):
             at = pl.ds(pl.multiple_of(g * SUB, SUB), SUB)
-            vals = [
-                x_ref[a // per, field, at, (a % per) * LANE : (a % per + 1) * LANE]
-                for a in range(outer)
-            ]
+            vals = [x_refs[a // per][field, a % per, at] for a in range(outer)]
             spec = rfft_list(vals)
             to = pl.ds(pl.multiple_of(field * rows + g * SUB, SUB), SUB)
             s_ref[0, to, :LANE] = spec[0][0]
@@ -218,14 +227,18 @@
 
         lax.fori_loop(0, rows // SUB, short, 0)
 
+
+def three(w, x, dims):
+    hi, lo = split(x)
+    out = w.shape[0] // 2
+    both = lax.dot_general(w, hi, dims, preferred_element_type=F32)
+    rest = lax.dot_general(w[:out], lo, dims, preferred_element_type=F32)
+    return both[:out] + (both[out:] + rest)
+
+
+def row_long(w_ref, o_ref, s_ref, rows):
     def long(k, _):
-        hi, lo = split(s_ref[k])
-        y = lax.dot_general(
-            w_ref[k],
-            jnp.concatenate([hi, hi, lo], axis=1),
-            (((1,), (1,)), ((), ())),
-            preferred_element_type=F32,
-        )
+        y = three(w_ref[k], s_ref[k], (((1,), (1,)), ((), ())))
         for field in range(2):
             for part in range(2):
                 o_ref[k, 2 * field + part] = y[
@@ -233,26 +246,27 @@
                 ]
         return 0
 
-    lax.fori_loop(0, blocks, long, 0, unroll=2)
-
-
-def row_forward(x, table):
-    sides, _, rows, width = x.shape
-    blocks = sides * width // LANE // 2
+    lax.fori_loop(0, s_ref.shape[0], long, 0, unroll=4)
+
+
+def row_forward(pieces, me, table):
+    _, per, rows, _ = pieces[0].shape
+    blocks = len(pieces) * per // 2
     step = LANE if rows % LANE == 0 else rows
     return pl.pallas_call(
         row_kernel,
-        grid=(rows // step,),
-        in_specs=[
-            pl.BlockSpec((sides, 2, step, width), lambda i: (0, 0, i, 0)),
-            whole(table),
-        ],
-        out_specs=pl.BlockSpec((blocks, 4, LANE, step), lambda i: (0, 0, 0, i)),
+        grid_spec=pltpu.PrefetchScalarGridSpec(
+            num_scalar_prefetch=1,
+            grid=(rows // step,),
+            in_specs=[pl.BlockSpec((2, per, step, LANE), lambda i, _: (0, 0, i, 0)) for _ in pieces]
+            + [whole(table)],
+            out_specs=pl.BlockSpec((blocks, 4, LANE, step), lambda i, _: (0, 0, 0, i)),
+            scratch_shapes=[pltpu.VMEM((blocks, 2 * step, 2 * LANE), F32)],
+        ),
         out_shape=jax.ShapeDtypeStruct((blocks, 4, LANE, rows), F32),
-        scratch_shapes=[pltpu.VMEM((blocks, 2 * step, 2 * LANE), F32)],
         compiler_params=params(),
         name="row_forward",
-    )(x, table)
+    )(me[None], *pieces, table)
 
 
 def col_kernel(x_ref, f2_ref, wf_ref, wb_ref, tw_ref, f1_ref, o_ref, a_ref, z_ref, *, chunk):
@@ -330,7 +344,7 @@
     step = n
     while step > 32 and step % 2 == 0:
         step //= 2
-    chunk = max(1, min(outer, 256 // step))
+    chunk = max(1, min(outer, 1024 // step))
     return pl.pallas_call(
         functools.partial(col_kernel, chunk=chunk),
         grid=(u, n // step),
@@ -350,20 +364,18 @@
     )(x, f2, *tables)
 
 
-def back_kernel(x_ref, w_ref, o_ref, z_ref, t_ref):
+def back_kernel(me_ref, x_ref, w_ref, *refs):
+    o_refs, (z_ref, t_ref) = refs[:-2], refs[-2:]
     blocks, _, _, rows = x_ref.shape
-    sides, _, width = o_ref.shape
+    sides = len(o_refs)
+    per = o_refs[0].shape[0]
     outer = 2 * blocks
-    per = width // LANE
 
     def long(k, _):
-        hi, lo = split(x_ref[k].reshape(2 * LANE, rows))
-        z_ref[k] = jnp.dot(
-            w_ref[k], jnp.concatenate([hi, hi, lo], axis=0), preferred_element_type=F32
-        )
+        z_ref[k] = three(w_ref[k], x_ref[k].reshape(2 * LANE, rows), (((1,), (0,)), ((), ())))
         return 0
 
-    lax.fori_loop(0, blocks, long, 0, unroll=2)
+    lax.fori_loop(0, blocks, long, 0, unroll=4)
 
     def short(g, _):
         at = pl.ds(pl.multiple_of(g * SUB, SUB), SUB)
@@ -378,44 +390,50 @@
 
     lax.fori_loop(0, LANE // SUB, short, 0)
 
-    for a in range(outer):
-        lanes = slice((a % per) * LANE, (a % per + 1) * LANE)
-        o_ref[a // per, :, lanes] = t_ref[a].T
-
-
-def row_back(x, table, sides):
+    for me in range(sides):
+
+        @pl.when(me_ref[0] == me)
+        def _(me=me):
+            for a in range(outer):
+                o_refs[(a // per - me) % sides][a % per] = t_ref[a].T
+
+
+def row_back(x, me, table, sides):
     blocks, _, _, rows = x.shape
-    width = 2 * blocks * LANE // sides
+    per = 2 * blocks // sides
     step = LANE if rows % LANE == 0 else rows
     return pl.pallas_call(
         back_kernel,
-        grid=(rows // step,),
-        in_specs=[
-            pl.BlockSpec((blocks, 2, LANE, step), lambda i: (0, 0, 0, i)),
-            whole(table),
-        ],
-        out_specs=pl.BlockSpec((sides, step, width), lambda i: (0, i, 0)),
-        out_shape=jax.ShapeDtypeStruct((sides, rows, width), F32),
-        scratch_shapes=[
-            pltpu.VMEM((blocks, 2 * LANE, step), F32),
-            pltpu.VMEM((2 * blocks, LANE, step), F32),
-        ],
+        grid_spec=pltpu.PrefetchScalarGridSpec(
+            num_scalar_prefetch=1,
+            grid=(rows // step,),
+            in_specs=[
+                pl.BlockSpec((blocks, 2, LANE, step), lambda i, _: (0, 0, 0, i)),
+                whole(table),
+            ],
+            out_specs=[pl.BlockSpec((per, step, LANE), lambda i, _: (0, i, 0))] * sides,
+            scratch_shapes=[
+                pltpu.VMEM((blocks, 2 * LANE, step), F32),
+                pltpu.VMEM((2 * blocks, LANE, step), F32),
+            ],
+        ),
+        out_shape=[jax.ShapeDtypeStruct((per, rows, LANE), F32)] * sides,
         compiler_params=params(),
         name="row_back",
-    )(x, table)
+    )(me[None], x, table)
 
 
 def diff_one(m2, m1, p1, p2):
-    return (p1 - m1) * (2.0 / 3.0) - (p2 - m2) * (1.0 / 12.0)
+    return 8.0 * (p1 - m1) - (p2 - m2)
 
 
 def diff_two(m2, m1, zero, p1, p2):
-    return (p1 + m1) * (4.0 / 3.0) - (p2 + m2) * (1.0 / 12.0) - 2.5 * zero
+    return 16.0 * (p1 + m1) - (p2 + m2) - 30.0 * zero
 
 
 def normal_of(ga, gb):
-    a = (1.0 + ga[0], ga[1], ga[2])
-    b = (gb[0], 1.0 + gb[1], gb[2])
+    a = (12.0 + ga[0], ga[1], ga[2])
+    b = (gb[0], 12.0 + gb[1], gb[2])
     normal = (
         a[1] * b[2] - a[2] * b[1],
         a[2] * b[0] - a[0] * b[2],
@@ -428,109 +446,145 @@
     return p[0] * q[0] + p[1] * q[1] + p[2] * q[2]
 
 
-def fill(ext_ref, index, refs, field, edge):
+def fill(ext_ref, index, refs, field, edge, i, n):
     block, prev, after = refs
     rows, width = block.shape[-2:]
+    count = width // LANE
     top_ref, low_ref, left_ref, right_ref = edge
-    i, n = pl.program_id(0), pl.num_programs(0)
-    mid = slice(LANE, LANE + width)
-    ext_ref[index, SUB : SUB + rows, mid] = block[field]
-    ext_ref[index, :SUB, mid] = jnp.where(i == 0, top_ref[index], prev[field])
-    ext_ref[index, SUB + rows :, mid] = jnp.where(i == n - 1, low_ref[index], after[field])
-    lines = left_ref.shape[1]
-    if lines == rows:
-        ext_ref[index, SUB : SUB + rows, :LANE] = left_ref[index]
-        ext_ref[index, SUB : SUB + rows, LANE + width :] = right_ref[index]
+    for j in range(count):
+        at = slice(j * LANE, (j + 1) * LANE)
+        ext_ref[index, 1 + j, SUB : SUB + rows] = block[field, :, at]
+        ext_ref[index, 1 + j, :SUB] = prev[field, :, at]
+        ext_ref[index, 1 + j, SUB + rows :] = after[field, :, at]
+
+    @pl.when(i == 0)
+    def _():
+        for j in range(count):
+            at = slice(j * LANE, (j + 1) * LANE)
+            ext_ref[index, 1 + j, SUB - RIM : SUB] = top_ref[index, :, at]
+
+    @pl.when(i == n - 1)
+    def _():
+        for j in range(count):
+            at = slice(j * LANE, (j + 1) * LANE)
+            ext_ref[index, 1 + j, SUB + rows : SUB + rows + RIM] = low_ref[index, :, at]
+
+    if left_ref.shape[1] == rows:
+        ext_ref[index, 0, SUB : SUB + rows] = left_ref[index]
+        ext_ref[index, 1 + count, SUB : SUB + rows] = right_ref[index]
     else:
         at = pl.ds(pl.multiple_of(i * rows, SUB), rows + 2 * SUB)
-        ext_ref[index, :, :LANE] = left_ref[index, at]
-        ext_ref[index, :, LANE + width :] = right_ref[index, at]
-
-
-def shifted(x, by, width):
-    total = x.shape[-1]
-    return pltpu.roll(x, (-by) % total, x.ndim - 1)[..., LANE : LANE + width]
-
-
-def tiles(rows, width, body):
-    wide = 2 * LANE if width % (2 * LANE) == 0 else LANE
-    across = width // wide
-
-    def step(t, _):
-        r = pl.multiple_of((t // across) * SUB, SUB)
-        c = pl.multiple_of((t % across) * wide, LANE)
-        body(r, c, wide)
-        return 0
-
-    lax.fori_loop(0, rows // SUB * across, step, 0)
-
-
-def around(ext_ref, index, r, c, wide):
-    return ext_ref[index, pl.ds(r, 3 * SUB), pl.ds(c, wide + 2 * LANE)]
-
-
-def vorticity_kernel(*refs):
+        ext_ref[index, 0] = left_ref[index, at]
+        ext_ref[index, 1 + count] = right_ref[index, at]
+
+
+def neighbours(x):
+    count = x.shape[0] - 2
+    lane = lax.broadcasted_iota(jnp.int32, (count, SUB, LANE), 2)
+    out = []
+    for by in (-2, -1):
+        moved = pltpu.roll(x, -by, 2)
+        out.append(jnp.where(lane < -by, moved[:count], moved[1 : 1 + count]))
+    for by in (1, 2):
+        moved = pltpu.roll(x, LANE - by, 2)
+        out.append(jnp.where(lane >= LANE - by, moved[2:], moved[1 : 1 + count]))
+    return out
+
+
+def tile_count(count, most):
+    while count % most:
+        most -= 1
+    return most
+
+
+def spread(start, rows):
+    if rows == SUB:
+        return pl.ds(start, SUB)
+    return pl.ds(start, SUB, stride=rows // SUB)
+
+
+def vorticity_kernel(base_ref, *refs):
     planes, heights, dipoles, edge = refs[0:3], refs[3:6], refs[6:9], refs[9:13]
     o_ref, ext_ref = refs[13], refs[14]
-    rows, width = o_ref.shape[-2:]
+    _, count, rows, _ = o_ref.shape
+    i = base_ref[0] + pl.program_id(0)
     for index, (source, field) in enumerate(
         [(planes, 0), (planes, 1), (heights, 0), (dipoles, 0)]
     ):
-        fill(ext_ref, index, source, field, edge)
-
-    def body(r, c, wide):
-        ga, gb = [], []
-        for index in range(4):
-            x = around(ext_ref, index, r, c, wide)
-            tall = x[:, LANE : LANE + wide]
-            ga.append(diff_one(*[tall[SUB + s : 2 * SUB + s] for s in (-2, -1, 1, 2)]))
-            flat = x[SUB : 2 * SUB]
-            gb.append(diff_one(*[shifted(flat, s, wide) for s in (-2, -1, 1, 2)]))
-        _, _, normal = normal_of(ga, gb)
-        inverse = lax.rsqrt(dot3(normal, normal))
-        o_ref[0, 0, pl.ds(r, SUB), pl.ds(c, wide)] = ga[3] * inverse
-        o_ref[0, 1, pl.ds(r, SUB), pl.ds(c, wide)] = gb[3] * inverse
-
-    tiles(rows, width, body)
+        fill(ext_ref, index, source, field, edge, i, base_ref[1])
+    many = tile_count(count, MANY)
+
+    def body(t, _):
+        for c in range(0, count, many):
+            ga, gb = [], []
+            for index in range(4):
+
+                def load(s, lo, hi):
+                    return ext_ref[index, lo:hi, spread(SUB + t + s, rows)]
+
+                ga.append(diff_one(*[load(s, c + 1, c + 1 + many) for s in (-2, -1, 1, 2)]))
+                gb.append(diff_one(*neighbours(load(0, c, c + many + 2))))
+            _, _, normal = normal_of(ga, gb)
+            inverse = 12.0 * lax.rsqrt(dot3(normal, normal))
+            o_ref[0, c : c + many, spread(t, rows)] = ga[3] * inverse
+            o_ref[1, c : c + many, spread(t, rows)] = gb[3] * inverse
+        return 0
+
+    lax.fori_loop(0, rows // SUB, body, 0)
 
 
 def geometry_kernel(*refs):
     planes, heights, edge = refs[0:3], refs[3:6], refs[6:10]
-    unit_ref, base_ref, ext_ref = refs[10:13]
-    rows, width = base_ref.shape[-2:]
+    unit_ref, base_ref, ext_ref, first_ref, second_ref = refs[10:15]
+    count, rows, _ = base_ref.shape
+    i, n = pl.program_id(0), pl.num_programs(0)
     for index, (source, field) in enumerate([(planes, 0), (planes, 1), (heights, 0)]):
-        fill(ext_ref, index, source, field, edge)
-
-    def body(r, c, wide):
-        ga, gb, caa, cbb, cab = [], [], [], [], []
-        for index in range(3):
-            x = around(ext_ref, index, r, c, wide)
-            moved = [shifted(x, s, wide) for s in (-2, -1, 1, 2)]
-            across = diff_one(*moved)
-            tall = x[:, LANE : LANE + wide]
-            rowed = [tall[SUB + s : 2 * SUB + s] for s in (-2, -1, 0, 1, 2)]
-            ga.append(diff_one(rowed[0], rowed[1], rowed[3], rowed[4]))
-            caa.append(diff_two(*rowed))
-            gb.append(across[SUB : 2 * SUB])
-            m = [v[SUB : 2 * SUB] for v in moved]
-            cbb.append(diff_two(m[0], m[1], rowed[2], m[2], m[3]))
-            cab.append(diff_one(*[across[SUB + s : 2 * SUB + s] for s in (-2, -1, 1, 2)]))
-            if index == 2:
-                height = rowed[2]
-        a, b, normal = normal_of(ga, gb)
-        inverse = lax.rsqrt(dot3(normal, normal))
-        top = (
-            dot3(a, a) * dot3(cbb, normal)
-            - 2.0 * dot3(a, b) * dot3(cab, normal)
-            + dot3(b, b) * dot3(caa, normal)
-        )
-        curvature = 0.5 * top * (inverse * inverse * inverse)
-        at = (pl.ds(r, SUB), pl.ds(c, wide))
-        for axis in range(3):
-            unit_ref[(axis,) + at] = normal[axis] * inverse
-        base_ref[at] = 0.3 * curvature - 0.5 * height
-
-    tiles(rows, width, body)
+        fill(ext_ref, index, source, field, edge, i, n)
+    many = tile_count(count, MANY)
+
+    def along(g, _):
+        at = pl.ds(pl.multiple_of(g * SUB, SUB), SUB)
+        for c in range(0, count, many):
+            for index in range(3):
+                flat = ext_ref[index, c : c + many + 2, at]
+                m2, m1, p1, p2 = neighbours(flat)
+                first_ref[index, c : c + many, at] = diff_one(m2, m1, p1, p2)
+                second_ref[index, c : c + many, at] = diff_two(m2, m1, flat[1 : 1 + many], p1, p2)
+        return 0
+
+    lax.fori_loop(0, rows // SUB + 2, along, 0)
+
+    def body(t, _):
+        for c in range(0, count, many):
+            ga, gb, caa, cbb, cab = [], [], [], [], []
+            for index in range(3):
+                steps = (-2, -1, 0, 1, 2)
+                v = [
+                    ext_ref[index, c + 1 : c + 1 + many, spread(SUB + t + s, rows)] for s in steps
+                ]
+                ga.append(diff_one(v[0], v[1], v[3], v[4]))
+                caa.append(diff_two(*v))
+                f = [first_ref[index, c : c + many, spread(SUB + t + s, rows)] for s in steps]
+                gb.append(f[2])
+                cab.append(diff_one(f[0], f[1], f[3], f[4]))
+                cbb.append(second_ref[index, c : c + many, spread(SUB + t, rows)])
+                if index == 2:
+                    height = v[2]
+            a, b, normal = normal_of(ga, gb)
+            inverse = lax.rsqrt(dot3(normal, normal))
+            top = (
+                dot3(a, a) * dot3(cbb, normal)
+                - (2.0 / 12.0) * dot3(a, b) * dot3(cab, normal)
+                + dot3(b, b) * dot3(caa, normal)
+            )
+            curvature = (0.5 * 12.0) * top * (inverse * inverse * inverse)
+            at = (slice(c, c + many), spread(t, rows))
+            for axis in range(3):
+                unit_ref[(axis,) + at] = normal[axis] * inverse
+            base_ref[at] = 0.3 * curvature - 0.5 * height
+        return 0
+
+    lax.fori_loop(0, rows // SUB, body, 0)
 
 
 def row_step(rows):
@@ -542,36 +596,54 @@
 
 def block_specs(count, step, rows, width):
     per, total = step // SUB, rows // SUB
+
+    def at(i, base):
+        return i + base[0][0] if base else i
+
     return [
-        pl.BlockSpec((count, step, width), lambda i: (0, i, 0)),
-        pl.BlockSpec((count, SUB, width), lambda i: (0, jnp.maximum(i * per - 1, 0), 0)),
-        pl.BlockSpec((count, SUB, width), lambda i: (0, jnp.minimum((i + 1) * per, total - 1), 0)),
+        pl.BlockSpec((count, step, width), lambda i, *base: (0, at(i, base), 0)),
+        pl.BlockSpec(
+            (count, SUB, width),
+            lambda i, *base: (0, jnp.maximum(at(i, base) * per - 1, 0), 0),
+        ),
+        pl.BlockSpec(
+            (count, SUB, width),
+            lambda i, *base: (0, jnp.minimum((at(i, base) + 1) * per, total - 1), 0),
+        ),
     ]
 
 
-def vorticity_stage(planes, height, dipole, edge, sides):
+def vorticity_stage(planes, height, dipole, edge, which, parts):
     _, rows, width = planes.shape
-    part = rows // sides
+    count = width // LANE
+    part = rows // parts
     step = row_step(part)
-    rim = lambda: pl.BlockSpec((4, step, LANE), lambda i: (0, i, 0))
+    rim = lambda: pl.BlockSpec((4, step, LANE), lambda i, base: (0, i + base[0], 0))
+    first = jnp.stack([which * (part // step), rows // step]).astype(jnp.int32)
     return pl.pallas_call(
         vorticity_kernel,
-        grid=(rows // step,),
-        in_specs=block_specs(2, step, rows, width)
-        + block_specs(1, step, rows, width) * 2
-        + [whole(edge[0]), whole(edge[1]), rim(), rim()],
-        out_specs=pl.BlockSpec(
-            (1, 2, step, width), lambda i: (i // (part // step), 0, i % (part // step), 0)
+        grid_spec=pltpu.PrefetchScalarGridSpec(
+            num_scalar_prefetch=1,
+            grid=(part // step,),
+            in_specs=block_specs(2, step, rows, width)
+            + block_specs(1, step, rows, width)
+            + block_specs(1, step, rows, width)
+            + [whole(edge[0]), whole(edge[1]), rim(), rim()],
+            out_specs=pl.BlockSpec((2, count, step, LANE), lambda i, base: (0, 0, i, 0)),
+            scratch_shapes=[pltpu.VMEM((4, count + 2, step + 2 * SUB, LANE), F32)],
         ),
-        out_shape=jax.ShapeDtypeStruct((sides, 2, part, width), F32),
-        scratch_shapes=[pltpu.VMEM((4, step + 2 * SUB, width + 2 * LANE), F32)],
+        out_shape=jax.ShapeDtypeStruct((2, count, part, LANE), F32),
         compiler_params=params(),
+        cost_estimate=pl.CostEstimate(
+            flops=80 * part * width, bytes_accessed=6 * 4 * part * width, transcendentals=part * width
+        ),
         name="vorticity_stage",
-    )(*[planes] * 3, *[height[None]] * 3, *[dipole[None]] * 3, *edge)
+    )(first, *[planes] * 3, *[height[None]] * 3, *[dipole[None]] * 3, *edge)
 
 
 def geometry_stage(planes, height, edge):
     _, rows, width = planes.shape
+    count = width // LANE
     step = row_step(rows)
     return pl.pallas_call(
         geometry_kernel,
@@ -580,14 +652,18 @@
         + block_specs(1, step, rows, width)
         + [whole(e) for e in edge],
         out_specs=[
-            pl.BlockSpec((3, step, width), lambda i: (0, i, 0)),
-            pl.BlockSpec((step, width), lambda i: (i, 0)),
+            pl.BlockSpec((3, count, step, LANE), lambda i: (0, 0, i, 0)),
+            pl.BlockSpec((count, step, LANE), lambda i: (0, i, 0)),
         ],
         out_shape=[
-            jax.ShapeDtypeStruct((3, rows, width), F32),
-            jax.ShapeDtypeStruct((rows, width), F32),
+            jax.ShapeDtypeStruct((3, count, rows, LANE), F32),
+            jax.ShapeDtypeStruct((count, rows, LANE), F32),
         ],
-        scratch_shapes=[pltpu.VMEM((3, step + 2 * SUB, width + 2 * LANE), F32)],
+        scratch_shapes=[
+            pltpu.VMEM((3, count + 2, step + 2 * SUB, LANE), F32),
+            pltpu.VMEM((3, count, step + 2 * SUB, LANE), F32),
+            pltpu.VMEM((3, count, step + 2 * SUB, LANE), F32),
+        ],
         compiler_params=params(),
         cost_estimate=pl.CostEstimate(
             flops=200 * rows * width, bytes_accessed=7 * 4 * rows * width, transcendentals=rows * width
@@ -596,30 +672,49 @@
     )(*[planes] * 3, *[height[None]] * 3, *edge)
 
 
-def final_kernel(speed_ref, unit_ref, base_ref, velocity_ref, update_ref):
-    speed = speed_ref[...]
-    for axis in range(3):
-        velocity_ref[axis] = speed * unit_ref[axis]
-    update_ref[...] = base_ref[...] + 0.5 * speed * speed
-
-
-def final_stage(speed, unit, base):
-    rows, width = base.shape
-    step = row_step(rows)
-    three = lambda: pl.BlockSpec((3, step, width), lambda i: (0, i, 0))
-    one = lambda: pl.BlockSpec((step, width), lambda i: (i, 0))
+def final_kernel(base_ref, speed_ref, unit_ref, rest_ref, *refs):
+    velocity_ref, update_ref = refs[-2:]
+    for j in range(unit_ref.shape[1]):
+        at = slice(j * LANE, (j + 1) * LANE)
+        speed = speed_ref[j]
+        for axis in range(3):
+            velocity_ref[axis, :, at] = speed * unit_ref[axis, j]
+        update_ref[:, at] = rest_ref[j] + 0.5 * speed * speed
+
+
+def final_stage(speed, unit, rest, which, before):
+    count, part, _ = speed.shape
+    rows, width = unit.shape[2], count * LANE
+    step = LANE if part % LANE == 0 else row_step(part)
+    first = (which * (part // step))[None].astype(jnp.int32)
+    n_before = len(before)
     return pl.pallas_call(
         final_kernel,
-        grid=(rows // step,),
-        in_specs=[one(), three(), one()],
-        out_specs=[three(), one()],
+        grid_spec=pltpu.PrefetchScalarGridSpec(
+            num_scalar_prefetch=1,
+            grid=(part // step,),
+            in_specs=[
+                pl.BlockSpec((count, step, LANE), lambda i, base: (0, i, 0)),
+                pl.BlockSpec((3, count, step, LANE), lambda i, base: (0, 0, i + base[0], 0)),
+                pl.BlockSpec((count, step, LANE), lambda i, base: (0, i + base[0], 0)),
+            ]
+            + [pl.BlockSpec(memory_space=pl.ANY)] * n_before,
+            out_specs=[
+                pl.BlockSpec((3, step, width), lambda i, base: (0, i + base[0], 0)),
+                pl.BlockSpec((step, width), lambda i, base: (i + base[0], 0)),
+            ],
+        ),
         out_shape=[
             jax.ShapeDtypeStruct((3, rows, width), F32),
             jax.ShapeDtypeStruct((rows, width), F32),
         ],
+        input_output_aliases={4 + k: k for k in range(n_before)},
         compiler_params=params(),
+        cost_estimate=pl.CostEstimate(
+            flops=6 * part * width, bytes_accessed=9 * 4 * part * width, transcendentals=0
+        ),
         name="final_stage",
-    )(speed, unit, base)
+    )(first, speed, unit, rest, *before)
 
 
 def both_ways(last, initial, axis):
@@ -640,14 +735,17 @@
         pieces = [shift_plane, height[None], dipole[None]]
         return jnp.concatenate([lax.slice_in_dim(p, a, b, axis=dim) for p in pieces], 0)
 
+    top, low = both_ways(cut(rows - RIM, rows, 1), cut(0, RIM, 1), "tr")
     left, right = both_ways(cut(width - LANE, width, 2), cut(0, LANE, 2), "tc")
-    top, low = both_ways(cut(rows - SUB, rows, 1), cut(0, SUB, 1), "tr")
-    vorticity = vorticity_stage(
-        shift_plane, height, dipole, (top, low, left, right), tc
-    )
-    sheet = lax.all_to_all(vorticity, "tc", split_axis=0, concat_axis=0, tiled=True)
+    me = lax.axis_index("tc").astype(jnp.int32)
+    edges = (top, low, left, right)
+    pieces = []
+    for away in range(1, tc):
+        send = vorticity_stage(shift_plane, height, dipole, edges, (me + away) % tc, tc)
+        pieces.append(lax.ppermute(send, "tc", [(i, (i + away) % tc) for i in range(tc)]))
+    own = vorticity_stage(shift_plane, height, dipole, edges, me, tc)
     row_table, back_table = row_tables(col_count)
-    spec = row_forward(sheet, row_table)
+    spec = row_forward([own] + pieces, me, row_table)
     blocks = spec.shape[0]
     n = blocks * LANE // devices
     u = max(1, n // LANE)
@@ -659,14 +757,16 @@
 
     ends = jnp.stack([top[:3], low[:3]])
     left_ends, right_ends = both_ways(ends[..., width - LANE :], ends[..., :LANE], "tc")
+    spare = ((0, 0), (SUB - RIM, SUB - RIM), (0, 0))
     edge = (
         top[:3],
         low[:3],
-        jnp.concatenate([left_ends[0], left[:3], left_ends[1]], 1),
-        jnp.concatenate([right_ends[0], right[:3], right_ends[1]], 1),
+        jnp.pad(jnp.concatenate([left_ends[0], left[:3], left_ends[1]], 1), spare),
+        jnp.pad(jnp.concatenate([right_ends[0], right[:3], right_ends[1]], 1), spare),
     )
     unit, base = geometry_stage(shift_plane, height, edge)
 
+    columns, unit, base = lax.optimization_barrier((columns, unit, base))
     direct = part % LANE == 0
     if not direct:
         columns = columns.transpose(1, 2, 3, 0, 4).reshape(1, u, 4, n, row_count)
@@ -683,10 +783,13 @@
     back = lax.all_to_all(partial, ("tr", "tc"), split_axis=0, concat_axis=0, tiled=True)
     back = back.reshape(blocks, pieces, 2, n, part)
     back = jnp.swapaxes(back, 1, 2).reshape(blocks, 2, LANE, part)
-    speed_rows = row_back(back, back_table, tc)
-    speed = lax.all_to_all(speed_rows, "tc", split_axis=0, concat_axis=0, tiled=True)
-    velocity_update, dipole_update = final_stage(speed.reshape(rows, width), unit, base)
-    return (velocity_update, dipole_update)
+    speeds = row_back(back, me, back_table, tc)
+    outs = final_stage(speeds[0], unit, base, me, ())
+    for away in range(1, tc):
+        turn = [(i, (i + away) % tc) for i in range(tc)]
+        speed = lax.ppermute(speeds[away], "tc", turn)
+        outs = final_stage(speed, unit, base, (me - away) % tc, outs)
+    return tuple(outs)
 
 
 def solution(mesh):

time: 501 us -> 398 us (0.79)
  Pallas kernels: 247 us -> 148 us
  waiting for transfers between devices: 194 us -> 123 us
  blocking collectives: 30.3 us -> 97.2 us
    all_to_all x2 -> x1, blocking collectives: 30.3 us -> 97.2 us  [local(): lax.all_to_all(partial, ('tr', 'tc'), split_axis=0, concat_axis=0, tiled=...]
    all_to_all x1, waiting for transfers between devices: 181 us -> 119 us  [local(): lax.all_to_all(spec, ('tr', 'tc'), split_axis=0, concat_axis=0, tiled=True)]
    pallas_call x1, Pallas kernels: 112 us -> 56.7 us  [geometry_stage(): pl.pallas_call(geometry_kernel, grid=(rows // step,), in_specs=block_spec...]
    pallas_call x4 -> x6, Pallas kernels: 116 us -> 75.2 us  [the longest x2 37 us: vorticity_stage(): pl.pallas_call(vorticity_kernel, grid_spec=pltpu.PrefetchScalarGridSpec(n...]
    ppermute x6, waiting for transfers between devices: 13.4 us -> 4.1 us  [both_ways(): return (lax.ppermute(last, axis, up), lax.ppermute(initial, axis, down))]
    all_to_all x1 -> x0, starting transfers between devices: 5.34 us -> none  [local(): lax.all_to_all(partial, ('tr', 'tc'), split_axis=0, concat_axis=0, tiled=...]
  transfers between devices with their start and end apart: 8 -> 9, of which waited for: 5 -> 4; matrix products, arithmetic and copies ran while one was open for 1% -> 2% of each run, Pallas kernels for 22% -> 21%
where the time goes in v2:
time: 398 us; the launch traced here: 397 us
  Pallas kernels  148 us (37%)
  waiting for transfers between devices  123 us (31%)
  blocking collectives  97.2 us (24%)
  starting transfers between devices  12.5 us (3%)
  local copies, waits for them, and re-layouts  10.6 us (3%)
  other arithmetic  4.32 us (1%)
    all_to_all x1, waiting for transfers between devices, local(): lax.all_to_all(spec, ('tr', 'tc'), split_axis=0, concat_axis=0, tiled=True)  119 us
    all_to_all x1, blocking collectives, local(): lax.all_to_all(partial, ('tr', 'tc'), split_axis=0, concat_axis=0, tiled=...  97.2 us
    pallas_call x1, Pallas kernels, geometry_stage(): pl.pallas_call(geometry_kernel, grid=(rows // step,), in_specs=block_spec...  56.7 us
    pallas_call x2, Pallas kernels, vorticity_stage(): pl.pallas_call(vorticity_kernel, grid_spec=pltpu.PrefetchScalarGridSpec(n...  37 us
    pallas_call x1, Pallas kernels, col_stage(): pl.pallas_call(functools.partial(col_kernel, chunk=chunk), grid=(u, n //...  16.5 us
    pallas_call x1, Pallas kernels, row_forward(): pl.pallas_call(row_kernel, grid_spec=pltpu.PrefetchScalarGridSpec(num_sca...  13.5 us
    pallas_call x2, Pallas kernels, final_stage(): pl.pallas_call(final_kernel, grid_spec=pltpu.PrefetchScalarGridSpec(num_s...  13 us
    pallas_call x1, Pallas kernels, row_back(): pl.pallas_call(back_kernel, grid_spec=pltpu.PrefetchScalarGridSpec(num_sc...  11.7 us
  transfers between devices with their start and end apart: 9, of which 4 were waited for; matrix products, arithmetic and copies ran while one was open for 2% of the time, Pallas kernels for 21%

profile of v2, /device:TPU:21, one launch (start us, length us, event | category | flops | bytes accessed | tf_op | source)
XLA Modules:
  0.0 396.9 jit_solution(2440545056211436887)
XLA Ops:
  0.6 1.3 fusion.1
  1.9 1.3 fusion.3
  3.2 0.1 pad_maximum_fusion
  3.3 0.7 collective-permute-start.2
  4.0 1.0 pad_maximum_fusion.1
  5.1 0.0 collective-permute-start.3
  5.1 1.0 fusion.5
  6.0 1.0 fusion.2
  7.1 1.3 collective-permute-start
  8.4 1.2 collective-permute-start.1
  9.6 0.6 pad_add_fusion.base_ref
  10.2 1.0 collective-permute-done.refs_9_
  11.2 2.1 collective-permute-done.1.refs_10_
  13.2 0.0 collective-permute-done.2.refs_11_
  13.2 0.0 collective-permute-done.3.refs_12_
  13.2 0.0 copy-done.3
  13.3 0.6 copy-done.5
  13.9 0.4 copy-done
  14.3 1.0 copy-done.1
  15.3 18.8 %vorticity_stage.3 = f32[2,16,256,128]{3,2,1,0:T(8,128)} custom-call(s32[2]{0:T(128)} %pad_add_fusion.base_ref, f32[2,512,2048]{2,1,0:T(8,128)} %refs_2_.6, f32[2,512,2048]{2,1,0:T(8,128)} %refs_2_.6, f32[2,512,2048]{2,1,0:T(8,128)} %refs_2_.6, f32[1,512,2048]{2,1,0:T(8,128)} %bitcast.25, f32[1,512,2048]{2,1,0:T(8,128)} %bitcast.26, ...), custom_call_target="tpu_custom_call" | custom-call | flops 41943040 | bytes 12582912 | tf_op jit(solution)/shard_map/vorticity_stage/pallas_call | solution.py:623
  34.0 0.2 collective-permute-start.4
  34.3 0.6 pad_add_fusion.1.base_ref
  34.9 18.3 %vorticity_stage.2.refs_0_ = f32[2,16,256,128]{3,2,1,0:T(8,128)} custom-call(s32[2]{0:T(128)} %pad_add_fusion.1.base_ref, f32[2,512,2048]{2,1,0:T(8,128)} %refs_2_.6, f32[2,512,2048]{2,1,0:T(8,128)} %refs_2_.6, f32[2,512,2048]{2,1,0:T(8,128)} %refs_2_.6, f32[1,512,2048]{2,1,0:T(8,128)} %bitcast.28, f32[1,512,2048]{2,1,0:T(8,128)} %bitcast.29, ...), custom_call_target="tpu_custom_call" | custom-call | flops 41943040 | bytes 12582912 | tf_op jit(solution)/shard_map/vorticity_stage/pallas_call | solution.py:623
  53.2 0.0 collective-permute-done.4.refs_1_
  53.2 13.5 %row_forward.1 = f32[16,4,128,256]{3,2,1,0:T(8,128)} custom-call(s32[1]{0:T(128)} %bitcast.1.me_ref, f32[2,16,256,128]{3,2,1,0:T(8,128)} %vorticity_stage.2.refs_0_, f32[2,16,256,128]{3,2,1,0:T(8,128)} %collective-permute-done.4.refs_1_, bf16[16,512,256]{2,1,0:T(8,128)(2,1)} %constant.53.clone.refs_2_), custom_call_target="tpu_custom_call" | custom-call | tf_op jit(solution)/shard_map/row_forward/pallas_call | solution.py:256
  66.7 7.4 %all-to-all-start = ((f32[16,1,4,128,256]{4,3,2,1,0:T(8,128)}), f32[16,1,4,128,256]{4,3,2,1,0:T(8,128)}, u32[]{:S(2)}, u32[]{:S(2)}) async-start(f32[16,1,4,128,256]{4,3,2,1,0:T(8,128)} %bitcast.42), calls=%async_computation | async-start | bytes 16777216 | tf_op jit(solution)/shard_map/all_to_all | solution.py:756
  74.1 0.0 slice-start.1
  74.1 0.0 copy-done.6
  74.1 0.6 slice_bitcast_fusion.4
  74.8 0.0 copy-done.4
  74.8 0.7 slice_bitcast_fusion.5
  75.4 0.4 collective-permute-start.6
  75.8 1.5 dynamic-slice_bitcast_fusion.f2_ref
  77.3 0.1 collective-permute-start.5
  77.5 0.0 collective-permute-done.6
  77.5 1.0 collective-permute-done.5
  78.5 0.9 select_maximum_fusion.2.refs_8_
  79.4 1.0 select_maximum_fusion.refs_9_
  80.4 56.7 %geometry_stage.1 = (f32[3,16,512,128]{3,2,1,0:T(8,128)}, f32[16,512,128]{2,1,0:T(8,128)}) custom-call(f32[2,512,2048]{2,1,0:T(8,128)} %refs_2_.6, f32[2,512,2048]{2,1,0:T(8,128)} %refs_2_.6, f32[2,512,2048]{2,1,0:T(8,128)} %refs_2_.6, f32[1,512,2048]{2,1,0:T(8,128)} %bitcast.31, f32[1,512,2048]{2,1,0:T(8,128)} %bitcast.32, f32[1,512,2048]{2,1,0:T(8,128)} %bitcast.33, ...), custom_call_target="tpu_custom_call" | custom-call | flops 209715200 | bytes 29360128 | tf_op jit(solution)/shard_map/geometry_stage/pallas_call | solution.py:648
  137.1 119.0 %all-to-all-done.x_ref = f32[16,1,4,128,256]{4,3,2,1,0:T(8,128)} async-done(((f32[16,1,4,128,256]{4,3,2,1,0:T(8,128)}), f32[16,1,4,128,256]{4,3,2,1,0:T(8,128)}, u32[]{:S(2)}, u32[]{:S(2)}) %all-to-all-start) | async-done | bytes 8388640 | tf_op jit(solution)/shard_map/all_to_all | solution.py:756
  256.1 16.5 %col_stage.1 = f32[16,1,2,128,256]{4,3,2,1,0:T(8,128)} custom-call(f32[16,1,4,128,256]{4,3,2,1,0:T(8,128)} %all-to-all-done.x_ref, f32[1,128,128]{2,1,0:T(8,128)} %dynamic-slice_bitcast_fusion.f2_ref, bf16[768,256]{1,0:T(8,128)(2,1)} %constant.55.clone.wf_ref, bf16[768,256]{1,0:T(8,128)(2,1)} %constant.56.clone.wb_ref, ...), custom_call_target="tpu_custom_call" | custom-call | tf_op jit(solution)/shard_map/col_stage/pallas_call | solution.py:348
  272.6 97.2 %all_to_all.10 = f32[16,1,2,128,256]{4,3,2,1,0:T(8,128)} all-to-all(f32[16,1,2,128,256]{4,3,2,1,0:T(8,128)} %col_stage.1), channel_id=1, replica_groups=mesh['groups'=2,'tr'=8,'tc'=2] {'tr','tc'}, dimensions={0} | all-to-all | bytes 8388608 | tf_op jit(solution)/shard_map/all_to_all | solution.py:783
  369.8 11.7 %row_back.1 = (f32[16,256,128]{2,1,0:T(8,128)}, f32[16,256,128]{2,1,0:T(8,128)}) custom-call(s32[1]{0:T(128)} %bitcast.1.me_ref, f32[16,2,128,256]{3,2,1,0:T(8,128)} %bitcast.43, bf16[16,512,256]{2,1,0:T(8,128)(2,1)} %constant.59.clone.w_ref), custom_call_target="tpu_custom_call" | custom-call | tf_op jit(solution)/shard_map/row_back/pallas_call | solution.py:405
  381.5 1.1 collective-permute-start.7
  382.6 6.5 %final_stage.2 = (f32[3,512,2048]{2,1,0:T(8,128)}, f32[512,2048]{1,0:T(8,128)}) custom-call(s32[1]{0:T(128)} %bitcast.15.base_ref, f32[16,256,128]{2,1,0:T(8,128)} %get-tuple-element.17.speed_ref, f32[3,16,512,128]{3,2,1,0:T(8,128)} %get-tuple-element.15.unit_ref, f32[16,512,128]{2,1,0:T(8,128)} %get-tuple-element.16.rest_ref), custom_call_target="tpu_custom_call" | custom-call | flops 3145728 | bytes 18874368 | tf_op jit(solution)/shard_map/final_stage/pallas_call | solution.py:691
  389.1 0.0 collective-permute-done.7.speed_ref
  389.1 1.3 copy-done.2
  390.4 6.5 %final_stage.3 = (f32[3,512,2048]{2,1,0:T(8,128)}, f32[512,2048]{1,0:T(8,128)}) custom-call(s32[1]{0:T(128)} %bitcast.base_ref, f32[16,256,128]{2,1,0:T(8,128)} %copy-done.2, f32[3,16,512,128]{3,2,1,0:T(8,128)} %get-tuple-element.15.unit_ref, f32[16,512,128]{2,1,0:T(8,128)} %get-tuple-element.16.rest_ref, ...), custom_call_target="tpu_custom_call", output_to_operand_aliasing={{0}: (4, {}), {1}: (5, {})} | custom-call | flops 3145728 | bytes 18874368 | tf_op jit(solution)/shard_map/final_stage/pallas_call | solution.py:691
  (15 shorter events, 0.1 us)
Async XLA Ops:
  3.3 10.0 %collective-permute-start.2 = (f32[4,512,128]{2,1,0:T(8,128)S(1)}, f32[4,512,128]{2,1,0:T(8,128)S(1)}, u32[]{:S(2)}, u32[]{:S(2)}) collective-permute-start(f32[4,512,128]{2,1,0:T(8,128)S(1)} %pad_maximum_fusion), channel_id=1, source_target_pairs={{0,1},{1,0},{2,3},{3,2},{4,5},{5,4},{6,7},{7,6},{8,9},{9,8},{10,11... | collective-permute-start | bytes 3145736 | tf_op jit(solution)/shard_map/ppermute | solution.py:724
  5.1 8.2 %collective-permute-start.3 = (f32[4,512,128]{2,1,0:T(8,128)}, f32[4,512,128]{2,1,0:T(8,128)S(1)}, u32[]{:S(2)}, u32[]{:S(2)}) collective-permute-start(f32[4,512,128]{2,1,0:T(8,128)} %pad_maximum_fusion.1), channel_id=1, source_target_pairs={{1,0},{0,1},{3,2},{2,3},{5,4},{4,5},{7,6},{6,7},{9,8},{8,9},{11,10... | collective-permute-start | bytes 3145736 | tf_op jit(solution)/shard_map/ppermute | solution.py:724
  7.1 4.1 %collective-permute-start = (f32[4,2,2048]{2,1,0:T(2,128)S(1)}, f32[4,2,2048]{2,1,0:T(2,128)S(1)}, u32[]{:S(2)}, u32[]{:S(2)}) collective-permute-start(f32[4,2,2048]{2,1,0:T(2,128)S(1)} %pad_maximum_fusion.2), channel_id=1, source_target_pairs={{0,2},{2,4},{4,6},{6,8},{8,10},{10,12},{12,14},{14,0},{1,3},{3,5},... | collective-permute-start | bytes 196616 | tf_op jit(solution)/shard_map/ppermute | solution.py:724
  8.4 4.9 %collective-permute-start.1 = (f32[4,2,2048]{2,1,0:T(2,128)S(1)}, f32[4,2,2048]{2,1,0:T(2,128)S(1)}, u32[]{:S(2)}, u32[]{:S(2)}) collective-permute-start(f32[4,2,2048]{2,1,0:T(2,128)S(1)} %pad_maximum_fusion.3), channel_id=1, source_target_pairs={{2,0},{4,2},{6,4},{8,6},{10,8},{12,10},{14,12},{0,14},{3,1},{5,3},... | collective-permute-start | bytes 196616 | tf_op jit(solution)/shard_map/ppermute | solution.py:724
  11.2 2.1 copy-start.3
  13.2 0.6 copy-start.5
  13.2 1.0 copy-start
  14.3 1.0 copy-start.1
  34.0 19.1 %collective-permute-start.4 = (f32[2,16,256,128]{3,2,1,0:T(8,128)}, f32[2,16,256,128]{3,2,1,0:T(8,128)}, u32[]{:S(2)}, u32[]{:S(2)}) collective-permute-start(f32[2,16,256,128]{3,2,1,0:T(8,128)} %vorticity_stage.3), channel_id=1, source_target_pairs={{0,1},{1,0},{2,3},{3,2},{4,5},{5,4},{6,7},{7,6},{8,9},{9,8},{10,11... | collective-permute-start | bytes 12582920 | tf_op jit(solution)/shard_map/ppermute | solution.py:745
  66.7 7.4 %copy-start.6 = (f32[4,2,2048]{2,1,0:T(2,128)S(1)}, f32[4,2,2048]{2,1,0:T(2,128)}, u32[]{:S(2)}) copy-start(f32[4,2,2048]{2,1,0:T(2,128)} %copy-done.5) | copy-start | bytes 196612
  66.7 8.1 %copy-start.4 = (f32[4,2,2048]{2,1,0:T(2,128)S(1)}, f32[4,2,2048]{2,1,0:T(2,128)}, u32[]{:S(2)}) copy-start(f32[4,2,2048]{2,1,0:T(2,128)} %copy-done.3) | copy-start | bytes 196612
  66.7 189.5 %all-to-all-start = ((f32[16,1,4,128,256]{4,3,2,1,0:T(8,128)}), f32[16,1,4,128,256]{4,3,2,1,0:T(8,128)}, u32[]{:S(2)}, u32[]{:S(2)}) async-start(f32[16,1,4,128,256]{4,3,2,1,0:T(8,128)} %bitcast.42), calls=%async_computation | async-start | bytes 16777216 | tf_op jit(solution)/shard_map/all_to_all | solution.py:756
  74.1 4.4 %slice-start = ((f32[4,512,128]{2,1,0:T(8,128)}), f32[3,512,128]{2,1,0:T(8,128)S(1)}, s32[]{:S(2)}) async-start(f32[4,512,128]{2,1,0:T(8,128)} %copy-done), calls=%async_computation.2 | async-start | bytes 1572864 | tf_op jit(solution)/shard_map/slice | solution.py:764
  74.1 5.3 %slice-start.1 = ((f32[4,512,128]{2,1,0:T(8,128)}), f32[3,512,128]{2,1,0:T(8,128)S(1)}, s32[]{:S(2)}) async-start(f32[4,512,128]{2,1,0:T(8,128)} %copy-done.1), calls=%async_computation.3 | async-start | bytes 1572864 | tf_op jit(solution)/shard_map/slice | solution.py:765
  75.4 2.0 collective-permute-start.6
  77.3 1.2 collective-permute-start.5
  381.5 7.6 %collective-permute-start.7 = (f32[16,256,128]{2,1,0:T(8,128)}, f32[16,256,128]{2,1,0:T(8,128)S(1)}, u32[]{:S(2)}, u32[]{:S(2)}) collective-permute-start(f32[16,256,128]{2,1,0:T(8,128)} %get-tuple-element.14), channel_id=1, source_target_pairs={{0,1},{1,0},{2,3},{3,2},{4,5},{5,4},{6,7},{7,6},{8,9},{9,8},{10,11... | collective-permute-start | bytes 6291464 | tf_op jit(solution)/shard_map/ppermute | solution.py:790
  389.1 1.3 copy-start.2

commit v3 on v2

--- a/solution.py
+++ b/solution.py
@@ -12,6 +12,8 @@
 SUB = 8
 MANY = 4
 RIM = 2
+CUTS = 2
+SOME = 8
 F32 = jnp.float32
 BF16 = jnp.bfloat16
 VMEM_LIMIT = 60 * 1024 * 1024
@@ -197,9 +199,10 @@
 def row_kernel(me_ref, *refs):
     x_refs, (w_ref, o_ref, s_ref) = refs[:-3], refs[-3:]
     sides = len(x_refs)
+    first = pl.program_id(1) == 0
     for me in range(sides):
 
-        @pl.when(me_ref[0] == me)
+        @pl.when(jnp.logical_and(first, me_ref[0] == me))
         def _(me=me):
             row_short([x_refs[(me - side) % sides] for side in range(sides)], s_ref)
 
@@ -237,8 +240,11 @@
 
 
 def row_long(w_ref, o_ref, s_ref, rows):
+    some = o_ref.shape[0]
+    start = pl.program_id(1) * some
+
     def long(k, _):
-        y = three(w_ref[k], s_ref[k], (((1,), (1,)), ((), ())))
+        y = three(w_ref[k], s_ref[start + k], (((1,), (1,)), ((), ())))
         for field in range(2):
             for part in range(2):
                 o_ref[k, 2 * field + part] = y[
@@ -246,21 +252,24 @@
                 ]
         return 0
 
-    lax.fori_loop(0, s_ref.shape[0], long, 0, unroll=4)
+    lax.fori_loop(0, some, long, 0, unroll=True)
 
 
 def row_forward(pieces, me, table):
     _, per, rows, _ = pieces[0].shape
     blocks = len(pieces) * per // 2
+    some = SOME if blocks % SOME == 0 else 1
     step = LANE if rows % LANE == 0 else rows
     return pl.pallas_call(
         row_kernel,
         grid_spec=pltpu.PrefetchScalarGridSpec(
             num_scalar_prefetch=1,
-            grid=(rows // step,),
-            in_specs=[pl.BlockSpec((2, per, step, LANE), lambda i, _: (0, 0, i, 0)) for _ in pieces]
-            + [whole(table)],
-            out_specs=pl.BlockSpec((blocks, 4, LANE, step), lambda i, _: (0, 0, 0, i)),
+            grid=(rows // step, blocks // some),
+            in_specs=[
+                pl.BlockSpec((2, per, step, LANE), lambda i, k, _: (0, 0, i, 0)) for _ in pieces
+            ]
+            + [pl.BlockSpec((some,) + table.shape[1:], lambda i, k, _: (k, 0, 0))],
+            out_specs=pl.BlockSpec((some, 4, LANE, step), lambda i, k, _: (k, 0, 0, i)),
             scratch_shapes=[pltpu.VMEM((blocks, 2 * step, 2 * LANE), F32)],
         ),
         out_shape=jax.ShapeDtypeStruct((blocks, 4, LANE, rows), F32),
@@ -269,9 +278,17 @@
     )(me[None], *pieces, table)
 
 
-def col_kernel(x_ref, f2_ref, wf_ref, wb_ref, tw_ref, f1_ref, o_ref, a_ref, z_ref, *, chunk):
-    sources, _, _, count, length = x_ref.shape
+def col_kernel(*refs, chunk, cuts):
+    x_refs = refs[:cuts]
+    f2_ref, wf_ref, wb_ref, tw_ref, f1_ref = refs[cuts : cuts + 5]
+    o_refs, (a_ref, z_ref) = refs[cuts + 5 : -2], refs[-2:]
+    count, length = x_refs[0].shape[-2:]
     per = length // LANE
+
+    def where(a):
+        lanes = slice((a % per) * LANE, (a % per + 1) * LANE)
+        return a // per % cuts, a // per // cuts, lanes
+
     outer = tw_ref.shape[1]
 
     for field in range(2):
@@ -280,8 +297,8 @@
             at = pl.ds(pl.multiple_of(g * SUB, SUB), SUB)
 
             def part(a, which):
-                lanes = slice((a % per) * LANE, (a % per + 1) * LANE)
-                return x_ref[a // per, 0, 2 * field + which, at, lanes]
+                cut, source, lanes = where(a)
+                return x_refs[cut][source, 0, 2 * field + which, at, lanes]
 
             spec = fft_list([(part(a, 0), part(a, 1)) for a in range(outer)], -1)
             for k in range(outer):
@@ -330,52 +347,64 @@
             vals.append((re, im))
         res = fft_list(vals, 1)
         for a in range(outer):
-            lanes = slice((a % per) * LANE, (a % per + 1) * LANE)
-            o_ref[a // per, 0, 0, at, lanes] = res[a][0]
-            o_ref[a // per, 0, 1, at, lanes] = res[a][1]
+            cut, source, lanes = where(a)
+            o_refs[cut][source, 0, 0, at, lanes] = res[a][0]
+            o_refs[cut][source, 0, 1, at, lanes] = res[a][1]
         return 0
 
     lax.fori_loop(0, count // SUB, last, 0)
 
 
-def col_stage(x, f2, tables):
-    sources, u, _, n, rows = x.shape
-    outer = sources * rows // LANE
+def col_stage(xs, f2, tables):
+    sources, u, _, n, rows = xs[0].shape
+    cuts = len(xs)
+    outer = sources * cuts * rows // LANE
     step = n
     while step > 32 and step % 2 == 0:
         step //= 2
     chunk = max(1, min(outer, 1024 // step))
+    block = lambda count: pl.BlockSpec(
+        (sources, 1, count, step, rows), lambda i, j: (0, i, 0, j, 0)
+    )
     return pl.pallas_call(
-        functools.partial(col_kernel, chunk=chunk),
+        functools.partial(col_kernel, chunk=chunk, cuts=cuts),
         grid=(u, n // step),
-        in_specs=[
-            pl.BlockSpec((sources, 1, 4, step, rows), lambda i, j: (0, i, 0, j, 0)),
-            pl.BlockSpec((1, step, LANE), lambda i, j: (i, j, 0)),
-        ]
+        in_specs=[block(4)] * cuts
+        + [pl.BlockSpec((1, step, LANE), lambda i, j: (i, j, 0))]
         + [whole(t) for t in tables],
-        out_specs=pl.BlockSpec((sources, 1, 2, step, rows), lambda i, j: (0, i, 0, j, 0)),
-        out_shape=jax.ShapeDtypeStruct((sources, u, 2, n, rows), F32),
+        out_specs=[block(2)] * cuts,
+        out_shape=[jax.ShapeDtypeStruct((sources, u, 2, n, rows), F32)] * cuts,
         scratch_shapes=[
             pltpu.VMEM((2, outer, step, 2 * LANE), F32),
             pltpu.VMEM((outer, step, 2 * LANE), F32),
         ],
         compiler_params=params(),
         name="col_stage",
-    )(x, f2, *tables)
+    )(*xs, f2, *tables)
 
 
 def back_kernel(me_ref, x_ref, w_ref, *refs):
     o_refs, (z_ref, t_ref) = refs[:-2], refs[-2:]
-    blocks, _, _, rows = x_ref.shape
+    some, _, _, rows = x_ref.shape
+    start = pl.program_id(1) * some
+
+    def long(k, _):
+        x = x_ref[k].reshape(2 * LANE, rows)
+        z_ref[start + k] = three(w_ref[k], x, (((1,), (0,)), ((), ())))
+        return 0
+
+    lax.fori_loop(0, some, long, 0, unroll=True)
+
+    @pl.when(pl.program_id(1) == pl.num_programs(1) - 1)
+    def _():
+        back_short(me_ref, o_refs, z_ref, t_ref)
+
+
+def back_short(me_ref, o_refs, z_ref, t_ref):
     sides = len(o_refs)
     per = o_refs[0].shape[0]
+    blocks = z_ref.shape[0]
     outer = 2 * blocks
-
-    def long(k, _):
-        z_ref[k] = three(w_ref[k], x_ref[k].reshape(2 * LANE, rows), (((1,), (0,)), ((), ())))
-        return 0
-
-    lax.fori_loop(0, blocks, long, 0, unroll=4)
 
     def short(g, _):
         at = pl.ds(pl.multiple_of(g * SUB, SUB), SUB)
@@ -401,17 +430,18 @@
 def row_back(x, me, table, sides):
     blocks, _, _, rows = x.shape
     per = 2 * blocks // sides
+    some = SOME if blocks % SOME == 0 else 1
     step = LANE if rows % LANE == 0 else rows
     return pl.pallas_call(
         back_kernel,
         grid_spec=pltpu.PrefetchScalarGridSpec(
             num_scalar_prefetch=1,
-            grid=(rows // step,),
+            grid=(rows // step, blocks // some),
             in_specs=[
-                pl.BlockSpec((blocks, 2, LANE, step), lambda i, _: (0, 0, 0, i)),
-                whole(table),
+                pl.BlockSpec((some, 2, LANE, step), lambda i, k, _: (k, 0, 0, i)),
+                pl.BlockSpec((some,) + table.shape[1:], lambda i, k, _: (k, 0, 0)),
             ],
-            out_specs=[pl.BlockSpec((per, step, LANE), lambda i, _: (0, i, 0))] * sides,
+            out_specs=[pl.BlockSpec((per, step, LANE), lambda i, k, _: (0, i, 0))] * sides,
             scratch_shapes=[
                 pltpu.VMEM((blocks, 2 * LANE, step), F32),
                 pltpu.VMEM((2 * blocks, LANE, step), F32),
@@ -685,7 +715,7 @@
 def final_stage(speed, unit, rest, which, before):
     count, part, _ = speed.shape
     rows, width = unit.shape[2], count * LANE
-    step = LANE if part % LANE == 0 else row_step(part)
+    step = row_step(part)
     first = (which * (part // step))[None].astype(jnp.int32)
     n_before = len(before)
     return pl.pallas_call(
@@ -739,21 +769,37 @@
     left, right = both_ways(cut(width - LANE, width, 2), cut(0, LANE, 2), "tc")
     me = lax.axis_index("tc").astype(jnp.int32)
     edges = (top, low, left, right)
-    pieces = []
-    for away in range(1, tc):
-        send = vorticity_stage(shift_plane, height, dipole, edges, (me + away) % tc, tc)
-        pieces.append(lax.ppermute(send, "tc", [(i, (i + away) % tc) for i in range(tc)]))
-    own = vorticity_stage(shift_plane, height, dipole, edges, me, tc)
     row_table, back_table = row_tables(col_count)
-    spec = row_forward([own] + pieces, me, row_table)
-    blocks = spec.shape[0]
+    direct = part % LANE == 0
+    cuts = CUTS if part % (CUTS * LANE) == 0 else 1
+    cut_rows = part // cuts
+    blocks = col_count // LANE // 2
     n = blocks * LANE // devices
     u = max(1, n // LANE)
     n = n // u
     pieces = LANE // n
-    spec = spec.reshape(blocks, 4, pieces, n, part)
-    spec = jnp.swapaxes(spec, 1, 2).reshape(devices, u, 4, n, part)
-    columns = lax.all_to_all(spec, ("tr", "tc"), split_axis=0, concat_axis=0, tiled=True)
+
+    def turn(x, away):
+        return lax.ppermute(x, "tc", [(i, (i + away) % tc) for i in range(tc)])
+
+    def swap(x):
+        return lax.all_to_all(x, ("tr", "tc"), split_axis=0, concat_axis=0, tiled=True)
+
+    columns = []
+    for h in range(cuts):
+
+        def stage(core):
+            return vorticity_stage(
+                shift_plane, height, dipole, edges, core * cuts + h, tc * cuts
+            )
+
+        sent = [turn(stage((me + away) % tc), away) for away in range(1, tc)]
+        spec = row_forward([stage(me)] + sent, me, row_table)
+        spec = spec.reshape(blocks, 4, pieces, n, cut_rows)
+        spec = jnp.swapaxes(spec, 1, 2).reshape(devices, u, 4, n, cut_rows)
+        if h + 1 < cuts:
+            spec, edges = lax.optimization_barrier((spec, edges))
+        columns.append(swap(spec))
 
     ends = jnp.stack([top[:3], low[:3]])
     left_ends, right_ends = both_ways(ends[..., width - LANE :], ends[..., :LANE], "tc")
@@ -767,9 +813,8 @@
     unit, base = geometry_stage(shift_plane, height, edge)
 
     columns, unit, base = lax.optimization_barrier((columns, unit, base))
-    direct = part % LANE == 0
     if not direct:
-        columns = columns.transpose(1, 2, 3, 0, 4).reshape(1, u, 4, n, row_count)
+        columns = [columns[0].transpose(1, 2, 3, 0, 4).reshape(1, u, 4, n, row_count)]
     number = row_numbers(col_count).reshape(-1)
     signed = np.where(number >= col_count // 2, number - col_count, number)
     freq = (signed / col_count).astype(np.float32)
@@ -779,16 +824,18 @@
     tables = col_tables(row_count, 1.0 / (row_count * col_count))
     partial = col_stage(columns, mine, tables)
     if not direct:
-        partial = partial.reshape(u, 2, n, devices, part).transpose(3, 0, 1, 2, 4)
-    back = lax.all_to_all(partial, ("tr", "tc"), split_axis=0, concat_axis=0, tiled=True)
-    back = back.reshape(blocks, pieces, 2, n, part)
-    back = jnp.swapaxes(back, 1, 2).reshape(blocks, 2, LANE, part)
-    speeds = row_back(back, me, back_table, tc)
-    outs = final_stage(speeds[0], unit, base, me, ())
-    for away in range(1, tc):
-        turn = [(i, (i + away) % tc) for i in range(tc)]
-        speed = lax.ppermute(speeds[away], "tc", turn)
-        outs = final_stage(speed, unit, base, (me - away) % tc, outs)
+        partial = [partial[0].reshape(u, 2, n, devices, part).transpose(3, 0, 1, 2, 4)]
+    backs = [swap(p) for p in partial]
+    outs = ()
+    for h in range(cuts):
+        back, outs = lax.optimization_barrier((backs[h], outs))
+        back = back.reshape(blocks, pieces, 2, n, cut_rows)
+        back = jnp.swapaxes(back, 1, 2).reshape(blocks, 2, LANE, cut_rows)
+        speeds = row_back(back, me, back_table, tc)
+        outs = final_stage(speeds[0], unit, base, me * cuts + h, outs)
+        for away in range(1, tc):
+            speed = turn(speeds[away], away)
+            outs = final_stage(speed, unit, base, (me - away) % tc * cuts + h, outs)
     return tuple(outs)
 
 

time: 398 us -> 385 us (0.967)
  blocking collectives: 97.2 us -> 52.2 us
  Pallas kernels: 148 us -> 162 us
  starting transfers between devices: 12.5 us -> 23.8 us
  local copies, waits for them, and re-layouts: 10.6 us -> 15.3 us
    all_to_all x1, blocking collectives: 97.2 us -> 52.2 us  [swap(): lax.all_to_all(x, ('tr', 'tc'), split_axis=0, concat_axis=0, tiled=True)]
    all_to_all x1 -> x3, starting transfers between devices: 7.4 us -> 18.1 us  [swap(): lax.all_to_all(x, ('tr', 'tc'), split_axis=0, concat_axis=0, tiled=True)]
    pallas_call x2 -> x4, Pallas kernels: 37 us -> 43.5 us  [vorticity_stage(): pl.pallas_call(vorticity_kernel, grid_spec=pltpu.PrefetchScalarGridSpec(n...]
    unnamed x14 -> x22, local copies, waits for them, and re-layouts: 3.32 us -> 8.03 us
    pallas_call x2 -> x4, Pallas kernels: 13 us -> 16.2 us  [final_stage(): pl.pallas_call(final_kernel, grid_spec=pltpu.PrefetchScalarGridSpec(num_s...]
    pallas_call x1 -> x2, Pallas kernels: 13.5 us -> 15.6 us  [row_forward(): pl.pallas_call(row_kernel, grid_spec=pltpu.PrefetchScalarGridSpec(num_sca...]
    pallas_call x1 -> x2, Pallas kernels: 11.7 us -> 13.4 us  [row_back(): pl.pallas_call(back_kernel, grid_spec=pltpu.PrefetchScalarGridSpec(num_sc...]
    all_to_all x1 -> x3, waiting for transfers between devices: 119 us -> 120 us  [swap(): lax.all_to_all(x, ('tr', 'tc'), split_axis=0, concat_axis=0, tiled=True)]
  transfers between devices with their start and end apart: 9 -> 13, of which waited for: 4 -> 6; matrix products, arithmetic and copies ran while one was open for 2% -> 3% of each run, Pallas kernels for 21% -> 30%
where the time goes in v3:
time: 385 us; the launch traced here: 384 us
  Pallas kernels  162 us (42%)
  waiting for transfers between devices  124 us (32%)
  blocking collectives  52.2 us (14%)
  starting transfers between devices  23.8 us (6%)
  local copies, waits for them, and re-layouts  15.3 us (4%)
  other arithmetic  5.56 us (1%)
    all_to_all x3, waiting for transfers between devices, swap(): lax.all_to_all(x, ('tr', 'tc'), split_axis=0, concat_axis=0, tiled=True)  120 us
    pallas_call x1, Pallas kernels, geometry_stage(): pl.pallas_call(geometry_kernel, grid=(rows // step,), in_specs=block_spec...  56.6 us
    all_to_all x1, blocking collectives, swap(): lax.all_to_all(x, ('tr', 'tc'), split_axis=0, concat_axis=0, tiled=True)  52.2 us
    pallas_call x4, Pallas kernels, vorticity_stage(): pl.pallas_call(vorticity_kernel, grid_spec=pltpu.PrefetchScalarGridSpec(n...  43.5 us
    all_to_all x3, starting transfers between devices, swap(): lax.all_to_all(x, ('tr', 'tc'), split_axis=0, concat_axis=0, tiled=True)  18.1 us
    pallas_call x1, Pallas kernels, col_stage(): pl.pallas_call(functools.partial(col_kernel, chunk=chunk, cuts=cuts), gri...  17 us
    pallas_call x4, Pallas kernels, final_stage(): pl.pallas_call(final_kernel, grid_spec=pltpu.PrefetchScalarGridSpec(num_s...  16.2 us
    pallas_call x2, Pallas kernels, row_forward(): pl.pallas_call(row_kernel, grid_spec=pltpu.PrefetchScalarGridSpec(num_sca...  15.6 us
  transfers between devices with their start and end apart: 13, of which 6 were waited for; matrix products, arithmetic and copies ran while one was open for 3% of the time, Pallas kernels for 30%

profile of v3, /device:TPU:21, one launch (start us, length us, event | category | flops | bytes accessed | tf_op | source)
XLA Modules:
  0.0 384.1 jit_solution(13654222829795433127)
XLA Ops:
  0.6 1.3 fusion.1
  1.9 1.3 fusion.3
  3.3 0.7 collective-permute-start.2
  4.0 1.0 pad_maximum_fusion.1
  5.1 1.0 fusion.5
  6.0 1.0 fusion.2
  7.1 1.3 collective-permute-start
  8.4 1.2 collective-permute-start.1
  10.1 1.0 collective-permute-done.refs_9_
  11.2 2.1 collective-permute-done.1.refs_10_
  13.3 0.6 copy-done.7
  14.3 1.0 copy-done.1
  15.2 11.3 %vorticity_stage.5 = f32[2,16,128,128]{3,2,1,0:T(8,128)} custom-call(s32[2]{0:T(128)} %pad_add_fusion.2.base_ref, f32[2,512,2048]{2,1,0:T(8,128)} %refs_2_.11, f32[2,512,2048]{2,1,0:T(8,128)} %refs_2_.11, f32[2,512,2048]{2,1,0:T(8,128)} %refs_2_.11, f32[1,512,2048]{2,1,0:T(8,128)} %bitcast.29, f32[1,512,2048]{2,1,0:T(8,128)} %bitcast.30, ...), custom_call_target="tpu_custom_call" | custom-call | flops 20971520 | bytes 6291456 | tf_op jit(solution)/shard_map/vorticity_stage/pallas_call | solution.py:653
  26.7 0.7 pad_add_fusion.3.base_ref
  27.4 10.7 %vorticity_stage.4.refs_0_ = f32[2,16,128,128]{3,2,1,0:T(8,128)} custom-call(s32[2]{0:T(128)} %pad_add_fusion.3.base_ref, f32[2,512,2048]{2,1,0:T(8,128)} %refs_2_.11, f32[2,512,2048]{2,1,0:T(8,128)} %refs_2_.11, f32[2,512,2048]{2,1,0:T(8,128)} %refs_2_.11, f32[1,512,2048]{2,1,0:T(8,128)} %bitcast.32, f32[1,512,2048]{2,1,0:T(8,128)} %bitcast.33, ...), custom_call_target="tpu_custom_call" | custom-call | flops 20971520 | bytes 6291456 | tf_op jit(solution)/shard_map/vorticity_stage/pallas_call | solution.py:653
  38.2 1.3 copy-done.4
  39.5 7.8 %row_forward.2 = f32[16,4,128,128]{3,2,1,0:T(8,128)} custom-call(s32[1]{0:T(128)} %bitcast.1.me_ref, f32[2,16,128,128]{3,2,1,0:T(8,128)} %vorticity_stage.4.refs_0_, f32[2,16,128,128]{3,2,1,0:T(8,128)} %copy-done.4, bf16[16,512,256]{2,1,0:T(8,128)(2,1)} %constant.59.clone.refs_2_), custom_call_target="tpu_custom_call" | custom-call | tf_op jit(solution)/shard_map/row_forward/pallas_call | solution.py:263
  47.3 7.3 %all-to-all-start = ((f32[16,1,4,128,128]{4,3,2,1,0:T(8,128)}), f32[16,1,4,128,128]{4,3,2,1,0:T(8,128)}, u32[]{:S(2)}, u32[]{:S(2)}) async-start(f32[16,1,4,128,128]{4,3,2,1,0:T(8,128)} %bitcast.59), calls=%async_computation | async-start | bytes 8388608 | tf_op jit(solution)/shard_map/all_to_all | solution.py:786
  54.5 0.7 pad_add_fusion.base_ref
  55.2 10.7 %vorticity_stage.7 = f32[2,16,128,128]{3,2,1,0:T(8,128)} custom-call(s32[2]{0:T(128)} %pad_add_fusion.base_ref, f32[2,512,2048]{2,1,0:T(8,128)} %refs_2_.11, f32[2,512,2048]{2,1,0:T(8,128)} %refs_2_.11, f32[2,512,2048]{2,1,0:T(8,128)} %refs_2_.11, f32[1,512,2048]{2,1,0:T(8,128)} %bitcast.35, f32[1,512,2048]{2,1,0:T(8,128)} %bitcast.36, ...), custom_call_target="tpu_custom_call" | custom-call | flops 20971520 | bytes 6291456 | tf_op jit(solution)/shard_map/vorticity_stage/pallas_call | solution.py:653
  66.4 0.6 pad_add_fusion.1.base_ref
  67.0 10.8 %vorticity_stage.6.refs_0_ = f32[2,16,128,128]{3,2,1,0:T(8,128)} custom-call(s32[2]{0:T(128)} %pad_add_fusion.1.base_ref, f32[2,512,2048]{2,1,0:T(8,128)} %refs_2_.11, f32[2,512,2048]{2,1,0:T(8,128)} %refs_2_.11, f32[2,512,2048]{2,1,0:T(8,128)} %refs_2_.11, f32[1,512,2048]{2,1,0:T(8,128)} %bitcast.38, f32[1,512,2048]{2,1,0:T(8,128)} %bitcast.39, ...), custom_call_target="tpu_custom_call" | custom-call | flops 20971520 | bytes 6291456 | tf_op jit(solution)/shard_map/vorticity_stage/pallas_call | solution.py:653
  77.8 1.3 copy-done.3
  79.1 7.8 %row_forward.3 = f32[16,4,128,128]{3,2,1,0:T(8,128)} custom-call(s32[1]{0:T(128)} %bitcast.1.me_ref, f32[2,16,128,128]{3,2,1,0:T(8,128)} %vorticity_stage.6.refs_0_, f32[2,16,128,128]{3,2,1,0:T(8,128)} %copy-done.3, bf16[16,512,256]{2,1,0:T(8,128)(2,1)} %constant.59.clone.refs_2_), custom_call_target="tpu_custom_call" | custom-call | tf_op jit(solution)/shard_map/row_forward/pallas_call | solution.py:263
  86.9 59.8 %all-to-all-done.refs_0_ = f32[16,1,4,128,128]{4,3,2,1,0:T(8,128)} async-done(((f32[16,1,4,128,128]{4,3,2,1,0:T(8,128)}), f32[16,1,4,128,128]{4,3,2,1,0:T(8,128)}, u32[]{:S(2)}, u32[]{:S(2)}) %all-to-all-start) | async-done | bytes 4194336 | tf_op jit(solution)/shard_map/all_to_all | solution.py:786
  146.7 5.3 %all-to-all-start.1 = ((f32[16,1,4,128,128]{4,3,2,1,0:T(8,128)}), f32[16,1,4,128,128]{4,3,2,1,0:T(8,128)}, u32[]{:S(2)}, u32[]{:S(2)}) async-start(f32[16,1,4,128,128]{4,3,2,1,0:T(8,128)} %bitcast.58), calls=%async_computation.1 | async-start | bytes 8388608 | tf_op jit(solution)/shard_map/all_to_all | solution.py:786
  152.1 0.6 slice_bitcast_fusion.4
  152.7 0.6 slice_bitcast_fusion.5
  153.8 1.5 dynamic-slice_bitcast_fusion.refs_2_
  155.4 1.0 collective-permute-done.6
  156.4 0.9 select_maximum_fusion.2.refs_8_
  157.4 1.0 select_maximum_fusion.refs_9_
  158.3 56.6 %geometry_stage.1 = (f32[3,16,512,128]{3,2,1,0:T(8,128)}, f32[16,512,128]{2,1,0:T(8,128)}) custom-call(f32[2,512,2048]{2,1,0:T(8,128)} %refs_2_.11, f32[2,512,2048]{2,1,0:T(8,128)} %refs_2_.11, f32[2,512,2048]{2,1,0:T(8,128)} %refs_2_.11, f32[1,512,2048]{2,1,0:T(8,128)} %bitcast.41, f32[1,512,2048]{2,1,0:T(8,128)} %bitcast.42, f32[1,512,2048]{2,1,0:T(8,128)} %bitcast.43, ...), custom_call_target="tpu_custom_call" | custom-call | flops 209715200 | bytes 29360128 | tf_op jit(solution)/shard_map/geometry_stage/pallas_call | solution.py:678
  214.9 29.3 %all-to-all-done.1.refs_1_ = f32[16,1,4,128,128]{4,3,2,1,0:T(8,128)} async-done(((f32[16,1,4,128,128]{4,3,2,1,0:T(8,128)}), f32[16,1,4,128,128]{4,3,2,1,0:T(8,128)}, u32[]{:S(2)}, u32[]{:S(2)}) %all-to-all-start.1) | async-done | bytes 4194336 | tf_op jit(solution)/shard_map/all_to_all | solution.py:786
  244.2 17.0 %col_stage.1 = (f32[16,1,2,128,128]{4,3,2,1,0:T(8,128)}, f32[16,1,2,128,128]{4,3,2,1,0:T(8,128)}) custom-call(f32[16,1,4,128,128]{4,3,2,1,0:T(8,128)} %all-to-all-done.refs_0_, f32[16,1,4,128,128]{4,3,2,1,0:T(8,128)} %all-to-all-done.1.refs_1_, f32[1,128,128]{2,1,0:T(8,128)} %dynamic-slice_bitcast_fusion.refs_2_, bf16[768,256]{1,0:T(8,128)(2,1)} %constant.61.clone.refs_3_, ...), custom_call_target="tpu_custom_call" | custom-call | tf_op jit(solution)/shard_map/col_stage/pallas_call | solution.py:369
  261.3 52.2 %all_to_all.20 = f32[16,1,2,128,128]{4,3,2,1,0:T(8,128)} all-to-all(f32[16,1,2,128,128]{4,3,2,1,0:T(8,128)} %get-tuple-element.38), channel_id=1, replica_groups=mesh['groups'=2,'tr'=8,'tc'=2] {'tr','tc'}, dimensions={0} | all-to-all | bytes 4194304 | tf_op jit(solution)/shard_map/all_to_all | solution.py:786
  313.4 5.5 %all-to-all-start.2 = ((f32[16,1,2,128,128]{4,3,2,1,0:T(8,128)}), f32[16,1,2,128,128]{4,3,2,1,0:T(8,128)S(1)}, u32[]{:S(2)}, u32[]{:S(2)}) async-start(f32[16,1,2,128,128]{4,3,2,1,0:T(8,128)} %get-tuple-element.37), calls=%async_computation.2 | async-start | bytes 4194304 | tf_op jit(solution)/shard_map/all_to_all | solution.py:786
  319.0 6.7 %row_back.2 = (f32[16,128,128]{2,1,0:T(8,128)}, f32[16,128,128]{2,1,0:T(8,128)}) custom-call(s32[1]{0:T(128)} %bitcast.1.me_ref, f32[16,2,128,128]{3,2,1,0:T(8,128)} %bitcast.61, bf16[16,512,256]{2,1,0:T(8,128)(2,1)} %constant.65.clone.w_ref), custom_call_target="tpu_custom_call" | custom-call | tf_op jit(solution)/shard_map/row_back/pallas_call | solution.py:435
  326.0 4.1 %final_stage.4 = (f32[3,512,2048]{2,1,0:T(8,128)}, f32[512,2048]{1,0:T(8,128)}) custom-call(s32[1]{0:T(128)} %bitcast.2.base_ref, f32[16,128,128]{2,1,0:T(8,128)} %get-tuple-element.42.speed_ref, f32[3,16,512,128]{3,2,1,0:T(8,128)} %get-tuple-element.40.unit_ref, f32[16,512,128]{2,1,0:T(8,128)} %get-tuple-element.41.rest_ref), custom_call_target="tpu_custom_call" | custom-call | flops 1572864 | bytes 9437184 | tf_op jit(solution)/shard_map/final_stage/pallas_call | solution.py:721
  330.1 1.0 copy-done.9
  331.1 4.1 %final_stage.5 = (f32[3,512,2048]{2,1,0:T(8,128)}, f32[512,2048]{1,0:T(8,128)}) custom-call(s32[1]{0:T(128)} %bitcast.17.base_ref, f32[16,128,128]{2,1,0:T(8,128)} %copy-done.9, f32[3,16,512,128]{3,2,1,0:T(8,128)} %get-tuple-element.40.unit_ref, f32[16,512,128]{2,1,0:T(8,128)} %get-tuple-element.41.rest_ref, ...), custom_call_target="tpu_custom_call", output_to_operand_aliasing={{0}: (4, {}), {1}: (5, {})} | custom-call | flops 1572864 | bytes 9437184 | tf_op jit(solution)/shard_map/final_stage/pallas_call | solution.py:721
  335.1 31.0 %all-to-all-done.2 = f32[16,1,2,128,128]{4,3,2,1,0:T(8,128)S(1)} async-done(((f32[16,1,2,128,128]{4,3,2,1,0:T(8,128)}), f32[16,1,2,128,128]{4,3,2,1,0:T(8,128)S(1)}, u32[]{:S(2)}, u32[]{:S(2)}) %all-to-all-start.2) | async-done | bytes 2097184 | tf_op jit(solution)/shard_map/all_to_all | solution.py:786
  366.1 1.3 copy-done.2
  367.5 6.7 %row_back.3 = (f32[16,128,128]{2,1,0:T(8,128)}, f32[16,128,128]{2,1,0:T(8,128)}) custom-call(s32[1]{0:T(128)} %bitcast.1.me_ref, f32[16,2,128,128]{3,2,1,0:T(8,128)} %bitcast.60, bf16[16,512,256]{2,1,0:T(8,128)(2,1)} %constant.65.clone.w_ref), custom_call_target="tpu_custom_call" | custom-call | tf_op jit(solution)/shard_map/row_back/pallas_call | solution.py:435
  374.1 0.9 collective-permute-start.9
  375.0 4.1 %final_stage.6 = (f32[3,512,2048]{2,1,0:T(8,128)}, f32[512,2048]{1,0:T(8,128)}) custom-call(s32[1]{0:T(128)} %bitcast.7.base_ref, f32[16,128,128]{2,1,0:T(8,128)} %get-tuple-element.49.speed_ref, f32[3,16,512,128]{3,2,1,0:T(8,128)} %get-tuple-element.40.unit_ref, ...), custom_call_target="tpu_custom_call", output_to_operand_aliasing={{0}: (4, {}), {1}: (5, {})} | custom-call | flops 1572864 | bytes 9437184 | tf_op jit(solution)/shard_map/final_stage/pallas_call | solution.py:721
  379.1 1.0 copy-done.10
  380.1 4.1 %final_stage.7 = (f32[3,512,2048]{2,1,0:T(8,128)}, f32[512,2048]{1,0:T(8,128)}) custom-call(s32[1]{0:T(128)} %bitcast.base_ref, f32[16,128,128]{2,1,0:T(8,128)} %copy-done.10, f32[3,16,512,128]{3,2,1,0:T(8,128)} %get-tuple-element.40.unit_ref, f32[16,512,128]{2,1,0:T(8,128)} %get-tuple-element.41.rest_ref, ...), custom_call_target="tpu_custom_call", output_to_operand_aliasing={{0}: (4, {}), {1}: (5, {})} | custom-call | flops 1572864 | bytes 9437184 | tf_op jit(solution)/shard_map/final_stage/pallas_call | solution.py:721
  (39 shorter events, 2.8 us)
Async XLA Ops:
  3.3 10.0 %collective-permute-start.2 = (f32[4,512,128]{2,1,0:T(8,128)S(1)}, f32[4,512,128]{2,1,0:T(8,128)S(1)}, u32[]{:S(2)}, u32[]{:S(2)}) collective-permute-start(f32[4,512,128]{2,1,0:T(8,128)S(1)} %pad_maximum_fusion), channel_id=1, source_target_pairs={{0,1},{1,0},{2,3},{3,2},{4,5},{5,4},{6,7},{7,6},{8,9},{9,8},{10,11... | collective-permute-start | bytes 3145736 | tf_op jit(solution)/shard_map/ppermute | solution.py:754
  5.1 8.2 %collective-permute-start.3 = (f32[4,512,128]{2,1,0:T(8,128)}, f32[4,512,128]{2,1,0:T(8,128)S(1)}, u32[]{:S(2)}, u32[]{:S(2)}) collective-permute-start(f32[4,512,128]{2,1,0:T(8,128)} %pad_maximum_fusion.1), channel_id=1, source_target_pairs={{1,0},{0,1},{3,2},{2,3},{5,4},{4,5},{7,6},{6,7},{9,8},{8,9},{11,10... | collective-permute-start | bytes 3145736 | tf_op jit(solution)/shard_map/ppermute | solution.py:754
  7.1 4.1 %collective-permute-start = (f32[4,2,2048]{2,1,0:T(2,128)S(1)}, f32[4,2,2048]{2,1,0:T(2,128)S(1)}, u32[]{:S(2)}, u32[]{:S(2)}) collective-permute-start(f32[4,2,2048]{2,1,0:T(2,128)S(1)} %pad_maximum_fusion.2), channel_id=1, source_target_pairs={{0,2},{2,4},{4,6},{6,8},{8,10},{10,12},{12,14},{14,0},{1,3},{3,5},... | collective-permute-start | bytes 196616 | tf_op jit(solution)/shard_map/ppermute | solution.py:754
  8.4 4.9 %collective-permute-start.1 = (f32[4,2,2048]{2,1,0:T(2,128)S(1)}, f32[4,2,2048]{2,1,0:T(2,128)S(1)}, u32[]{:S(2)}, u32[]{:S(2)}) collective-permute-start(f32[4,2,2048]{2,1,0:T(2,128)S(1)} %pad_maximum_fusion.3), channel_id=1, source_target_pairs={{2,0},{4,2},{6,4},{8,6},{10,8},{12,10},{14,12},{0,14},{3,1},{5,3},... | collective-permute-start | bytes 196616 | tf_op jit(solution)/shard_map/ppermute | solution.py:754
  11.2 2.1 copy-start.5
  13.2 0.6 copy-start.7
  13.2 1.0 copy-start
  14.3 1.0 copy-start.1
  26.5 11.6 %collective-permute-start.4 = (f32[2,16,128,128]{3,2,1,0:T(8,128)}, f32[2,16,128,128]{3,2,1,0:T(8,128)S(1)}, u32[]{:S(2)}, u32[]{:S(2)}) collective-permute-start(f32[2,16,128,128]{3,2,1,0:T(8,128)} %vorticity_stage.5), channel_id=1, source_target_pairs={{0,1},{1,0},{2,3},{3,2},{4,5},{5,4},{6,7},{7,6},{8,9},{9,8},{10,11... | collective-permute-start | bytes 6291464 | tf_op jit(solution)/shard_map/ppermute | solution.py:783
  38.1 1.3 copy-start.4
  47.3 99.5 %all-to-all-start = ((f32[16,1,4,128,128]{4,3,2,1,0:T(8,128)}), f32[16,1,4,128,128]{4,3,2,1,0:T(8,128)}, u32[]{:S(2)}, u32[]{:S(2)}) async-start(f32[16,1,4,128,128]{4,3,2,1,0:T(8,128)} %bitcast.59), calls=%async_computation | async-start | bytes 8388608 | tf_op jit(solution)/shard_map/all_to_all | solution.py:786
  65.9 11.8 %collective-permute-start.5 = (f32[2,16,128,128]{3,2,1,0:T(8,128)}, f32[2,16,128,128]{3,2,1,0:T(8,128)S(1)}, u32[]{:S(2)}, u32[]{:S(2)}) collective-permute-start(f32[2,16,128,128]{3,2,1,0:T(8,128)} %vorticity_stage.7), channel_id=1, source_target_pairs={{0,1},{1,0},{2,3},{3,2},{4,5},{5,4},{6,7},{7,6},{8,9},{9,8},{10,11... | collective-permute-start | bytes 6291464 | tf_op jit(solution)/shard_map/ppermute | solution.py:783
  77.8 1.3 copy-start.3
  146.7 5.3 %copy-start.8 = (f32[4,2,2048]{2,1,0:T(2,128)S(1)}, f32[4,2,2048]{2,1,0:T(2,128)}, u32[]{:S(2)}) copy-start(f32[4,2,2048]{2,1,0:T(2,128)} %copy-done.7) | copy-start | bytes 196612
  146.7 6.0 %copy-start.6 = (f32[4,2,2048]{2,1,0:T(2,128)S(1)}, f32[4,2,2048]{2,1,0:T(2,128)}, u32[]{:S(2)}) copy-start(f32[4,2,2048]{2,1,0:T(2,128)} %copy-done.5) | copy-start | bytes 196612
  146.7 9.7 %slice-start = ((f32[4,512,128]{2,1,0:T(8,128)}), f32[3,512,128]{2,1,0:T(8,128)S(1)}, s32[]{:S(2)}) async-start(f32[4,512,128]{2,1,0:T(8,128)} %copy-done), calls=%async_computation.4 | async-start | bytes 1572864 | tf_op jit(solution)/shard_map/slice | solution.py:810
  146.7 97.5 %all-to-all-start.1 = ((f32[16,1,4,128,128]{4,3,2,1,0:T(8,128)}), f32[16,1,4,128,128]{4,3,2,1,0:T(8,128)}, u32[]{:S(2)}, u32[]{:S(2)}) async-start(f32[16,1,4,128,128]{4,3,2,1,0:T(8,128)} %bitcast.58), calls=%async_computation.1 | async-start | bytes 8388608 | tf_op jit(solution)/shard_map/all_to_all | solution.py:786
  152.0 5.3 %slice-start.1 = ((f32[4,512,128]{2,1,0:T(8,128)}), f32[3,512,128]{2,1,0:T(8,128)S(1)}, s32[]{:S(2)}) async-start(f32[4,512,128]{2,1,0:T(8,128)} %copy-done.1), calls=%async_computation.5 | async-start | bytes 1572864 | tf_op jit(solution)/shard_map/slice | solution.py:811
  153.4 2.0 collective-permute-start.7
  155.3 1.2 collective-permute-start.6
  313.4 52.7 %all-to-all-start.2 = ((f32[16,1,2,128,128]{4,3,2,1,0:T(8,128)}), f32[16,1,2,128,128]{4,3,2,1,0:T(8,128)S(1)}, u32[]{:S(2)}, u32[]{:S(2)}) async-start(f32[16,1,2,128,128]{4,3,2,1,0:T(8,128)} %get-tuple-element.37), calls=%async_computation.2 | async-start | bytes 4194304 | tf_op jit(solution)/shard_map/all_to_all | solution.py:786
  325.7 4.4 %collective-permute-start.8 = (f32[16,128,128]{2,1,0:T(8,128)}, f32[16,128,128]{2,1,0:T(8,128)S(1)}, u32[]{:S(2)}, u32[]{:S(2)}) collective-permute-start(f32[16,128,128]{2,1,0:T(8,128)} %get-tuple-element.39), channel_id=1, source_target_pairs={{0,1},{1,0},{2,3},{3,2},{4,5},{5,4},{6,7},{7,6},{8,9},{9,8},{10,11... | collective-permute-start | bytes 3145736 | tf_op jit(solution)/shard_map/ppermute | solution.py:783
  330.1 1.0 copy-start.9
  366.1 1.3 copy-start.2
  374.1 4.9 %collective-permute-start.9 = (f32[16,128,128]{2,1,0:T(8,128)}, f32[16,128,128]{2,1,0:T(8,128)S(1)}, u32[]{:S(2)}, u32[]{:S(2)}) collective-permute-start(f32[16,128,128]{2,1,0:T(8,128)} %get-tuple-element.48), channel_id=1, source_target_pairs={{0,1},{1,0},{2,3},{3,2},{4,5},{5,4},{6,7},{7,6},{8,9},{9,8},{10,11... | collective-permute-start | bytes 3145736 | tf_op jit(solution)/shard_map/ppermute | solution.py:783
  379.1 1.0 copy-start.10

commit v4 on v3

--- a/solution.py
+++ b/solution.py
@@ -265,9 +265,7 @@
         grid_spec=pltpu.PrefetchScalarGridSpec(
             num_scalar_prefetch=1,
             grid=(rows // step, blocks // some),
-            in_specs=[
-                pl.BlockSpec((2, per, step, LANE), lambda i, k, _: (0, 0, i, 0)) for _ in pieces
-            ]
+            in_specs=[pl.BlockSpec((2, per, step, LANE), lambda i, k, _: (0, 0, i, 0))] * len(pieces)
             + [pl.BlockSpec((some,) + table.shape[1:], lambda i, k, _: (k, 0, 0))],
             out_specs=pl.BlockSpec((some, 4, LANE, step), lambda i, k, _: (k, 0, 0, i)),
             scratch_shapes=[pltpu.VMEM((blocks, 2 * step, 2 * LANE), F32)],
@@ -533,31 +531,42 @@
     return pl.ds(start, SUB, stride=rows // SUB)
 
 
-def vorticity_kernel(base_ref, *refs):
+def vorticity_kernel(me_ref, *refs, start, total):
     planes, heights, dipoles, edge = refs[0:3], refs[3:6], refs[6:9], refs[9:13]
     o_ref, ext_ref = refs[13], refs[14]
     _, count, rows, _ = o_ref.shape
-    i = base_ref[0] + pl.program_id(0)
+    i = start(me_ref) + pl.program_id(0)
     for index, (source, field) in enumerate(
         [(planes, 0), (planes, 1), (heights, 0), (dipoles, 0)]
     ):
-        fill(ext_ref, index, source, field, edge, i, base_ref[1])
-    many = tile_count(count, MANY)
+        fill(ext_ref, index, source, field, edge, i, total)
+    lane = lax.broadcasted_iota(jnp.int32, (SUB, LANE), 1)
 
     def body(t, _):
-        for c in range(0, count, many):
+        rolled = {}
+
+        def roll(index, c, by):
+            key = (index, c, by)
+            if key not in rolled:
+                x = ext_ref[index, c, spread(SUB + t, rows)]
+                rolled[key] = pltpu.roll(x, (-by) % LANE, 1)
+            return rolled[key]
+
+        def shift(index, c, by):
+            if by < 0:
+                return jnp.where(lane < -by, roll(index, c - 1, by), roll(index, c, by))
+            return jnp.where(lane >= LANE - by, roll(index, c + 1, by), roll(index, c, by))
+
+        for c in range(count):
             ga, gb = [], []
             for index in range(4):
-
-                def load(s, lo, hi):
-                    return ext_ref[index, lo:hi, spread(SUB + t + s, rows)]
-
-                ga.append(diff_one(*[load(s, c + 1, c + 1 + many) for s in (-2, -1, 1, 2)]))
-                gb.append(diff_one(*neighbours(load(0, c, c + many + 2))))
+                v = [ext_ref[index, c + 1, spread(SUB + t + s, rows)] for s in (-2, -1, 1, 2)]
+                ga.append(diff_one(*v))
+                gb.append(diff_one(*[shift(index, c + 1, s) for s in (-2, -1, 1, 2)]))
             _, _, normal = normal_of(ga, gb)
             inverse = 12.0 * lax.rsqrt(dot3(normal, normal))
-            o_ref[0, c : c + many, spread(t, rows)] = ga[3] * inverse
-            o_ref[1, c : c + many, spread(t, rows)] = gb[3] * inverse
+            o_ref[0, c, spread(t, rows)] = ga[3] * inverse
+            o_ref[1, c, spread(t, rows)] = gb[3] * inverse
         return 0
 
     lax.fori_loop(0, rows // SUB, body, 0)
@@ -617,49 +626,51 @@
     lax.fori_loop(0, rows // SUB, body, 0)
 
 
-def row_step(rows):
-    step = 64
+def row_step(rows, step=64):
     while rows % step:
         step //= 2
     return step
 
 
-def block_specs(count, step, rows, width):
+def block_specs(count, step, rows, width, start=None):
     per, total = step // SUB, rows // SUB
 
-    def at(i, base):
-        return i + base[0][0] if base else i
+    def at(i, me):
+        return i + start(*me) if start else i
 
     return [
-        pl.BlockSpec((count, step, width), lambda i, *base: (0, at(i, base), 0)),
+        pl.BlockSpec((count, step, width), lambda i, *me: (0, at(i, me), 0)),
         pl.BlockSpec(
             (count, SUB, width),
-            lambda i, *base: (0, jnp.maximum(at(i, base) * per - 1, 0), 0),
+            lambda i, *me: (0, jnp.maximum(at(i, me) * per - 1, 0), 0),
         ),
         pl.BlockSpec(
             (count, SUB, width),
-            lambda i, *base: (0, jnp.minimum((at(i, base) + 1) * per, total - 1), 0),
+            lambda i, *me: (0, jnp.minimum((at(i, me) + 1) * per, total - 1), 0),
         ),
     ]
 
 
-def vorticity_stage(planes, height, dipole, edge, which, parts):
+def vorticity_stage(planes, height, dipole, edge, me, part_of, parts):
     _, rows, width = planes.shape
     count = width // LANE
     part = rows // parts
-    step = row_step(part)
-    rim = lambda: pl.BlockSpec((4, step, LANE), lambda i, base: (0, i + base[0], 0))
-    first = jnp.stack([which * (part // step), rows // step]).astype(jnp.int32)
+    step = row_step(part, 32)
+
+    def at(me_ref):
+        return part_of(me_ref[0]) * (part // step)
+
+    rim = lambda: pl.BlockSpec((4, step, LANE), lambda i, me: (0, i + at(me), 0))
     return pl.pallas_call(
-        vorticity_kernel,
+        functools.partial(vorticity_kernel, start=at, total=rows // step),
         grid_spec=pltpu.PrefetchScalarGridSpec(
             num_scalar_prefetch=1,
             grid=(part // step,),
-            in_specs=block_specs(2, step, rows, width)
-            + block_specs(1, step, rows, width)
-            + block_specs(1, step, rows, width)
+            in_specs=block_specs(2, step, rows, width, at)
+            + block_specs(1, step, rows, width, at)
+            + block_specs(1, step, rows, width, at)
             + [whole(edge[0]), whole(edge[1]), rim(), rim()],
-            out_specs=pl.BlockSpec((2, count, step, LANE), lambda i, base: (0, 0, i, 0)),
+            out_specs=pl.BlockSpec((2, count, step, LANE), lambda i, me: (0, 0, i, 0)),
             scratch_shapes=[pltpu.VMEM((4, count + 2, step + 2 * SUB, LANE), F32)],
         ),
         out_shape=jax.ShapeDtypeStruct((2, count, part, LANE), F32),
@@ -668,7 +679,7 @@
             flops=80 * part * width, bytes_accessed=6 * 4 * part * width, transcendentals=part * width
         ),
         name="vorticity_stage",
-    )(first, *[planes] * 3, *[height[None]] * 3, *[dipole[None]] * 3, *edge)
+    )(me[None], *[planes] * 3, *[height[None]] * 3, *[dipole[None]] * 3, *edge)
 
 
 def geometry_stage(planes, height, edge):
@@ -702,7 +713,7 @@
     )(*[planes] * 3, *[height[None]] * 3, *edge)
 
 
-def final_kernel(base_ref, speed_ref, unit_ref, rest_ref, *refs):
+def final_kernel(me_ref, speed_ref, unit_ref, rest_ref, *refs):
     velocity_ref, update_ref = refs[-2:]
     for j in range(unit_ref.shape[1]):
         at = slice(j * LANE, (j + 1) * LANE)
@@ -712,11 +723,14 @@
         update_ref[:, at] = rest_ref[j] + 0.5 * speed * speed
 
 
-def final_stage(speed, unit, rest, which, before):
+def final_stage(speed, unit, rest, me, part_of, before):
     count, part, _ = speed.shape
     rows, width = unit.shape[2], count * LANE
     step = row_step(part)
-    first = (which * (part // step))[None].astype(jnp.int32)
+
+    def at(me_ref):
+        return part_of(me_ref[0]) * (part // step)
+
     n_before = len(before)
     return pl.pallas_call(
         final_kernel,
@@ -724,14 +738,14 @@
             num_scalar_prefetch=1,
             grid=(part // step,),
             in_specs=[
-                pl.BlockSpec((count, step, LANE), lambda i, base: (0, i, 0)),
-                pl.BlockSpec((3, count, step, LANE), lambda i, base: (0, 0, i + base[0], 0)),
-                pl.BlockSpec((count, step, LANE), lambda i, base: (0, i + base[0], 0)),
+                pl.BlockSpec((count, step, LANE), lambda i, me: (0, i, 0)),
+                pl.BlockSpec((3, count, step, LANE), lambda i, me: (0, 0, i + at(me), 0)),
+                pl.BlockSpec((count, step, LANE), lambda i, me: (0, i + at(me), 0)),
             ]
             + [pl.BlockSpec(memory_space=pl.ANY)] * n_before,
             out_specs=[
-                pl.BlockSpec((3, step, width), lambda i, base: (0, i + base[0], 0)),
-                pl.BlockSpec((step, width), lambda i, base: (i + base[0], 0)),
+                pl.BlockSpec((3, step, width), lambda i, me: (0, i + at(me), 0)),
+                pl.BlockSpec((step, width), lambda i, me: (i + at(me), 0)),
             ],
         ),
         out_shape=[
@@ -744,7 +758,42 @@
             flops=6 * part * width, bytes_accessed=9 * 4 * part * width, transcendentals=0
         ),
         name="final_stage",
-    )(first, speed, unit, rest, *before)
+    )(me[None], speed, unit, rest, *before)
+
+
+def edge_kernel(*refs):
+    ins, (last_ref, first_ref, low_ref, top_ref) = refs[:12], refs[12:]
+    for k, field in enumerate((0, 1, 0, 0)):
+        source = max(k - 1, 0) * 4
+        last_ref[k] = ins[source][field]
+        first_ref[k] = ins[source + 1][field]
+        low_ref[k] = ins[source + 2][field, SUB - RIM :]
+        top_ref[k] = ins[source + 3][field, :RIM]
+
+
+def edge_stage(planes, height, dipole):
+    _, rows, width = planes.shape
+    specs, args = [], []
+    for x in (planes, height[None], dipole[None]):
+        c = x.shape[0]
+        specs += [
+            pl.BlockSpec((c, rows, LANE), lambda i: (0, 0, width // LANE - 1)),
+            pl.BlockSpec((c, rows, LANE), lambda i: (0, 0, 0)),
+            pl.BlockSpec((c, SUB, width), lambda i: (0, rows // SUB - 1, 0)),
+            pl.BlockSpec((c, SUB, width), lambda i: (0, 0, 0)),
+        ]
+        args += [x] * 4
+    strip = jax.ShapeDtypeStruct((4, rows, LANE), F32)
+    rim = jax.ShapeDtypeStruct((4, RIM, width), F32)
+    return pl.pallas_call(
+        edge_kernel,
+        grid=(1,),
+        in_specs=specs,
+        out_specs=[pl.BlockSpec(o.shape, lambda i: (0, 0, 0)) for o in (strip, strip, rim, rim)],
+        out_shape=[strip, strip, rim, rim],
+        compiler_params=params(),
+        name="edge_stage",
+    )(*args)
 
 
 def both_ways(last, initial, axis):
@@ -761,12 +810,9 @@
     row_count, col_count = rows * tr, width * tc
     part = rows // tc
 
-    def cut(a, b, dim):
-        pieces = [shift_plane, height[None], dipole[None]]
-        return jnp.concatenate([lax.slice_in_dim(p, a, b, axis=dim) for p in pieces], 0)
-
-    top, low = both_ways(cut(rows - RIM, rows, 1), cut(0, RIM, 1), "tr")
-    left, right = both_ways(cut(width - LANE, width, 2), cut(0, LANE, 2), "tc")
+    last, initial, last_rows, initial_rows = edge_stage(shift_plane, height, dipole)
+    top, low = both_ways(last_rows, initial_rows, "tr")
+    left, right = both_ways(last, initial, "tc")
     me = lax.axis_index("tc").astype(jnp.int32)
     edges = (top, low, left, right)
     row_table, back_table = row_tables(col_count)
@@ -788,13 +834,12 @@
     columns = []
     for h in range(cuts):
 
-        def stage(core):
-            return vorticity_stage(
-                shift_plane, height, dipole, edges, core * cuts + h, tc * cuts
-            )
-
-        sent = [turn(stage((me + away) % tc), away) for away in range(1, tc)]
-        spec = row_forward([stage(me)] + sent, me, row_table)
+        def stage(away):
+            part_of = lambda core, h=h: lax.rem(core + away, tc) * cuts + h
+            return vorticity_stage(shift_plane, height, dipole, edges, me, part_of, tc * cuts)
+
+        sent = [turn(stage(away), away) for away in range(1, tc)]
+        spec = row_forward([stage(0)] + sent, me, row_table)
         spec = spec.reshape(blocks, 4, pieces, n, cut_rows)
         spec = jnp.swapaxes(spec, 1, 2).reshape(devices, u, 4, n, cut_rows)
         if h + 1 < cuts:
@@ -832,10 +877,10 @@
         back = back.reshape(blocks, pieces, 2, n, cut_rows)
         back = jnp.swapaxes(back, 1, 2).reshape(blocks, 2, LANE, cut_rows)
         speeds = row_back(back, me, back_table, tc)
-        outs = final_stage(speeds[0], unit, base, me * cuts + h, outs)
-        for away in range(1, tc):
-            speed = turn(speeds[away], away)
-            outs = final_stage(speed, unit, base, (me - away) % tc * cuts + h, outs)
+        for away in range(tc):
+            speed = turn(speeds[away], away) if away else speeds[0]
+            part_of = lambda core, h=h, away=away: lax.rem(core + tc - away, tc) * cuts + h
+            outs = final_stage(speed, unit, base, me, part_of, outs)
     return tuple(outs)
 
 

time: 385 us -> 377 us (0.979)
  waiting for transfers between devices: 124 us -> 130 us
  local copies, waits for them, and re-layouts: 15.3 us -> 10.2 us
    slice x4 -> x0, local copies, waits for them, and re-layouts: 4.51 us -> none  [cut(): lax.slice_in_dim(p, a, b, axis=dim)]
    all_to_all x3, waiting for transfers between devices: 120 us -> 125 us  [swap(): lax.all_to_all(x, ('tr', 'tc'), split_axis=0, concat_axis=0, tiled=True)]
    pallas_call x4 -> x5, Pallas kernels: 43.5 us -> 40 us  [the longest x4 37 us: vorticity_stage(): pl.pallas_call(functools.partial(vorticity_kernel, start=at, total=rows /...]
  transfers between devices with their start and end apart: 13 -> 13, of which waited for: 6 -> 6; matrix products, arithmetic and copies ran while one was open for 3% -> 1% of each run, Pallas kernels for 30% -> 29%
where the time goes in v4:
time: 377 us
  Pallas kernels  159 us (42%)
  waiting for transfers between devices  130 us (34%)
  blocking collectives  52.2 us (14%)
  starting transfers between devices  23.5 us (6%)
  local copies, waits for them, and re-layouts  10.2 us (3%)
    all_to_all x3, waiting for transfers between devices, swap(): lax.all_to_all(x, ('tr', 'tc'), split_axis=0, concat_axis=0, tiled=True)  125 us
    pallas_call x1, Pallas kernels, geometry_stage(): pl.pallas_call(geometry_kernel, grid=(rows // step,), in_specs=block_spec...  56.5 us
    all_to_all x1, blocking collectives, swap(): lax.all_to_all(x, ('tr', 'tc'), split_axis=0, concat_axis=0, tiled=True)  52.2 us
    pallas_call x4, Pallas kernels, vorticity_stage(): pl.pallas_call(functools.partial(vorticity_kernel, start=at, total=rows /...  37 us
    all_to_all x3, starting transfers between devices, swap(): lax.all_to_all(x, ('tr', 'tc'), split_axis=0, concat_axis=0, tiled=True)  17.8 us
    pallas_call x1, Pallas kernels, col_stage(): pl.pallas_call(functools.partial(col_kernel, chunk=chunk, cuts=cuts), gri...  17 us
    pallas_call x4, Pallas kernels, final_stage(): pl.pallas_call(final_kernel, grid_spec=pltpu.PrefetchScalarGridSpec(num_s...  16.2 us
    pallas_call x2, Pallas kernels, row_forward(): pl.pallas_call(row_kernel, grid_spec=pltpu.PrefetchScalarGridSpec(num_sca...  15.6 us
  transfers between devices with their start and end apart: 13, of which 6 were waited for; matrix products, arithmetic and copies ran while one was open for 1% of the time, Pallas kernels for 29%

profile of v4, /device:TPU:21, one launch (start us, length us, event | category | flops | bytes accessed | tf_op | source)
XLA Modules:
  0.0 376.9 jit_solution(13841130442619016969)
XLA Ops:
  0.6 3.1 edge_stage.1
  3.7 0.7 collective-permute-start.2
  4.4 0.1 collective-permute-start.3
  4.4 1.2 collective-permute-start
  5.6 1.2 collective-permute-start.1
  6.8 1.9 collective-permute-done.refs_9_
  8.7 2.1 collective-permute-done.1.refs_10_
  10.8 0.6 copy-done.7
  11.4 0.4 copy-done
  11.8 0.4 copy-done.1
  12.2 9.4 %vorticity_stage.5 = f32[2,16,128,128]{3,2,1,0:T(8,128)} custom-call(s32[1]{0:T(128)} %bitcast.me_ref, f32[2,512,2048]{2,1,0:T(8,128)} %refs_2_.13, f32[2,512,2048]{2,1,0:T(8,128)} %refs_2_.13, f32[2,512,2048]{2,1,0:T(8,128)} %refs_2_.13, f32[1,512,2048]{2,1,0:T(8,128)} %bitcast.25, f32[1,512,2048]{2,1,0:T(8,128)} %bitcast.26, f32[1,512,2048]{2,1,0:T(8,128)} %bitcast.27, ...), custom_call_target="tpu_custom_call" | custom-call | flops 20971520 | bytes 6291456 | tf_op jit(solution)/shard_map/vorticity_stage/pallas_call | solution.py:664
  21.7 0.4 collective-permute-start.4
  22.1 9.1 %vorticity_stage.4.refs_0_ = f32[2,16,128,128]{3,2,1,0:T(8,128)} custom-call(s32[1]{0:T(128)} %bitcast.me_ref, f32[2,512,2048]{2,1,0:T(8,128)} %refs_2_.13, f32[2,512,2048]{2,1,0:T(8,128)} %refs_2_.13, f32[2,512,2048]{2,1,0:T(8,128)} %refs_2_.13, f32[1,512,2048]{2,1,0:T(8,128)} %bitcast.28, f32[1,512,2048]{2,1,0:T(8,128)} %bitcast.29, ...), custom_call_target="tpu_custom_call" | custom-call | flops 20971520 | bytes 6291456 | tf_op jit(solution)/shard_map/vorticity_stage/pallas_call | solution.py:664
  31.3 1.4 copy-done.4
  32.6 7.8 %row_forward.2 = f32[16,4,128,128]{3,2,1,0:T(8,128)} custom-call(s32[1]{0:T(128)} %bitcast.me_ref, f32[2,16,128,128]{3,2,1,0:T(8,128)} %vorticity_stage.4.refs_0_, f32[2,16,128,128]{3,2,1,0:T(8,128)} %copy-done.4, bf16[16,512,256]{2,1,0:T(8,128)(2,1)} %constant.32.clone.refs_2_), custom_call_target="tpu_custom_call" | custom-call | tf_op jit(solution)/shard_map/row_forward/pallas_call | solution.py:263
  40.4 6.9 %all-to-all-start = ((f32[16,1,4,128,128]{4,3,2,1,0:T(8,128)}), f32[16,1,4,128,128]{4,3,2,1,0:T(8,128)}, u32[]{:S(2)}, u32[]{:S(2)}) async-start(f32[16,1,4,128,128]{4,3,2,1,0:T(8,128)} %bitcast.57), calls=%async_computation | async-start | bytes 8388608 | tf_op jit(solution)/shard_map/all_to_all | solution.py:832
  47.3 9.2 %vorticity_stage.7 = f32[2,16,128,128]{3,2,1,0:T(8,128)} custom-call(s32[1]{0:T(128)} %bitcast.me_ref, f32[2,512,2048]{2,1,0:T(8,128)} %refs_2_.13, f32[2,512,2048]{2,1,0:T(8,128)} %refs_2_.13, f32[2,512,2048]{2,1,0:T(8,128)} %refs_2_.13, f32[1,512,2048]{2,1,0:T(8,128)} %bitcast.31, f32[1,512,2048]{2,1,0:T(8,128)} %bitcast.32, f32[1,512,2048]{2,1,0:T(8,128)} %bitcast.33, ...), custom_call_target="tpu_custom_call" | custom-call | flops 20971520 | bytes 6291456 | tf_op jit(solution)/shard_map/vorticity_stage/pallas_call | solution.py:664
  56.4 0.4 collective-permute-start.5
  56.9 9.2 %vorticity_stage.6.refs_0_ = f32[2,16,128,128]{3,2,1,0:T(8,128)} custom-call(s32[1]{0:T(128)} %bitcast.me_ref, f32[2,512,2048]{2,1,0:T(8,128)} %refs_2_.13, f32[2,512,2048]{2,1,0:T(8,128)} %refs_2_.13, f32[2,512,2048]{2,1,0:T(8,128)} %refs_2_.13, f32[1,512,2048]{2,1,0:T(8,128)} %bitcast.34, f32[1,512,2048]{2,1,0:T(8,128)} %bitcast.35, ...), custom_call_target="tpu_custom_call" | custom-call | flops 20971520 | bytes 6291456 | tf_op jit(solution)/shard_map/vorticity_stage/pallas_call | solution.py:664
  66.1 1.3 copy-done.3
  67.4 7.8 %row_forward.3 = f32[16,4,128,128]{3,2,1,0:T(8,128)} custom-call(s32[1]{0:T(128)} %bitcast.me_ref, f32[2,16,128,128]{3,2,1,0:T(8,128)} %vorticity_stage.6.refs_0_, f32[2,16,128,128]{3,2,1,0:T(8,128)} %copy-done.3, bf16[16,512,256]{2,1,0:T(8,128)(2,1)} %constant.32.clone.refs_2_), custom_call_target="tpu_custom_call" | custom-call | tf_op jit(solution)/shard_map/row_forward/pallas_call | solution.py:263
  75.2 64.3 %all-to-all-done.refs_0_ = f32[16,1,4,128,128]{4,3,2,1,0:T(8,128)} async-done(((f32[16,1,4,128,128]{4,3,2,1,0:T(8,128)}), f32[16,1,4,128,128]{4,3,2,1,0:T(8,128)}, u32[]{:S(2)}, u32[]{:S(2)}) %all-to-all-start) | async-done | bytes 4194336 | tf_op jit(solution)/shard_map/all_to_all | solution.py:832
  139.5 5.3 %all-to-all-start.1 = ((f32[16,1,4,128,128]{4,3,2,1,0:T(8,128)}), f32[16,1,4,128,128]{4,3,2,1,0:T(8,128)}, u32[]{:S(2)}, u32[]{:S(2)}) async-start(f32[16,1,4,128,128]{4,3,2,1,0:T(8,128)} %bitcast.56), calls=%async_computation.1 | async-start | bytes 8388608 | tf_op jit(solution)/shard_map/all_to_all | solution.py:832
  144.8 0.6 slice_bitcast_fusion.4
  145.5 0.6 slice_bitcast_fusion.5
  146.1 0.4 collective-permute-start.7
  146.5 1.5 dynamic-slice_bitcast_fusion.refs_2_
  148.0 0.1 collective-permute-start.6
  148.2 1.0 collective-permute-done.6
  149.2 0.9 select_maximum_fusion.2.refs_8_
  150.1 1.0 select_maximum_fusion.refs_9_
  151.1 56.5 %geometry_stage.1 = (f32[3,16,512,128]{3,2,1,0:T(8,128)}, f32[16,512,128]{2,1,0:T(8,128)}) custom-call(f32[2,512,2048]{2,1,0:T(8,128)} %refs_2_.13, f32[2,512,2048]{2,1,0:T(8,128)} %refs_2_.13, f32[2,512,2048]{2,1,0:T(8,128)} %refs_2_.13, f32[1,512,2048]{2,1,0:T(8,128)} %bitcast.37, f32[1,512,2048]{2,1,0:T(8,128)} %bitcast.38, f32[1,512,2048]{2,1,0:T(8,128)} %bitcast.39, ...), custom_call_target="tpu_custom_call" | custom-call | flops 209715200 | bytes 29360128 | tf_op jit(solution)/shard_map/geometry_stage/pallas_call | solution.py:689
  207.6 29.4 %all-to-all-done.1.refs_1_ = f32[16,1,4,128,128]{4,3,2,1,0:T(8,128)} async-done(((f32[16,1,4,128,128]{4,3,2,1,0:T(8,128)}), f32[16,1,4,128,128]{4,3,2,1,0:T(8,128)}, u32[]{:S(2)}, u32[]{:S(2)}) %all-to-all-start.1) | async-done | bytes 4194336 | tf_op jit(solution)/shard_map/all_to_all | solution.py:832
  237.0 17.0 %col_stage.1 = (f32[16,1,2,128,128]{4,3,2,1,0:T(8,128)}, f32[16,1,2,128,128]{4,3,2,1,0:T(8,128)}) custom-call(f32[16,1,4,128,128]{4,3,2,1,0:T(8,128)} %all-to-all-done.refs_0_, f32[16,1,4,128,128]{4,3,2,1,0:T(8,128)} %all-to-all-done.1.refs_1_, f32[1,128,128]{2,1,0:T(8,128)} %dynamic-slice_bitcast_fusion.refs_2_, bf16[768,256]{1,0:T(8,128)(2,1)} %constant.34.clone.refs_3_, ...), custom_call_target="tpu_custom_call" | custom-call | tf_op jit(solution)/shard_map/col_stage/pallas_call | solution.py:367
  254.0 52.2 %all_to_all.20 = f32[16,1,2,128,128]{4,3,2,1,0:T(8,128)} all-to-all(f32[16,1,2,128,128]{4,3,2,1,0:T(8,128)} %get-tuple-element.46), channel_id=1, replica_groups=mesh['groups'=2,'tr'=8,'tc'=2] {'tr','tc'}, dimensions={0} | all-to-all | bytes 4194304 | tf_op jit(solution)/shard_map/all_to_all | solution.py:832
  306.2 5.5 %all-to-all-start.2 = ((f32[16,1,2,128,128]{4,3,2,1,0:T(8,128)}), f32[16,1,2,128,128]{4,3,2,1,0:T(8,128)S(1)}, u32[]{:S(2)}, u32[]{:S(2)}) async-start(f32[16,1,2,128,128]{4,3,2,1,0:T(8,128)} %get-tuple-element.45), calls=%async_computation.2 | async-start | bytes 4194304 | tf_op jit(solution)/shard_map/all_to_all | solution.py:832
  311.7 6.7 %row_back.2 = (f32[16,128,128]{2,1,0:T(8,128)}, f32[16,128,128]{2,1,0:T(8,128)}) custom-call(s32[1]{0:T(128)} %bitcast.me_ref, f32[16,2,128,128]{3,2,1,0:T(8,128)} %bitcast.59, bf16[16,512,256]{2,1,0:T(8,128)(2,1)} %constant.38.clone.w_ref), custom_call_target="tpu_custom_call" | custom-call | tf_op jit(solution)/shard_map/row_back/pallas_call | solution.py:433
  318.4 0.4 collective-permute-start.8
  318.8 4.1 %final_stage.4 = (f32[3,512,2048]{2,1,0:T(8,128)}, f32[512,2048]{1,0:T(8,128)}) custom-call(s32[1]{0:T(128)} %bitcast.me_ref, f32[16,128,128]{2,1,0:T(8,128)} %get-tuple-element.50.speed_ref, f32[3,16,512,128]{3,2,1,0:T(8,128)} %get-tuple-element.48.unit_ref, f32[16,512,128]{2,1,0:T(8,128)} %get-tuple-element.49.rest_ref), custom_call_target="tpu_custom_call" | custom-call | flops 1572864 | bytes 9437184 | tf_op jit(solution)/shard_map/final_stage/pallas_call | solution.py:735
  322.8 1.0 copy-done.10
  323.8 4.1 %final_stage.5 = (f32[3,512,2048]{2,1,0:T(8,128)}, f32[512,2048]{1,0:T(8,128)}) custom-call(s32[1]{0:T(128)} %bitcast.me_ref, f32[16,128,128]{2,1,0:T(8,128)} %copy-done.10, f32[3,16,512,128]{3,2,1,0:T(8,128)} %get-tuple-element.48.unit_ref, f32[16,512,128]{2,1,0:T(8,128)} %get-tuple-element.49.rest_ref, ...), custom_call_target="tpu_custom_call", output_to_operand_aliasing={{0}: (4, {}), {1}: (5, {})} | custom-call | flops 1572864 | bytes 9437184 | tf_op jit(solution)/shard_map/final_stage/pallas_call | solution.py:735
  327.9 31.0 %all-to-all-done.2 = f32[16,1,2,128,128]{4,3,2,1,0:T(8,128)S(1)} async-done(((f32[16,1,2,128,128]{4,3,2,1,0:T(8,128)}), f32[16,1,2,128,128]{4,3,2,1,0:T(8,128)S(1)}, u32[]{:S(2)}, u32[]{:S(2)}) %all-to-all-start.2) | async-done | bytes 2097184 | tf_op jit(solution)/shard_map/all_to_all | solution.py:832
  358.8 1.4 copy-done.2
  360.2 6.7 %row_back.3 = (f32[16,128,128]{2,1,0:T(8,128)}, f32[16,128,128]{2,1,0:T(8,128)}) custom-call(s32[1]{0:T(128)} %bitcast.me_ref, f32[16,2,128,128]{3,2,1,0:T(8,128)} %bitcast.58, bf16[16,512,256]{2,1,0:T(8,128)(2,1)} %constant.38.clone.w_ref), custom_call_target="tpu_custom_call" | custom-call | tf_op jit(solution)/shard_map/row_back/pallas_call | solution.py:433
  366.9 0.9 collective-permute-start.9
  367.8 4.1 %final_stage.6 = (f32[3,512,2048]{2,1,0:T(8,128)}, f32[512,2048]{1,0:T(8,128)}) custom-call(s32[1]{0:T(128)} %bitcast.me_ref, f32[16,128,128]{2,1,0:T(8,128)} %get-tuple-element.57.speed_ref, f32[3,16,512,128]{3,2,1,0:T(8,128)} %get-tuple-element.48.unit_ref, ...), custom_call_target="tpu_custom_call", output_to_operand_aliasing={{0}: (4, {}), {1}: (5, {})} | custom-call | flops 1572864 | bytes 9437184 | tf_op jit(solution)/shard_map/final_stage/pallas_call | solution.py:735
  371.8 1.0 copy-done.9
  372.8 4.1 %final_stage.7 = (f32[3,512,2048]{2,1,0:T(8,128)}, f32[512,2048]{1,0:T(8,128)}) custom-call(s32[1]{0:T(128)} %bitcast.me_ref, f32[16,128,128]{2,1,0:T(8,128)} %copy-done.9, f32[3,16,512,128]{3,2,1,0:T(8,128)} %get-tuple-element.48.unit_ref, f32[16,512,128]{2,1,0:T(8,128)} %get-tuple-element.49.rest_ref, ...), custom_call_target="tpu_custom_call", output_to_operand_aliasing={{0}: (4, {}), {1}: (5, {})} | custom-call | flops 1572864 | bytes 9437184 | tf_op jit(solution)/shard_map/final_stage/pallas_call | solution.py:735
  (28 shorter events, 0.1 us)
Async XLA Ops:
  3.7 7.1 %collective-permute-start.2 = (f32[4,512,128]{2,1,0:T(8,128)}, f32[4,512,128]{2,1,0:T(8,128)S(1)}, u32[]{:S(2)}, u32[]{:S(2)}) collective-permute-start(f32[4,512,128]{2,1,0:T(8,128)} %get-tuple-element.34), channel_id=1, source_target_pairs={{0,1},{1,0},{2,3},{3,2},{4,5},{5,4},{6,7},{7,6},{8,9},{9,8},{10,11... | collective-permute-start | bytes 3145736 | tf_op jit(solution)/shard_map/ppermute | solution.py:803
  4.4 6.5 %collective-permute-start.3 = (f32[4,512,128]{2,1,0:T(8,128)}, f32[4,512,128]{2,1,0:T(8,128)S(1)}, u32[]{:S(2)}, u32[]{:S(2)}) collective-permute-start(f32[4,512,128]{2,1,0:T(8,128)} %get-tuple-element.35), channel_id=1, source_target_pairs={{1,0},{0,1},{3,2},{2,3},{5,4},{4,5},{7,6},{6,7},{9,8},{8,9},{11,10... | collective-permute-start | bytes 3145736 | tf_op jit(solution)/shard_map/ppermute | solution.py:803
  4.4 4.3 %collective-permute-start = (f32[4,2,2048]{2,1,0:T(2,128)}, f32[4,2,2048]{2,1,0:T(2,128)S(1)}, u32[]{:S(2)}, u32[]{:S(2)}) collective-permute-start(f32[4,2,2048]{2,1,0:T(2,128)} %get-tuple-element.32), channel_id=1, source_target_pairs={{0,2},{2,4},{4,6},{6,8},{8,10},{10,12},{12,14},{14,0},{1,3},{3,5},... | collective-permute-start | bytes 196616 | tf_op jit(solution)/shard_map/ppermute | solution.py:803
  5.6 5.2 %collective-permute-start.1 = (f32[4,2,2048]{2,1,0:T(2,128)}, f32[4,2,2048]{2,1,0:T(2,128)S(1)}, u32[]{:S(2)}, u32[]{:S(2)}) collective-permute-start(f32[4,2,2048]{2,1,0:T(2,128)} %get-tuple-element.33), channel_id=1, source_target_pairs={{2,0},{4,2},{6,4},{8,6},{10,8},{12,10},{14,12},{0,14},{3,1},{5,3},... | collective-permute-start | bytes 196616 | tf_op jit(solution)/shard_map/ppermute | solution.py:803
  8.7 2.1 copy-start.5
  10.8 0.6 copy-start.7
  10.8 1.0 copy-start
  10.8 1.4 copy-start.1
  21.7 9.6 %collective-permute-start.4 = (f32[2,16,128,128]{3,2,1,0:T(8,128)}, f32[2,16,128,128]{3,2,1,0:T(8,128)S(1)}, u32[]{:S(2)}, u32[]{:S(2)}) collective-permute-start(f32[2,16,128,128]{3,2,1,0:T(8,128)} %vorticity_stage.5), channel_id=1, source_target_pairs={{0,1},{1,0},{2,3},{3,2},{4,5},{5,4},{6,7},{7,6},{8,9},{9,8},{10,11... | collective-permute-start | bytes 6291464 | tf_op jit(solution)/shard_map/ppermute | solution.py:829
  31.2 1.4 copy-start.4
  40.4 99.1 %all-to-all-start = ((f32[16,1,4,128,128]{4,3,2,1,0:T(8,128)}), f32[16,1,4,128,128]{4,3,2,1,0:T(8,128)}, u32[]{:S(2)}, u32[]{:S(2)}) async-start(f32[16,1,4,128,128]{4,3,2,1,0:T(8,128)} %bitcast.57), calls=%async_computation | async-start | bytes 8388608 | tf_op jit(solution)/shard_map/all_to_all | solution.py:832
  56.4 9.7 %collective-permute-start.5 = (f32[2,16,128,128]{3,2,1,0:T(8,128)}, f32[2,16,128,128]{3,2,1,0:T(8,128)S(1)}, u32[]{:S(2)}, u32[]{:S(2)}) collective-permute-start(f32[2,16,128,128]{3,2,1,0:T(8,128)} %vorticity_stage.7), channel_id=1, source_target_pairs={{0,1},{1,0},{2,3},{3,2},{4,5},{5,4},{6,7},{7,6},{8,9},{9,8},{10,11... | collective-permute-start | bytes 6291464 | tf_op jit(solution)/shard_map/ppermute | solution.py:829
  66.1 1.3 copy-start.3
  139.5 5.3 %copy-start.8 = (f32[4,2,2048]{2,1,0:T(2,128)S(1)}, f32[4,2,2048]{2,1,0:T(2,128)}, u32[]{:S(2)}) copy-start(f32[4,2,2048]{2,1,0:T(2,128)} %copy-done.7) | copy-start | bytes 196612
  139.5 6.0 %copy-start.6 = (f32[4,2,2048]{2,1,0:T(2,128)S(1)}, f32[4,2,2048]{2,1,0:T(2,128)}, u32[]{:S(2)}) copy-start(f32[4,2,2048]{2,1,0:T(2,128)} %copy-done.5) | copy-start | bytes 196612
  139.5 9.7 %slice-start = ((f32[4,512,128]{2,1,0:T(8,128)}), f32[3,512,128]{2,1,0:T(8,128)S(1)}, s32[]{:S(2)}) async-start(f32[4,512,128]{2,1,0:T(8,128)} %copy-done), calls=%async_computation.4 | async-start | bytes 1572864 | tf_op jit(solution)/shard_map/slice | solution.py:855
  139.5 97.5 %all-to-all-start.1 = ((f32[16,1,4,128,128]{4,3,2,1,0:T(8,128)}), f32[16,1,4,128,128]{4,3,2,1,0:T(8,128)}, u32[]{:S(2)}, u32[]{:S(2)}) async-start(f32[16,1,4,128,128]{4,3,2,1,0:T(8,128)} %bitcast.56), calls=%async_computation.1 | async-start | bytes 8388608 | tf_op jit(solution)/shard_map/all_to_all | solution.py:832
  144.8 5.3 %slice-start.1 = ((f32[4,512,128]{2,1,0:T(8,128)}), f32[3,512,128]{2,1,0:T(8,128)S(1)}, s32[]{:S(2)}) async-start(f32[4,512,128]{2,1,0:T(8,128)} %copy-done.1), calls=%async_computation.5 | async-start | bytes 1572864 | tf_op jit(solution)/shard_map/slice | solution.py:856
  146.1 2.0 collective-permute-start.7
  148.0 1.2 collective-permute-start.6
  306.2 52.7 %all-to-all-start.2 = ((f32[16,1,2,128,128]{4,3,2,1,0:T(8,128)}), f32[16,1,2,128,128]{4,3,2,1,0:T(8,128)S(1)}, u32[]{:S(2)}, u32[]{:S(2)}) async-start(f32[16,1,2,128,128]{4,3,2,1,0:T(8,128)} %get-tuple-element.45), calls=%async_computation.2 | async-start | bytes 4194304 | tf_op jit(solution)/shard_map/all_to_all | solution.py:832
  318.4 4.4 %collective-permute-start.8 = (f32[16,128,128]{2,1,0:T(8,128)}, f32[16,128,128]{2,1,0:T(8,128)S(1)}, u32[]{:S(2)}, u32[]{:S(2)}) collective-permute-start(f32[16,128,128]{2,1,0:T(8,128)} %get-tuple-element.47), channel_id=1, source_target_pairs={{0,1},{1,0},{2,3},{3,2},{4,5},{5,4},{6,7},{7,6},{8,9},{9,8},{10,11... | collective-permute-start | bytes 3145736 | tf_op jit(solution)/shard_map/ppermute | solution.py:829
  322.8 1.0 copy-start.10
  358.8 1.4 copy-start.2
  366.9 4.9 %collective-permute-start.9 = (f32[16,128,128]{2,1,0:T(8,128)}, f32[16,128,128]{2,1,0:T(8,128)S(1)}, u32[]{:S(2)}, u32[]{:S(2)}) collective-permute-start(f32[16,128,128]{2,1,0:T(8,128)} %get-tuple-element.56), channel_id=1, source_target_pairs={{0,1},{1,0},{2,3},{3,2},{4,5},{5,4},{6,7},{7,6},{8,9},{9,8},{10,11... | collective-permute-start | bytes 3145736 | tf_op jit(solution)/shard_map/ppermute | solution.py:829
  371.8 1.0 copy-start.9
